TPU v7x, 32 devices: a whole 2x2x4 slice. The times are simulated.
32 devices in a mesh: dp: 8 (over y, x, core), mp: 4 (over z).
Axes of the slice: x: 2, y: 2, z: 4, core: 2. Of those that a mesh axis runs over, the one named last changes fastest.
Arguments:
- tokens: bfloat16 [5120, 2048], P(('dp', 'mp')), may hold values from -6 to 6
- attn_gain: float32 [2048], replicated, may hold values from 0.5 to 1.5
- query_down: bfloat16 [2048, 1024], replicated, may hold values from -0.125 to 0.125
- query_up: bfloat16 [1024, 4096], P(None, 'mp'), may hold values from -0.375 to 0.375
- key_value: bfloat16 [2048, 512], replicated, may hold values from -0.125 to 0.125
- attn_out: bfloat16 [4096, 2048], P('mp'), may hold values from -0.375 to 0.375
- mlp_gain: float32 [2048], replicated, may hold values from 0.5 to 1.5
- gate_weight: bfloat16 [2048, 5632], P(None, 'mp'), may hold values from -0.125 to 0.125
- up_weight: bfloat16 [2048, 5632], P(None, 'mp'), may hold values from -0.125 to 0.125
- down_weight: bfloat16 [5632, 2048], P('mp'), may hold values from -0.078125 to 0.078125
- out_grad: bfloat16 [5120, 2048], P(('dp', 'mp')), may hold values from -6 to 6
Outputs:
- layer_out: bfloat16 [5120, 2048], P(('dp', 'mp'))
- tokens_grad: float32 [5120, 2048], P(('dp', 'mp'))
- attn_gain_grad: float32 [2048], P('mp')
- query_down_grad: float32 [2048, 1024], P('mp')
- query_up_grad: float32 [1024, 4096], P(None, 'mp')
- key_value_grad: float32 [2048, 512], P('mp')
- attn_out_grad: float32 [4096, 2048], P('mp')
- mlp_gain_grad: float32 [2048], P('mp')
- gate_grad: float32 [2048, 5632], P(None, 'mp')
- up_grad: float32 [2048, 5632], P(None, 'mp')
- down_grad: float32 [5632, 2048], P('mp')
All inputs are finite; a program needn't handle non-finite values.
Results may differ from a plain program's by a relative error of at most 0.025.
Values may be sent and summed in bfloat16 or wider, within the bound.
No kernel may reach another device: no remote copies, remote signals or barrier semaphores. Data moves between devices by JAX's collectives and lax.ppermute only.
A program may use at most 192 MiB of HBM per device.

v0:
```python
import jax
import jax.numpy as jnp
from jax import lax
from jax.sharding import PartitionSpec as P

HEAD_DIM = 256
SHORT_PART = 128
LONG_PART = 512


EPS = 1e-06


def normalize(rows, gain):
    return rows * lax.rsqrt(jnp.mean(rows * rows, axis=-1, keepdims=True) + EPS) * gain


def segment_bounds():
    return ((0, SHORT_PART), (SHORT_PART, LONG_PART))


def score_block(
    query_rows, pair_all, group_index, own_group, offset, extent, local_heads, head_dim
):
    pair_block = lax.dynamic_index_in_dim(pair_all, group_index, 0, keepdims=False)
    key_rows = pair_block[offset : offset + extent, :head_dim]
    value_rows = pair_block[offset : offset + extent, head_dim:]
    raw_scores = jnp.einsum(
        "rd,kd->rk", query_rows, key_rows, preferred_element_type=jnp.float32
    ) * head_dim ** (-0.5)
    query_pos = jnp.arange(extent * local_heads, dtype=jnp.int32) // local_heads
    key_pos = jnp.arange(extent, dtype=jnp.int32)
    visible = (group_index < own_group) | (key_pos[None, :] <= query_pos[:, None])
    return (jnp.where(visible, raw_scores, -jnp.inf), key_rows, value_rows)


def forward_segment(query_rows, pair_all, own_group, offset, extent, local_heads, head_dim):
    row_count = query_rows.shape[0]

    def online_pass(group_index, running):
        maxima, totals, summed = running
        scores, key_rows, value_rows = score_block(
            query_rows, pair_all, group_index, own_group, offset, extent, local_heads, head_dim
        )
        new_max = jnp.maximum(maxima, jnp.max(scores, axis=1))
        rescale = jnp.exp(maxima - new_max)
        weights = jnp.exp(scores - new_max[:, None])
        totals = totals * rescale + jnp.sum(weights, axis=1)
        summed = summed * rescale[:, None] + jnp.dot(
            weights.astype(jnp.bfloat16), value_rows, preferred_element_type=jnp.float32
        )
        return (new_max, totals, summed)

    start_state = (
        jnp.full((row_count,), -jnp.inf, jnp.float32),
        jnp.zeros((row_count,), jnp.float32),
        jnp.zeros((row_count, head_dim), jnp.float32),
    )
    maxima, totals, summed = lax.fori_loop(0, own_group + 1, online_pass, start_state)
    log_total = maxima + jnp.log(totals)
    return (log_total, summed / totals[:, None])


def backward_segment(
    query_rows,
    pair_all,
    own_group,
    offset,
    extent,
    local_heads,
    head_dim,
    log_total,
    delta_sum,
    grad_rows,
    pair_grads,
):
    row_count = query_rows.shape[0]

    def main_pass(group_index, state_pair):
        query_grad, grads_now = state_pair
        scores, key_rows, value_rows = score_block(
            query_rows, pair_all, group_index, own_group, offset, extent, local_heads, head_dim
        )
        chance = jnp.exp(scores - log_total[:, None])
        chance_grad = jnp.einsum(
            "rd,kd->rk", grad_rows, value_rows, preferred_element_type=jnp.float32
        )
        score_low = (chance * (chance_grad - delta_sum[:, None]) * head_dim ** (-0.5)).astype(
            jnp.bfloat16
        )
        query_grad = query_grad + jnp.dot(score_low, key_rows, preferred_element_type=jnp.float32)
        key_grad = jnp.einsum(
            "rk,rd->kd", score_low, query_rows, preferred_element_type=jnp.float32
        )
        value_grad = jnp.einsum(
            "rk,rd->kd", chance.astype(jnp.bfloat16), grad_rows, preferred_element_type=jnp.float32
        )
        corner = (group_index, offset, 0)
        current = lax.dynamic_slice(grads_now, corner, (1, extent, 2 * head_dim))
        update = current + jnp.concatenate([key_grad, value_grad], axis=1)[None]
        return (query_grad, lax.dynamic_update_slice(grads_now, update, corner))

    start_state = (jnp.zeros((row_count, head_dim), jnp.float32), pair_grads)
    return lax.fori_loop(0, own_group + 1, main_pass, start_state)


def attention(query_full, pair_all, own_group, local_heads, head_dim):
    log_parts = []
    exact_parts = []
    pieces = []
    for bounds in segment_bounds():
        offset, extent = bounds
        query_rows = query_full[offset : offset + extent].reshape(extent * local_heads, head_dim)
        log_total, summed = forward_segment(
            query_rows, pair_all, own_group, offset, extent, local_heads, head_dim
        )
        log_parts.append(log_total)
        exact_parts.append(summed)
        pieces.append(summed.astype(jnp.bfloat16).reshape(extent, local_heads * head_dim))
    return ((tuple(log_parts), tuple(exact_parts)), jnp.concatenate(pieces, axis=0))


def attention_back(query_full, pair_all, own_group, local_heads, head_dim, log_parts, attended_low):
    totals_parts, exact_parts = log_parts
    pair_grads = jnp.zeros(pair_all.shape, jnp.float32)
    pieces = []
    for bounds, log_total, exact in zip(segment_bounds(), totals_parts, exact_parts):
        offset, extent = bounds
        query_rows = query_full[offset : offset + extent].reshape(extent * local_heads, head_dim)
        grad_rows = attended_low[offset : offset + extent].reshape(extent * local_heads, head_dim)
        delta_sum = jnp.sum(grad_rows.astype(jnp.float32) * exact, axis=1)
        query_grad, pair_grads = backward_segment(
            query_rows,
            pair_all,
            own_group,
            offset,
            extent,
            local_heads,
            head_dim,
            log_total,
            delta_sum,
            grad_rows,
            pair_grads,
        )
        pieces.append(query_grad.reshape(extent, local_heads * head_dim))
    return (jnp.concatenate(pieces, axis=0), pair_grads)


def gated(gate_in, up_in):
    return jax.nn.silu(gate_in) * up_in


def shards(
    tokens,
    attn_gain,
    query_down,
    query_up,
    key_value,
    attn_out,
    mlp_gain,
    gate_weight,
    up_weight,
    down_weight,
    out_grad,
):
    head_dim = HEAD_DIM
    local_heads = query_up.shape[1] // head_dim
    own_group = lax.axis_index("dp")
    inputs = tokens.astype(jnp.float32)
    normal_one = normalize(inputs, attn_gain).astype(jnp.bfloat16)
    latent = jnp.dot(normal_one, query_down, preferred_element_type=jnp.float32).astype(
        jnp.bfloat16
    )
    pair_local = jnp.dot(normal_one, key_value, preferred_element_type=jnp.float32).astype(
        jnp.bfloat16
    )

    def attention_inputs():
        latent_full = lax.all_gather(latent, "mp", axis=0, tiled=True)
        pair_flat = lax.all_gather(pair_local, ("dp", "mp"), axis=0, tiled=True)
        pair_all = pair_flat.reshape(lax.axis_size("dp"), latent_full.shape[0], 2 * head_dim)
        query_full = jnp.dot(latent_full, query_up, preferred_element_type=jnp.float32).astype(
            jnp.bfloat16
        )
        log_parts, attended = attention(query_full, pair_all, own_group, local_heads, head_dim)
        return (latent_full, pair_all, query_full, log_parts, attended)

    latent_full, pair_all, query_full, log_parts, attended = attention_inputs()
    hidden_res = inputs + lax.psum_scatter(
        jnp.dot(attended, attn_out, preferred_element_type=jnp.float32).astype(jnp.bfloat16),
        "mp",
        scatter_dimension=0,
        tiled=True,
    ).astype(jnp.float32)
    normal_two = normalize(hidden_res, mlp_gain).astype(jnp.bfloat16)

    def mlp_inputs():
        normal_full = lax.all_gather(normal_two, "mp", axis=0, tiled=True)
        gate = jnp.dot(normal_full, gate_weight, preferred_element_type=jnp.float32)
        upward = jnp.dot(normal_full, up_weight, preferred_element_type=jnp.float32)
        activated = gated(gate, upward).astype(jnp.bfloat16)
        return (normal_full, gate, upward, activated)

    normal_full, gate, upward, activated = mlp_inputs()
    result = hidden_res + lax.psum_scatter(
        jnp.dot(activated, down_weight, preferred_element_type=jnp.float32).astype(jnp.bfloat16),
        "mp",
        scatter_dimension=0,
        tiled=True,
    ).astype(jnp.float32)
    latent_full, pair_all, query_full, log_parts, attended = attention_inputs()
    normal_full, gate, upward, activated = mlp_inputs()
    grad_full = lax.all_gather(out_grad, "mp", axis=0, tiled=True)
    down_wgrad = jnp.einsum("tf,td->fd", activated, grad_full, preferred_element_type=jnp.float32)
    act_grad = jnp.einsum("td,fd->tf", grad_full, down_weight, preferred_element_type=jnp.float32)
    _, gated_pull = jax.vjp(gated, gate, upward)
    gate_grad32, up_grad32 = gated_pull(act_grad)
    gate_low = gate_grad32.astype(jnp.bfloat16)
    up_low = up_grad32.astype(jnp.bfloat16)
    gate_wgrad = jnp.einsum("td,tf->df", normal_full, gate_low, preferred_element_type=jnp.float32)
    up_wgrad = jnp.einsum("td,tf->df", normal_full, up_low, preferred_element_type=jnp.float32)
    normal_two_grad = lax.psum_scatter(
        (
            jnp.einsum("tf,df->td", gate_low, gate_weight, preferred_element_type=jnp.float32)
            + jnp.einsum("tf,df->td", up_low, up_weight, preferred_element_type=jnp.float32)
        ).astype(jnp.bfloat16),
        "mp",
        scatter_dimension=0,
        tiled=True,
    ).astype(jnp.float32)
    _, norm_pull_two = jax.vjp(normalize, hidden_res, mlp_gain)
    resid_from_norm, mlp_gain_part = norm_pull_two(normal_two_grad)
    hidden_grad = out_grad.astype(jnp.float32) + resid_from_norm
    branch_full = lax.all_gather(hidden_grad.astype(jnp.bfloat16), "mp", axis=0, tiled=True)
    out_wgrad = jnp.einsum("tk,td->kd", attended, branch_full, preferred_element_type=jnp.float32)
    attended_low = jnp.einsum(
        "td,kd->tk", branch_full, attn_out, preferred_element_type=jnp.float32
    ).astype(jnp.bfloat16)
    query_grad, pair_grads = attention_back(
        query_full, pair_all, own_group, local_heads, head_dim, log_parts, attended_low
    )
    query_low = query_grad.astype(jnp.bfloat16)
    up_query_wgrad = jnp.einsum(
        "tr,tk->rk", latent_full, query_low, preferred_element_type=jnp.float32
    )
    latent_low = lax.psum_scatter(
        jnp.einsum("tk,rk->tr", query_low, query_up, preferred_element_type=jnp.float32).astype(
            jnp.bfloat16
        ),
        "mp",
        scatter_dimension=0,
        tiled=True,
    )
    pair_flat_grads = pair_grads.reshape(pair_grads.shape[0] * pair_grads.shape[1], 2 * head_dim)
    pair_low = lax.psum_scatter(
        pair_flat_grads, ("dp", "mp"), scatter_dimension=0, tiled=True
    ).astype(jnp.bfloat16)
    down_query_part = jnp.einsum(
        "td,tr->dr", normal_one, latent_low, preferred_element_type=jnp.float32
    )
    pair_weight_part = jnp.einsum(
        "td,tp->dp", normal_one, pair_low, preferred_element_type=jnp.float32
    )
    normal_one_grad = jnp.einsum(
        "tr,dr->td", latent_low, query_down, preferred_element_type=jnp.float32
    ) + jnp.einsum("tp,dp->td", pair_low, key_value, preferred_element_type=jnp.float32)
    _, norm_pull_one = jax.vjp(normalize, inputs, attn_gain)
    input_from_norm, attn_gain_part = norm_pull_one(normal_one_grad)
    input_grad = hidden_grad + input_from_norm
    shared = (
        lax.psum_scatter(
            attn_gain_part.astype(jnp.bfloat16), "mp", scatter_dimension=0, tiled=True
        ).astype(jnp.float32),
        lax.psum_scatter(
            down_query_part.astype(jnp.bfloat16), "mp", scatter_dimension=0, tiled=True
        ).astype(jnp.float32),
        lax.psum_scatter(
            pair_weight_part.astype(jnp.bfloat16), "mp", scatter_dimension=0, tiled=True
        ).astype(jnp.float32),
        lax.psum_scatter(
            mlp_gain_part.astype(jnp.bfloat16), "mp", scatter_dimension=0, tiled=True
        ).astype(jnp.float32),
    )
    summed = (
        lax.psum(shared[0].astype(jnp.bfloat16), "dp").astype(jnp.float32),
        lax.psum(shared[1].astype(jnp.bfloat16), "dp").astype(jnp.float32),
        lax.psum(up_query_wgrad.astype(jnp.bfloat16), "dp").astype(jnp.float32),
        lax.psum(shared[2].astype(jnp.bfloat16), "dp").astype(jnp.float32),
        lax.psum(out_wgrad.astype(jnp.bfloat16), "dp").astype(jnp.float32),
        lax.psum(shared[3].astype(jnp.bfloat16), "dp").astype(jnp.float32),
        lax.psum(gate_wgrad.astype(jnp.bfloat16), "dp").astype(jnp.float32),
        lax.psum(up_wgrad.astype(jnp.bfloat16), "dp").astype(jnp.float32),
        lax.psum(down_wgrad.astype(jnp.bfloat16), "dp").astype(jnp.float32),
    )
    return (
        result.astype(jnp.bfloat16),
        input_grad,
        summed[0],
        summed[1],
        summed[2],
        summed[3],
        summed[4],
        summed[5],
        summed[6],
        summed[7],
        summed[8],
    )


def solution(mesh):
    return jax.shard_map(
        shards,
        mesh=mesh,
        in_specs=(
            P(("dp", "mp"), None),
            P(),
            P(),
            P(None, "mp"),
            P(),
            P("mp", None),
            P(),
            P(None, "mp"),
            P(None, "mp"),
            P("mp", None),
            P(("dp", "mp"), None),
        ),
        out_specs=(
            P(("dp", "mp"), None),
            P(("dp", "mp"), None),
            P("mp"),
            P("mp", None),
            P(None, "mp"),
            P("mp", None),
            P("mp", None),
            P("mp"),
            P(None, "mp"),
            P(None, "mp"),
            P("mp", None),
        ),
        check_vma=False,
    )
```

profile of v0, /device:TPU:0, one launch (start us, length us, event | category | flops | bytes accessed | tf_op | source)
XLA Modules:
  0.0 1634.6 jit_solution(8185057888868172604)
XLA Ops:
  16.4 32.6 %all-gather.8.cloned.1.call-done = bf16[640,1024]{1,0:T(8,128)(2,1)} async-done(((bf16[160,1024]{1,0:T(8,128)(2,1)}), bf16[640,1024]{1,0:T(8,128)(2,1)}) %all-gather.8.cloned.1.call-update) | async-done | bytes 1310736 | tf_op jit(solution)/shard_map/all_gather | solution.py:179
  56.6 60.1 %all-gather.6.cloned.1.call-done = bf16[5120,512]{1,0:T(8,128)(2,1)} async-done(((bf16[160,512]{1,0:T(8,128)(2,1)}), bf16[5120,512]{1,0:T(8,128)(2,1)}) %all-gather.6.cloned.1.call-update) | async-done | bytes 5242896 | tf_op jit(solution)/shard_map/all_gather | solution.py:180
  118.2 8.1 while.73
  133.0 6.9 while.72
  144.9 6.3 convolution_convert_fusion.6
  151.3 156.2 %reduce-scatter.8.cloned.1.call-done = bf16[160,2048]{1,0:T(8,128)(2,1)} async-done(((bf16[640,2048]{1,0:T(8,128)(2,1)}), bf16[160,2048]{1,0:T(8,128)(2,1)}) %reduce-scatter.8.cloned.1.call-update) | async-done | bytes 655376 | tf_op jit(solution)/shard_map/reduce_scatter | solution.py:189
  312.3 53.5 %all-gather.10.cloned.1.call-done = bf16[640,2048]{1,0:T(8,128)(2,1)} async-done(((bf16[160,2048]{1,0:T(8,128)(2,1)}), bf16[640,2048]{1,0:T(8,128)(2,1)}) %all-gather.10.cloned.1.call-update) | async-done | bytes 2621456 | tf_op jit(solution)/shard_map/all_gather | solution.py:198
  365.8 9.6 fusion.86
  375.4 8.7 fusion.87
  384.1 36.7 %all-gather.12.cloned.1.call-done = bf16[640,2048]{1,0:T(8,128)(2,1)} async-done(((bf16[160,2048]{1,0:T(8,128)(2,1)}), bf16[640,2048]{1,0:T(8,128)(2,1)}) %all-gather.12.cloned.1.call-update) | async-done | bytes 2621456 | tf_op jit(solution)/shard_map/all_gather | solution.py:213
  420.9 12.2 multiply_convert_fusion
  433.0 7.6 fusion.88
  440.7 8.3 add_convert_fusion
  449.2 50.8 %reduce-scatter.12.cloned.1.call-done = bf16[160,2048]{1,0:T(8,128)(2,1)} async-done(((bf16[640,2048]{1,0:T(8,128)(2,1)}), bf16[160,2048]{1,0:T(8,128)(2,1)}) %reduce-scatter.12.cloned.1.call-update) | async-done | bytes 655376 | tf_op jit(solution)/shard_map/reduce_scatter | solution.py:222
  505.2 53.4 %all-gather.14.cloned.1.call-done = bf16[640,2048]{1,0:T(8,128)(2,1)} async-done(((bf16[160,2048]{1,0:T(8,128)(2,1)}), bf16[640,2048]{1,0:T(8,128)(2,1)}) %all-gather.14.cloned.1.call-update) | async-done | bytes 2621456 | tf_op jit(solution)/shard_map/all_gather | solution.py:234
  578.4 17.7 %while.74 = (s32[]{:T(128)}, f32[512,256]{1,0:T(8,128)}, f32[8,640,512]{1,2,0:T(8,128)}, s32[]{:T(128)}, s32[]{:T(128)}, /*index=5*/bf16[8,640,512]{2,1,0:T(8,12...) while((s32[]{:T(128)}, f32[512,256]{1,0:T(8,128)}, ...), condition=%wide.region_16.17_spmd, body=%wide.region_15.16_spmd.sunk | while | flops 168693760 | bytes 7938229 | solution.py:104
  597.6 13.8 while.75
  621.9 11.2 copy.26
  633.2 239.0 %reduce-scatter.14.cloned.1.call-done = bf16[160,1024]{1,0:T(8,128)(2,1)} async-done(((bf16[640,1024]{1,0:T(8,128)(2,1)}), bf16[160,1024]{1,0:T(8,128)(2,1)}) %reduce-scatter.14.cloned.1.call-update) | async-done | bytes 327696 | tf_op jit(solution)/shard_map/reduce_scatter | solution.py:246
  877.1 226.1 %reduce-scatter.16.cloned.1.call-done = f32[160,512]{1,0:T(8,128)} async-done(((f32[5120,512]{1,0:T(8,128)}), f32[160,512]{1,0:T(8,128)}) %reduce-scatter.16.cloned.1.call-update) | async-done | bytes 327696 | tf_op jit(solution)/shard_map/reduce_scatter | solution.py:255
  1106.3 9.1 convolution_convert_fusion.5
  1115.6 8.8 convolution_convert_fusion.1
  1124.4 6.8 convolution_convert_fusion.2
  1131.3 6.5 convolution_convert_fusion
  1146.1 34.0 %reduce-scatter.18.cloned.1.call-done = bf16[512,1024]{1,0:T(8,128)(2,1)} async-done(((bf16[2048,1024]{1,0:T(8,128)(2,1)}), bf16[512,1024]{1,0:T(8,128)(2,1)}) %reduce-scatter.18.cloned.1.call-update) | async-done | bytes 1048592 | tf_op jit(solution)/shard_map/reduce_scatter | solution.py:274
  1180.1 46.8 %reduce-scatter.20.cloned.1.call-done = bf16[512,512]{1,0:T(8,128)(2,1)} async-done(((bf16[2048,512]{1,0:T(8,128)(2,1)}), bf16[512,512]{1,0:T(8,128)(2,1)}) %reduce-scatter.20.cloned.1.call-update) | async-done | bytes 524304 | tf_op jit(solution)/shard_map/reduce_scatter | solution.py:277
  1234.8 10.4 all-reduce.4
  1245.4 13.0 all-reduce.2
  1259.6 21.3 %reduce-scatter.10.cloned.1.call-done = bf16[160,2048]{1,0:T(8,128)(2,1)} async-done(((bf16[640,2048]{1,0:T(8,128)(2,1)}), bf16[160,2048]{1,0:T(8,128)(2,1)}) %reduce-scatter.10.cloned.1.call-update) | async-done | bytes 655376 | tf_op jit(solution)/shard_map/reduce_scatter | solution.py:205
  1285.1 313.4 %all-reduce.7.cloned.1.call-done = (bf16[512,1024]{1,0:T(8,128)(2,1)}, bf16[1024,1024]{1,0:T(8,128)(2,1)}, bf16[512,512]{1,0:T(8,128)(2,1)}, bf16[1024,2048]{1,0...) async-done(((bf16[512,1024]{1,0:T(8,128)(2,1)}, bf16[1024,1024]{1,0:T(8,128)(2,1)}, bf16[512,512]{1,0:T(8,128)(2,1)}, ...) | async-done | bytes 25165840 | tf_op jit(solution)/shard_map/psum | solution.py:286
  1598.5 8.6 convert_element_type.218
  1612.3 6.0 convert_element_type.222
  (238 shorter events, 162.0 us)
Async XLA Ops:
  7.2 41.8 %copy-start = (bf16[1024,1024]{1,0:T(8,128)(2,1)S(1)}, bf16[1024,1024]{1,0:T(8,128)(2,1)}, u32[]{:S(2)}) copy-start(bf16[1024,1024]{1,0:T(8,128)(2,1)} %param.22) | copy-start | bytes 6291460
  7.2 41.8 %all-gather.8.cloned.1.call-start = ((), (), s32[]{:S(2)}) async-start(), calls=%async_computation.8 | async-start | bytes 1638400 | tf_op jit(solution)/shard_map/all_gather | solution.py:179
  13.4 103.3 %all-gather.6.cloned.1.call-start = ((), (), s32[]{:S(2)}) async-start(), calls=%async_computation.7 | async-start | bytes 5406720 | tf_op jit(solution)/shard_map/all_gather | solution.py:180
  16.3 291.2 %reduce-scatter.8.cloned.1.call-start = ((), (), s32[]{:S(2)}) async-start(), calls=%async_computation.9 | async-start | bytes 3276800 | tf_op jit(solution)/shard_map/reduce_scatter | solution.py:189
  139.9 11.4 copy-start.6
  151.3 157.7 %copy-start.27 = (f32[2048]{0:T(1024)S(1)}, f32[2048]{0:T(1024)}, u32[]{:S(2)}) copy-start(f32[2048]{0:T(1024)} %param.25) | copy-start | bytes 24580
  151.3 214.5 %all-gather.10.cloned.1.call-start = ((), (), s32[]{:S(2)}) async-start(), calls=%async_computation.10 | async-start | bytes 3276800 | tf_op jit(solution)/shard_map/all_gather | solution.py:198
  309.0 193.5 %copy-start.35 = (f32[160]{0:T(256)}, f32[160]{0:T(256)S(1)}, u32[]{:S(2)}) copy-start(f32[160]{0:T(256)S(1)} %fusion.76) | copy-start | bytes 1924
  311.2 109.7 %all-gather.12.cloned.1.call-start = ((), (), s32[]{:S(2)}) async-start(), calls=%async_computation.12 | async-start | bytes 3276800 | tf_op jit(solution)/shard_map/all_gather | solution.py:213
  311.8 188.2 %reduce-scatter.12.cloned.1.call-start = ((), (), s32[]{:S(2)}) async-start(), calls=%async_computation.13 | async-start | bytes 3276800 | tf_op jit(solution)/shard_map/reduce_scatter | solution.py:222
  365.8 9.6 copy-start.43
  448.9 51.1 %copy-start.8 = (bf16[160,2048]{1,0:T(8,128)(2,1)S(1)}, bf16[160,2048]{1,0:T(8,128)(2,1)}, u32[]{:S(2)}) copy-start(bf16[160,2048]{1,0:T(8,128)(2,1)} %reduce-scatter.8.cloned.1.call-done) | copy-start | bytes 1966084
  449.0 109.6 %all-gather.14.cloned.1.call-start = ((), (), s32[]{:S(2)}) async-start(), calls=%async_computation.14 | async-start | bytes 3276800 | tf_op jit(solution)/shard_map/all_gather | solution.py:234
  502.5 62.0 %copy-start.40 = (f32[160]{0:T(256)}, f32[160]{0:T(256)S(1)}, u32[]{:S(2)}) copy-start(f32[160]{0:T(256)S(1)} %multiply_multiply_fusion.1) | copy-start | bytes 1924
  504.0 368.2 %reduce-scatter.14.cloned.1.call-start = ((), (), s32[]{:S(2)}) async-start(), calls=%async_computation.15 | async-start | bytes 1638400 | tf_op jit(solution)/shard_map/reduce_scatter | solution.py:246
  621.9 481.3 %reduce-scatter.16.cloned.1.call-start = ((), (), s32[]{:S(2)}) async-start(), calls=%async_computation.16 | async-start | bytes 10813440 | tf_op jit(solution)/shard_map/reduce_scatter | solution.py:255
  633.1 239.1 %copy-start.4 = (bf16[160,2048]{1,0:T(8,128)(2,1)S(1)}, bf16[160,2048]{1,0:T(8,128)(2,1)}, u32[]{:S(2)}) copy-start(bf16[160,2048]{1,0:T(8,128)(2,1)} %param.19) | copy-start | bytes 1966084
  633.1 239.1 %copy-start.25 = (f32[2048]{0:T(1024)S(1)}, f32[2048]{0:T(1024)}, u32[]{:S(2)}) copy-start(f32[2048]{0:T(1024)} %param.20) | copy-start | bytes 24580
  633.1 239.1 %copy-start.34 = (f32[160]{0:T(256)S(1)}, f32[160]{0:T(256)}, u32[]{:S(2)}) copy-start(f32[160]{0:T(256)} %copy-done.33) | copy-start | bytes 1924
  633.2 546.9 %reduce-scatter.18.cloned.1.call-start = ((), (), s32[]{:S(2)}) async-start(), calls=%async_computation.17 | async-start | bytes 5242880 | tf_op jit(solution)/shard_map/reduce_scatter | solution.py:274
  876.6 350.3 %reduce-scatter.20.cloned.1.call-start = ((), (), s32[]{:S(2)}) async-start(), calls=%async_computation.18 | async-start | bytes 2621440 | tf_op jit(solution)/shard_map/reduce_scatter | solution.py:277
  1106.3 174.6 %reduce-scatter.10.cloned.1.call-start = ((), (), s32[]{:S(2)}) async-start(), calls=%async_computation.11 | async-start | bytes 3276800 | tf_op jit(solution)/shard_map/reduce_scatter | solution.py:205
  1115.5 483.0 %all-reduce.7.cloned.1.call-start = ((), (), s32[]{:S(2)}) async-start(), calls=%async_computation.19 | async-start | bytes 50331648 | tf_op jit(solution)/shard_map/psum | solution.py:286
  1115.5 8.9 copy-start.44
  1115.6 8.9 copy-start.50
  1232.7 26.9 %copy-start.39 = (f32[160]{0:T(256)S(1)}, f32[160]{0:T(256)}, u32[]{:S(2)}) copy-start(f32[160]{0:T(256)} %copy-done.38) | copy-start | bytes 1924
  1232.7 48.2 %copy-start.9 = (bf16[160,2048]{1,0:T(8,128)(2,1)S(1)}, bf16[160,2048]{1,0:T(8,128)(2,1)}, u32[]{:S(2)}) copy-start(bf16[160,2048]{1,0:T(8,128)(2,1)} %reduce-scatter.8.cloned.1.call-done) | copy-start | bytes 1966084
  1232.7 48.2 %copy-start.28 = (f32[2048]{0:T(1024)S(1)}, f32[2048]{0:T(1024)}, u32[]{:S(2)}) copy-start(f32[2048]{0:T(1024)} %param.25) | copy-start | bytes 24580
  1232.7 48.2 %copy-start.36 = (f32[160]{0:T(256)S(1)}, f32[160]{0:T(256)}, u32[]{:S(2)}) copy-start(f32[160]{0:T(256)} %copy-done.35) | copy-start | bytes 1924
  1232.7 48.2 %copy-start.41 = (f32[160]{0:T(256)S(1)}, f32[160]{0:T(256)}, u32[]{:S(2)}) copy-start(f32[160]{0:T(256)} %copy-done.40) | copy-start | bytes 1924
  1598.5 8.6 copy-start.13
  1598.5 13.8 slice-start
  (37 other events, 125.2 us)
Sparse Core Ops, SparseCore 0:
  13.5 35.3 all-gather.7
  52.4 64.3 all-gather.5
  151.4 156.1 reduce-scatter.7
  311.3 54.4 all-gather.9
  367.2 53.5 all-gather.11
  449.1 50.8 reduce-scatter.11
  504.1 54.4 all-gather.13
  622.0 250.1 reduce-scatter.13
  875.1 227.9 reduce-scatter.15
  1105.8 74.1 reduce-scatter.17
  1182.5 44.3 reduce-scatter.19
  1229.0 51.8 reduce-scatter.9
  1287.2 311.1 all-reduce.6
where the time goes:
time: 1650 us; the launch traced here: 1630 us
  waiting for transfers between devices  1320 us (80%)
  matrix products  146 us (9%)
  other arithmetic  61.7 us (4%)
  local copies, waits for them, and re-layouts  61.6 us (4%)
  blocking collectives  23.5 us (1%)
    psum x1, waiting for transfers between devices, shards(): lax.psum(shared[1].astype(jnp.bfloat16), 'dp').astype(jnp.float32)  313 us
    reduce_scatter x1, waiting for transfers between devices, shards(): lax.psum_scatter(jnp.einsum('tk,rk->tr', query_low, query_up, preferred_e...  239 us
    reduce_scatter x1, waiting for transfers between devices, shards(): lax.psum_scatter(pair_flat_grads, ('dp', 'mp'), scatter_dimension=0, tile...  226 us
    reduce_scatter x1, waiting for transfers between devices, shards(): lax.psum_scatter(jnp.dot(attended, attn_out, preferred_element_type=jnp.f...  156 us
    all_gather x1, waiting for transfers between devices, attention_inputs(): pair_flat = lax.all_gather(pair_local, ('dp', 'mp'), axis=0, tiled=True)  60.1 us
    all_gather x1, waiting for transfers between devices, mlp_inputs(): normal_full = lax.all_gather(normal_two, 'mp', axis=0, tiled=True)  53.5 us
    all_gather x1, waiting for transfers between devices, shards(): lax.all_gather(hidden_grad.astype(jnp.bfloat16), 'mp', axis=0, tiled=True)  53.4 us
    reduce_scatter x1, waiting for transfers between devices, shards(): lax.psum_scatter((jnp.einsum('tf,df->td', gate_low, gate_weight, preferre...  50.8 us
  transfers between devices with their start and end apart: 13, of which 13 were waited for; matrix products, arithmetic and copies ran while one was open for 6% of the time, Pallas kernels for 0%

commit v1 on v0

v1 whole, which is shorter than its diff:
```python
import functools

import jax
import jax.numpy as jnp
from jax import lax
from jax.experimental import pallas as pl
from jax.experimental.pallas import tpu as pltpu
from jax.sharding import PartitionSpec as P

HEAD_DIM = 256
EPS = 1e-06
SHORT_PART = 128
LONG_PART = 512
BLOCK = SHORT_PART + LONG_PART
LOG2E = 1.4426950408889634


def dotf(left, right):
    return jnp.dot(left, right, preferred_element_type=jnp.float32)


def chunks_of(heads):
    short = [(0, heads * SHORT_PART)]
    long = [(heads * SHORT_PART + h * LONG_PART, LONG_PART) for h in range(heads)]
    return ((0, SHORT_PART, short), (SHORT_PART, LONG_PART, long))


def spread(heads, head_dim, source, turned):
    for h in range(heads):
        cols = slice(h * head_dim, (h + 1) * head_dim)
        turned[:, h * SHORT_PART : (h + 1) * SHORT_PART] = source[:SHORT_PART, cols].T
        first = heads * SHORT_PART + h * LONG_PART
        turned[:, first : first + LONG_PART] = source[SHORT_PART:, cols].T


def visible_in(extent, width):
    key_pos = lax.broadcasted_iota(jnp.int32, (extent, width), 0)
    query_pos = lax.broadcasted_iota(jnp.int32, (extent, width), 1) & (extent - 1)
    return key_pos <= query_pos


def forward_kernel(heads, head_dim, group, query, pair, out, kept, logs, turned, maxima, totals):
    factor = head_dim ** (-0.5) * LOG2E
    spread(heads, head_dim, query, turned)
    kept[...] = jnp.zeros_like(kept)
    maxima[...] = jnp.full_like(maxima, -jnp.inf)
    totals[...] = jnp.zeros_like(totals)
    own = group[0]

    def one_block(index, masked):
        for offset, extent, chunks in chunks_of(heads):
            first = pl.multiple_of(index * BLOCK + offset, SHORT_PART)
            keys = pair[pl.ds(first, extent), :head_dim]
            values = pair[pl.ds(first, extent), head_dim:].T
            for column, width in chunks:
                at = slice(column, column + width)
                scores = dotf(keys, turned[:, at]) * factor
                if masked:
                    scores = jnp.where(visible_in(extent, width), scores, -jnp.inf)
                old = maxima[:, at]
                new = jnp.maximum(old, jnp.max(scores, axis=0, keepdims=True))
                rescale = jnp.exp2(old - new)
                weights = jnp.exp2(scores - new)
                maxima[:, at] = new
                totals[:, at] = totals[:, at] * rescale + jnp.sum(weights, axis=0, keepdims=True)
                kept[:, at] = kept[:, at] * rescale + dotf(values, weights.astype(jnp.bfloat16))

    def step(index, carry):
        one_block(index, False)
        return carry

    lax.fori_loop(0, own, step, 0)
    one_block(own, True)
    logs[...] = maxima[...] + jnp.log2(totals[...])
    for h in range(heads):
        cols = slice(h * head_dim, (h + 1) * head_dim)
        for rows, first, width in (
            (slice(0, SHORT_PART), h * SHORT_PART, SHORT_PART),
            (slice(SHORT_PART, BLOCK), heads * SHORT_PART + h * LONG_PART, LONG_PART),
        ):
            at = slice(first, first + width)
            exact = kept[:, at] * (1.0 / totals[:, at])
            kept[:, at] = exact
            out[rows, cols] = exact.T.astype(jnp.bfloat16)


def backward_kernel(
    heads, head_dim, group, query, grad, pair, kept, logs,
    query_grad, pair_grad, turned, grad_turned, total, delta, short_query, short_grad,
):
    scale = head_dim ** (-0.5)
    factor = scale * LOG2E
    spread(heads, head_dim, query, turned)
    spread(heads, head_dim, grad, grad_turned)
    for h in range(heads):
        cols = slice(h * head_dim, (h + 1) * head_dim)
        rows = slice(h * SHORT_PART, (h + 1) * SHORT_PART)
        short_query[rows, :] = query[:SHORT_PART, cols]
        short_grad[rows, :] = grad[:SHORT_PART, cols]
    delta[...] = jnp.sum(grad_turned[...].astype(jnp.float32) * kept[...], axis=0, keepdims=True)
    total[...] = jnp.zeros_like(total)
    own = group[0]

    def one_block(index, masked):
        for offset, extent, chunks in chunks_of(heads):
            first = pl.multiple_of(index * BLOCK + offset, SHORT_PART)
            keys = pair[pl.ds(first, extent), :head_dim]
            values = pair[pl.ds(first, extent), head_dim:]
            keys_turned = keys.T
            key_sum = None
            value_sum = None
            for h, (column, width) in enumerate(chunks):
                at = slice(column, column + width)
                if offset == 0:
                    rows_query, rows_grad = short_query[...], short_grad[...]
                else:
                    cols = slice(h * head_dim, (h + 1) * head_dim)
                    rows_query, rows_grad = query[SHORT_PART:, cols], grad[SHORT_PART:, cols]
                scores = dotf(keys, turned[:, at]) * factor
                chance = jnp.exp2(scores - logs[:, at])
                if masked:
                    chance = jnp.where(visible_in(extent, width), chance, 0.0)
                chance_grad = dotf(values, grad_turned[:, at])
                score_low = (chance * (chance_grad - delta[:, at])).astype(jnp.bfloat16)
                key_part = dotf(score_low, rows_query)
                value_part = dotf(chance.astype(jnp.bfloat16), rows_grad)
                key_sum = key_part if key_sum is None else key_sum + key_part
                value_sum = value_part if value_sum is None else value_sum + value_part
                total[:, at] += dotf(keys_turned, score_low)
            pair_grad[pl.ds(first, extent), :head_dim] = (key_sum * scale).astype(jnp.bfloat16)
            pair_grad[pl.ds(first, extent), head_dim:] = value_sum.astype(jnp.bfloat16)

    def step(index, carry):
        one_block(index, False)
        return carry

    def clear(index, carry):
        first = pl.multiple_of(index * BLOCK, SHORT_PART)
        pair_grad[pl.ds(first, BLOCK), :] = jnp.zeros((BLOCK, 2 * head_dim), jnp.bfloat16)
        return carry

    lax.fori_loop(0, own, step, 0)
    one_block(own, True)
    lax.fori_loop(own + 1, pair.shape[0] // BLOCK, clear, 0)
    for h in range(heads):
        cols = slice(h * head_dim, (h + 1) * head_dim)
        for rows, first, width in (
            (slice(0, SHORT_PART), h * SHORT_PART, SHORT_PART),
            (slice(SHORT_PART, BLOCK), heads * SHORT_PART + h * LONG_PART, LONG_PART),
        ):
            query_grad[rows, cols] = (total[:, first : first + width] * scale).T.astype(jnp.bfloat16)


def whole(count):
    return [pl.BlockSpec(memory_space=pltpu.VMEM)] * count


def attention_forward(group, query, pair, heads, head_dim):
    columns = heads * BLOCK
    return pl.pallas_call(
        functools.partial(forward_kernel, heads, head_dim),
        out_shape=(
            jax.ShapeDtypeStruct(query.shape, jnp.bfloat16),
            jax.ShapeDtypeStruct((head_dim, columns), jnp.float32),
            jax.ShapeDtypeStruct((1, columns), jnp.float32),
        ),
        in_specs=[pl.BlockSpec(memory_space=pltpu.SMEM)] + whole(2),
        out_specs=tuple(whole(3)),
        scratch_shapes=[
            pltpu.VMEM((head_dim, columns), jnp.bfloat16),
            pltpu.VMEM((1, columns), jnp.float32),
            pltpu.VMEM((1, columns), jnp.float32),
        ],
        compiler_params=pltpu.CompilerParams(vmem_limit_bytes=50 << 20),
        cost_estimate=pl.CostEstimate(
            flops=2 * columns * pair.shape[0] * head_dim * 2,
            bytes_accessed=2 * (pair.size + 2 * query.size) + 4 * query.size,
            transcendentals=columns * pair.shape[0] // 2,
        ),
        name="attention_forward",
    )(group, query, pair)


def attention_backward(group, query, grad, pair, kept, logs, heads, head_dim):
    columns = heads * BLOCK
    return pl.pallas_call(
        functools.partial(backward_kernel, heads, head_dim),
        out_shape=(
            jax.ShapeDtypeStruct(query.shape, jnp.bfloat16),
            jax.ShapeDtypeStruct(pair.shape, jnp.bfloat16),
        ),
        in_specs=[pl.BlockSpec(memory_space=pltpu.SMEM)] + whole(5),
        out_specs=tuple(whole(2)),
        scratch_shapes=[
            pltpu.VMEM((head_dim, columns), jnp.bfloat16),
            pltpu.VMEM((head_dim, columns), jnp.bfloat16),
            pltpu.VMEM((head_dim, columns), jnp.float32),
            pltpu.VMEM((1, columns), jnp.float32),
            pltpu.VMEM((heads * SHORT_PART, head_dim), jnp.bfloat16),
            pltpu.VMEM((heads * SHORT_PART, head_dim), jnp.bfloat16),
        ],
        compiler_params=pltpu.CompilerParams(vmem_limit_bytes=56 << 20),
        cost_estimate=pl.CostEstimate(
            flops=2 * columns * pair.shape[0] * head_dim * 5,
            bytes_accessed=2 * (2 * pair.size + 3 * query.size) + 4 * query.size,
            transcendentals=columns * pair.shape[0] // 2,
        ),
        name="attention_backward",
    )(group, query, grad, pair, kept, logs)


def normalize(rows, gain):
    return rows * lax.rsqrt(jnp.mean(rows * rows, axis=-1, keepdims=True) + EPS) * gain


def gated(gate_in, up_in):
    return jax.nn.silu(gate_in) * up_in


def bits_of(count):
    return max(count.bit_length() - 1, 0)


def trade(array, bit):
    count = lax.axis_size("dp")
    return lax.ppermute(array, "dp", [(i, i ^ (1 << bit)) for i in range(count)])


def orders():
    rest = list(range(1, bits_of(lax.axis_size("dp"))))
    return [0] + rest, [0] + rest[::-1]


def halve(array, bit, axis):
    half = array.shape[axis] // 2
    mine = (lax.axis_index("dp") >> bit) & 1
    send = lax.dynamic_slice_in_dim(array, (1 - mine) * half, half, axis)
    keep = lax.dynamic_slice_in_dim(array, mine * half, half, axis)
    return keep, trade(send, bit)


def scatter_sum(array, order, axis):
    for bit in order:
        keep, other = halve(array, bit, axis)
        array = (keep.astype(jnp.float32) + other.astype(jnp.float32)).astype(jnp.bfloat16)
    return array


def gather_pieces(piece, order, axis):
    for bit in order[:0:-1]:
        piece = jnp.concatenate([piece, trade(piece, bit)], axis=axis)
    return piece, trade(piece, 0)


def places(order):
    me = lax.axis_index("dp")
    own = jnp.int32(0)
    for bit in order[1:]:
        own = own * 2 + ((me >> bit) & 1)
    count = 1 << (len(order) - 1)
    relative = jnp.arange(count, dtype=jnp.int32) ^ own
    core = me & 1
    return jnp.concatenate([core * count + relative, (1 - core) * count + relative])


def lay_kernel(arrays, pieces, row_of, column_of, *refs):
    out = refs[arrays]
    step = pl.program_id(0)
    for a in range(arrays):

        @pl.when((step >= a * pieces) & (step < (a + 1) * pieces))
        def _(source=refs[a]):
            out[...] = source[...].astype(jnp.float32)


def lay_out(sets, rows_of, columns_of, axis, shape, name):
    pieces = lax.axis_size("dp") // 2
    block = list(sets[0].shape)
    block[axis] //= pieces

    def source_map(a):
        def at(step, rows, columns):
            piece = jnp.clip(step - a * pieces, 0, pieces - 1)
            return (piece, 0) if axis == 0 else (0, piece)

        return at

    return pl.pallas_call(
        functools.partial(lay_kernel, len(sets), pieces),
        grid_spec=pltpu.PrefetchScalarGridSpec(
            num_scalar_prefetch=2,
            grid=(len(sets) * pieces,),
            in_specs=[pl.BlockSpec(tuple(block), source_map(a)) for a in range(len(sets))],
            out_specs=pl.BlockSpec(
                tuple(block), lambda step, rows, columns: (rows[step], columns[step])
            ),
        ),
        out_shape=jax.ShapeDtypeStruct(shape, jnp.float32),
        compiler_params=pltpu.CompilerParams(vmem_limit_bytes=40 << 20),
        cost_estimate=pl.CostEstimate(
            flops=0, bytes_accessed=6 * shape[0] * shape[1], transcendentals=0
        ),
        name=name,
    )(rows_of, columns_of, *sets)


def sum_both(low, high, axis):
    first, second = orders()
    low = gather_pieces(scatter_sum(low, first, axis), first, axis)
    high = gather_pieces(scatter_sum(high, second, axis), second, axis)
    return (low, places(first)), (high, places(second))


def sum_over_blocks(partial, axis, name):
    half = partial.shape[1 - axis] // 2
    low = lax.slice_in_dim(partial, 0, half, axis=1 - axis)
    high = lax.slice_in_dim(partial, half, 2 * half, axis=1 - axis)
    (low, low_places), (high, high_places) = sum_both(low, high, axis)
    along = jnp.concatenate([low_places, high_places])
    across = (jnp.arange(along.shape[0], dtype=jnp.int32) >= low_places.shape[0]).astype(jnp.int32)
    rows_of, columns_of = (along, across) if axis == 0 else (across, along)
    return lay_out(low + high, rows_of, columns_of, axis, partial.shape, name)


def sum_two_over_blocks(one, two, names):
    outs = []
    for (sets, along), name in zip(sum_both(one, two, 0), names):
        outs.append(lay_out(sets, along, jnp.zeros_like(along), 0, one.shape, name))
    return outs


def sum_small(array):
    for axis in ("mp", "dp"):
        count = lax.axis_size(axis)
        for bit in range(bits_of(count)):
            pairs = [(i, i ^ (1 << bit)) for i in range(count)]
            array = array + lax.ppermute(array, axis, pairs)
    return array


def sum_pairs(pair_grads):
    count = lax.axis_size("dp")
    first, second = orders()
    blocks = pair_grads.reshape(count, -1, pair_grads.shape[1])
    half = blocks.shape[1] // 2

    def halved(array, order):
        pending = list(range(bits_of(count)))
        for bit in order:
            rest = array.shape[1:]
            place = len(pending) - 1 - pending.index(bit)
            pending.remove(bit)
            view = array.reshape((1 << place, 2, -1) + rest)
            mine = (lax.axis_index("dp") >> bit) & 1
            keep = lax.dynamic_slice_in_dim(view, mine, 1, 1).reshape((-1,) + rest)
            send = lax.dynamic_slice_in_dim(view, 1 - mine, 1, 1).reshape((-1,) + rest)
            other = trade(send, bit)
            array = (keep.astype(jnp.float32) + other.astype(jnp.float32)).astype(jnp.bfloat16)
        return array[0]

    low = halved(blocks[:, :half], first)
    high = halved(blocks[:, half:], second)
    return jnp.concatenate([low, high], axis=0)


def shards(
    tokens,
    attn_gain,
    query_down,
    query_up,
    key_value,
    attn_out,
    mlp_gain,
    gate_weight,
    up_weight,
    down_weight,
    out_grad,
):
    head_dim = HEAD_DIM
    local_heads = query_up.shape[1] // head_dim
    ranks = lax.axis_size("mp")
    rank = lax.axis_index("mp")
    group = lax.axis_index("dp").reshape(1)
    share = query_down.shape[0] // ranks

    def gather(rows):
        return lax.all_gather(rows, "mp", axis=0, tiled=True)

    def scatter(rows):
        return lax.psum_scatter(rows, "mp", scatter_dimension=0, tiled=True)

    inputs = tokens.astype(jnp.float32)
    normal_one = normalize(inputs, attn_gain).astype(jnp.bfloat16)
    latent = dotf(normal_one, query_down).astype(jnp.bfloat16)
    pair_local = dotf(normal_one, key_value).astype(jnp.bfloat16)
    latent_full = gather(latent)
    pair_all = lax.all_gather(pair_local, ("dp", "mp"), axis=0, tiled=True)
    grad_full = gather(out_grad)
    normal_share = lax.all_to_all(normal_one, "mp", split_axis=1, concat_axis=0, tiled=True)
    query_full = dotf(latent_full, query_up).astype(jnp.bfloat16)
    attended, kept, logs = attention_forward(group, query_full, pair_all, local_heads, head_dim)
    attended, grad_full, normal_share = lax.optimization_barrier(
        (attended, grad_full, normal_share)
    )
    hidden_res = inputs + scatter(dotf(attended, attn_out).astype(jnp.bfloat16)).astype(jnp.float32)
    normal_two = normalize(hidden_res, mlp_gain).astype(jnp.bfloat16)
    normal_full = gather(normal_two)
    gate = dotf(normal_full, gate_weight)
    upward = dotf(normal_full, up_weight)
    activated = gated(gate, upward).astype(jnp.bfloat16)
    act_grad = jnp.einsum("td,fd->tf", grad_full, down_weight, preferred_element_type=jnp.float32)
    _, gated_pull = jax.vjp(gated, gate, upward)
    gate_grad32, up_grad32 = gated_pull(act_grad)
    gate_low = gate_grad32.astype(jnp.bfloat16)
    up_low = up_grad32.astype(jnp.bfloat16)
    normal_two_grad = scatter(
        (
            jnp.einsum("tf,df->td", gate_low, gate_weight, preferred_element_type=jnp.float32)
            + jnp.einsum("tf,df->td", up_low, up_weight, preferred_element_type=jnp.float32)
        ).astype(jnp.bfloat16)
    ).astype(jnp.float32)

    def weight_grad(left, right):
        return jnp.einsum("tk,td->kd", left, right, preferred_element_type=jnp.float32).astype(
            jnp.bfloat16
        )

    down_sum = sum_over_blocks(weight_grad(activated, grad_full), 1, "down_grad")
    gate_sum, up_sum = sum_two_over_blocks(
        weight_grad(normal_full, gate_low),
        weight_grad(normal_full, up_low),
        ("gate_grad", "up_grad"),
    )
    result = hidden_res + scatter(dotf(activated, down_weight).astype(jnp.bfloat16)).astype(
        jnp.float32
    )
    _, norm_pull_two = jax.vjp(normalize, hidden_res, mlp_gain)
    resid_from_norm, mlp_gain_part = norm_pull_two(normal_two_grad)
    hidden_grad = out_grad.astype(jnp.float32) + resid_from_norm
    branch_full = gather(hidden_grad.astype(jnp.bfloat16))
    attended_low = jnp.einsum(
        "td,kd->tk", branch_full, attn_out, preferred_element_type=jnp.float32
    ).astype(jnp.bfloat16)
    out_sum = sum_over_blocks(weight_grad(attended, branch_full), 0, "attn_out_grad")
    query_low, pair_grads = attention_backward(
        group, query_full, attended_low, pair_all, kept, logs, local_heads, head_dim
    )
    latent_low = scatter(
        jnp.einsum("tk,rk->tr", query_low, query_up, preferred_element_type=jnp.float32).astype(
            jnp.bfloat16
        )
    )
    pair_low = scatter(sum_pairs(pair_grads))
    up_query_sum = sum_over_blocks(weight_grad(latent_full, query_low), 0, "query_up_grad")
    low_full = gather(latent_low)
    pair_full = gather(pair_low)
    down_query_sum = sum_over_blocks(weight_grad(normal_share, low_full), 0, "query_down_grad")
    pair_weight_sum = sum_over_blocks(weight_grad(normal_share, pair_full), 0, "key_value_grad")
    normal_one_grad = jnp.einsum(
        "tr,dr->td", latent_low, query_down, preferred_element_type=jnp.float32
    ) + jnp.einsum("tp,dp->td", pair_low, key_value, preferred_element_type=jnp.float32)
    _, norm_pull_one = jax.vjp(normalize, inputs, attn_gain)
    input_from_norm, attn_gain_part = norm_pull_one(normal_one_grad)
    input_grad = hidden_grad + input_from_norm
    attn_gain_sum = lax.dynamic_slice_in_dim(sum_small(attn_gain_part), rank * share, share)
    mlp_gain_sum = lax.dynamic_slice_in_dim(sum_small(mlp_gain_part), rank * share, share)
    return (
        result.astype(jnp.bfloat16),
        input_grad,
        attn_gain_sum,
        down_query_sum,
        up_query_sum,
        pair_weight_sum,
        out_sum,
        mlp_gain_sum,
        gate_sum,
        up_sum,
        down_sum,
    )


def solution(mesh):
    return jax.shard_map(
        shards,
        mesh=mesh,
        in_specs=(
            P(("dp", "mp"), None),
            P(),
            P(),
            P(None, "mp"),
            P(),
            P("mp", None),
            P(),
            P(None, "mp"),
            P(None, "mp"),
            P("mp", None),
            P(("dp", "mp"), None),
        ),
        out_specs=(
            P(("dp", "mp"), None),
            P(("dp", "mp"), None),
            P("mp"),
            P("mp", None),
            P(None, "mp"),
            P("mp", None),
            P("mp", None),
            P("mp"),
            P(None, "mp"),
            P(None, "mp"),
            P("mp", None),
        ),
        check_vma=False,
    )
```

time: 1650 us -> 924 us (0.56)
  waiting for transfers between devices: 1320 us -> 465 us
  starting transfers between devices: 1.58 us -> 101 us
  Pallas kernels: 0 us -> 90.7 us
  matrix products: 146 us -> 109 us
  local copies, waits for them, and re-layouts: 61.6 us -> 40.7 us
    reduce_scatter x7 -> x5, waiting for transfers between devices: 774 us -> 51 us  [scatter(): return lax.psum_scatter(rows, 'mp', scatter_dimension=0, tiled=True)]
    psum x1 -> x0, waiting for transfers between devices: 313 us -> none  [shards(): lax.psum(shared[1].astype(jnp.bfloat16), 'dp').astype(jnp.float32)]
    ppermute x0 -> x88, waiting for transfers between devices: none -> 209 us  [the longest x78 197 us: trade(): return lax.ppermute(array, 'dp', [(i, i ^ 1 << bit) for i in range(count)])]
    ppermute x0 -> x88, starting transfers between devices: none -> 92.7 us  [the longest x78 86.6 us: trade(): return lax.ppermute(array, 'dp', [(i, i ^ 1 << bit) for i in range(count)])]
    pallas_call x0 -> x9, Pallas kernels: none -> 90.7 us  [the longest x7 71.9 us: lay_out(): pl.pallas_call(functools.partial(lay_kernel, len(sets), pieces), grid_spe...]
    all_gather x5 -> x6, waiting for transfers between devices: 236 us -> 204 us  [the longest x5 139 us: gather(): return lax.all_gather(rows, 'mp', axis=0, tiled=True)]
    dot_general x28 -> x14, matrix products: 104 us -> 71.9 us  [the longest x7 42.9 us: dotf(): return jnp.dot(left, right, preferred_element_type=jnp.float32)]
    concatenate x0 -> x27, other arithmetic: none -> 28.8 us  [the longest x24 27.1 us: gather_pieces(): piece = jnp.concatenate([piece, trade(piece, bit)], axis=axis)]
  transfers between devices with their start and end apart: 13 -> 100, of which waited for: 13 -> 47; matrix products, arithmetic and copies ran while one was open for 6% -> 17% of each run, Pallas kernels for 0% -> 9%
where the time goes in v1:
time: 924 us; the launch traced here: 913 us
  waiting for transfers between devices  465 us (50%)
  matrix products  109 us (12%)
  starting transfers between devices  101 us (11%)
  Pallas kernels  90.7 us (10%)
  other arithmetic  73.6 us (8%)
  local copies, waits for them, and re-layouts  40.7 us (4%)
  blocking collectives  17.5 us (2%)
  between operations  15.6 us (2%)
    ppermute x78, waiting for transfers between devices, trade(): return lax.ppermute(array, 'dp', [(i, i ^ 1 << bit) for i in range(count)])  197 us
    all_gather x5, waiting for transfers between devices, gather(): return lax.all_gather(rows, 'mp', axis=0, tiled=True)  139 us
    ppermute x78, starting transfers between devices, trade(): return lax.ppermute(array, 'dp', [(i, i ^ 1 << bit) for i in range(count)])  86.6 us
    pallas_call x7, Pallas kernels, lay_out(): pl.pallas_call(functools.partial(lay_kernel, len(sets), pieces), grid_spe...  71.9 us
    all_gather x1, waiting for transfers between devices, shards(): pair_all = lax.all_gather(pair_local, ('dp', 'mp'), axis=0, tiled=True)  65 us
    reduce_scatter x5, waiting for transfers between devices, scatter(): return lax.psum_scatter(rows, 'mp', scatter_dimension=0, tiled=True)  51 us
    dot_general x7, matrix products, dotf(): return jnp.dot(left, right, preferred_element_type=jnp.float32)  42.9 us
    dot_general x7, matrix products, weight_grad(): jnp.einsum('tk,td->kd', left, right, preferred_element_type=jnp.float32)  29 us
  transfers between devices with their start and end apart: 100, of which 47 were waited for; matrix products, arithmetic and copies ran while one was open for 17% of the time, Pallas kernels for 9%

profile of v1, /device:TPU:0, one launch (start us, length us, event | category | flops | bytes accessed | tf_op | source)
XLA Modules:
  0.0 913.0 jit_solution(8266549078195413419)
XLA Ops:
  25.7 38.7 %all-gather.7.cloned.1.call-done = bf16[640,1024]{1,0:T(8,128)(2,1)} async-done(((bf16[160,1024]{1,0:T(8,128)(2,1)}), bf16[640,1024]{1,0:T(8,128)(2,1)}) %all-gather.7.cloned.1.call-update) | async-done | bytes 1310736 | tf_op jit(solution)/shard_map/all_gather | solution.py:387
  67.3 65.0 %all-gather.9.cloned.1.call-done.pair = bf16[5120,512]{1,0:T(8,128)(2,1)} async-done(((bf16[160,512]{1,0:T(8,128)(2,1)}), bf16[5120,512]{1,0:T(8,128)(2,1)}) %all-gather.9.cloned.1.call-update) | async-done | bytes 5242896 | tf_op jit(solution)/shard_map/all_gather | solution.py:397
  132.3 7.0 attention_forward.1
  141.0 46.6 %all-gather.11.cloned.1.call-done = bf16[640,2048]{1,0:T(8,128)(2,1)} async-done(((bf16[160,2048]{1,0:T(8,128)(2,1)}), bf16[640,2048]{1,0:T(8,128)(2,1)}) %all-gather.11.cloned.1.call-update) | async-done | bytes 2621456 | tf_op jit(solution)/shard_map/all_gather | solution.py:387
  187.6 7.0 convolution_convert_fusion.5
  194.6 51.0 %reduce-scatter.6.cloned.1.call-done = bf16[160,2048]{1,0:T(8,128)(2,1)} async-done(((bf16[640,2048]{1,0:T(8,128)(2,1)}), bf16[160,2048]{1,0:T(8,128)(2,1)}) %reduce-scatter.6.cloned.1.call-update) | async-done | bytes 655376 | tf_op jit(solution)/shard_map/reduce_scatter | solution.py:390
  249.7 54.1 %all-gather.13.cloned.1.call-done = bf16[640,2048]{1,0:T(8,128)(2,1)} async-done(((bf16[160,2048]{1,0:T(8,128)(2,1)}), bf16[640,2048]{1,0:T(8,128)(2,1)}) %all-gather.13.cloned.1.call-update) | async-done | bytes 2621456 | tf_op jit(solution)/shard_map/all_gather | solution.py:387
  303.8 9.6 %fusion.36 = f32[640,1408]{1,0:T(8,128)} fusion(bf16[640,2048]{1,0:T(8,128)(2,1)} %all-gather.13.cloned.1.call-done, bf16[2048,1408]{1,0:T(8,128)(2,1)} %param.19), kind=kOutput, calls=%fused_computation.190 | convolution fusion | flops 3690987520 | bytes 11993088 | tf_op jit(solution)/shard_map/dot_general | solution.py:19
  313.5 8.8 fusion.35
  322.3 9.3 %multiply_convert_fusion = (bf16[640,1408]{1,0:T(8,128)(2,1)}, bf16[640,1408]{1,0:T(8,128)(2,1)}, bf16[640,1408]{1,0:T(8,128)(2,1)}) fusion(f32[640,1408]{1,0:T(8,128)} %fusion.35, f32[640,1408]{1,0:T(8,128)} %fusion.36, bf16[640,2048]{1,0:T(8,128)(2,1)S(1)} %copy-done.74, bf16[1408,2048]{1,0:T(8,128)(2,1)S(1)} %bitcast.98), kind=kOutput, calls=%fused_computation.11 | convolution fusion | flops 3705405440 | bytes 21004288 | tf_op jit(solution)/shard_map/td,fd->tf/dot_general | solution.py:411
  331.7 7.0 convolution_convert_fusion
  401.3 29.8 %collective-permute-done.71 = bf16[512,1408]{1,0:T(8,128)(2,1)S(1)} collective-permute-done((bf16[512,1408]{1,0:T(8,128)(2,1)S(1)}, bf16[512,1408]{1,0:T(8,128)(2,1)S(1)}, u32[]{:S(2)}, u32[]{:S(2)}) %collective-permute-start.71) | collective-permute-done | bytes 1441824 | tf_op jit(solution)/shard_map/ppermute | solution.py:226
  443.1 9.8 %collective-permute-done.66 = bf16[256,1408]{1,0:T(8,128)(2,1)} collective-permute-done((bf16[256,1408]{1,0:T(8,128)(2,1)}, bf16[256,1408]{1,0:T(8,128)(2,1)}, u32[]{:S(2)}, u32[]{:S(2)}) %collective-permute-start.66) | collective-permute-done | bytes 720928 | tf_op jit(solution)/shard_map/ppermute | solution.py:226
  459.5 14.1 %collective-permute-done.67 = bf16[256,1408]{1,0:T(8,128)(2,1)S(1)} collective-permute-done((bf16[256,1408]{1,0:T(8,128)(2,1)S(1)}, bf16[256,1408]{1,0:T(8,128)(2,1)S(1)}, u32[]{:S(2)}, u32[]{:S(2)}) %collective-permute-start.67) | collective-permute-done | bytes 720928 | tf_op jit(solution)/shard_map/ppermute | solution.py:226
  481.5 35.9 %collective-permute-done.85 = bf16[704,256]{1,0:T(8,128)(2,1)S(1)} collective-permute-done((bf16[704,256]{1,0:T(8,128)(2,1)S(1)}, bf16[704,256]{1,0:T(8,128)(2,1)S(1)}, u32[]{:S(2)}, u32[]{:S(2)}) %collective-permute-start.85) | collective-permute-done | bytes 360480 | tf_op jit(solution)/shard_map/ppermute | solution.py:226
  539.3 6.9 convolution_convert_fusion.7.grad
  546.2 11.8 %attention_backward.1 = (bf16[640,1024]{1,0:T(8,128)(2,1)}, bf16[5120,512]{1,0:T(8,128)(2,1)}) custom-call(s32[1]{0:T(128)} %bitcast.group, bf16[640,1024]{1,0:T(8,128)(2,1)} %copy-done.1, bf16[640,1024]{1,0:T(8,128)(2,1)} %convolution_convert_fusion.7.grad, bf16[5120,512]{1,0:T(8,128)(2,1)} %all-gather.9.cloned.1.call-done.pair, ...), custom_call_target="tpu_custom_call" | custom-call | flops 33554432000 | bytes 17039360 | tf_op jit(solution)/shard_map/attention_backward/pallas_call | solution.py:186
  589.1 8.2 collective-permute-start.24
  597.5 6.4 collective-permute-done.24
  603.9 14.4 %collective-permute-start.30 = (bf16[256,512]{1,0:T(8,128)(2,1)S(1)}, bf16[256,512]{1,0:T(8,128)(2,1)S(1)}, u32[]{:S(2)}, u32[]{:S(2)}) collective-permute-start(bf16[256,512]{1,0:T(8,128)(2,1)S(1)} %constant_dynamic-slice_fusion.25), channel_id=1, source_target_pairs={{0,16},{4,20},{8,24},{12,28},{16,0},{20,4},{24,8},{28,12},{1,17},{... | collective-permute-start | bytes 786440 | tf_op jit(solution)/shard_map/ppermute | solution.py:226
  639.2 10.8 %collective-permute-done.1 = bf16[2,320,512]{2,1,0:T(8,128)(2,1)S(1)} collective-permute-done((bf16[2,320,512]{2,1,0:T(8,128)(2,1)S(1)}, bf16[2,320,512]{2,1,0:T(8,128)(2,1)S(1)}, u32[]{:S(2)}, u32[]{:S(2)}) %collective-permute-start.1) | collective-permute-done | bytes 655392 | tf_op jit(solution)/shard_map/ppermute | solution.py:226
  671.2 8.2 collective-permute-done.48
  687.6 6.8 collective-permute-done.49
  722.8 8.1 convolution_convert_fusion.4
  730.9 12.7 %down_grad.1 = f32[1408,2048]{1,0:T(8,128)} custom-call(s32[16]{0:T(128)S(1)} %compare_convert_fusion.column_of.row_of, s32[16]{0:T(128)S(1)} %pad_add_fusion.row_of.column_of, bf16[704,1024]{1,0:T(8,128)(2,1)S(1)} %pad_maximum_fusion.4.refs_0_, bf16[704,1024]{1,0:T(8,128)(2,1)} %collective-permute-done.81.refs_1_, ...), custom_call_target="tpu_custom_call" | custom-call | bytes 17301504 | tf_op jit(solution)/shard_map/down_grad/pallas_call | solution.py:288
  744.9 9.6 %gate_grad.1 = f32[2048,1408]{1,0:T(8,128)} custom-call(s32[8]{0:T(128)S(1)} %get-tuple-element.49.row_of, s32[8]{0:T(128)S(1)} %broadcast_10_column_of.2.column_of, bf16[1024,1408]{1,0:T(8,128)(2,1)} %pad_maximum_fusion.refs_0_, bf16[1024,1408]{1,0:T(8,128)(2,1)} %collective-permute-done.69.refs_1_), custom_call_target="tpu_custom_call" | custom-call | bytes 17301504 | tf_op jit(solution)/shard_map/gate_grad/pallas_call | solution.py:288
  754.5 9.6 %up_grad.1 = f32[2048,1408]{1,0:T(8,128)} custom-call(s32[8]{0:T(128)S(1)} %get-tuple-element.50.row_of, s32[8]{0:T(128)S(1)} %broadcast_10_column_of.2.column_of, bf16[1024,1408]{1,0:T(8,128)(2,1)} %pad_maximum_fusion.1.refs_0_, bf16[1024,1408]{1,0:T(8,128)(2,1)} %collective-permute-done.75.refs_1_), custom_call_target="tpu_custom_call" | custom-call | bytes 17301504 | tf_op jit(solution)/shard_map/up_grad/pallas_call | solution.py:288
  764.1 11.0 %query_up_grad.1 = f32[1024,1024]{1,0:T(8,128)} custom-call(s32[16]{0:T(128)S(1)} %pad_add_fusion.row_of.column_of, s32[16]{0:T(128)S(1)} %compare_convert_fusion.column_of.row_of, bf16[512,512]{1,0:T(8,128)(2,1)} %pad_maximum_fusion.11.refs_0_, bf16[512,512]{1,0:T(8,128)(2,1)} %collective-permute-done.28.refs_1_, ...), custom_call_target="tpu_custom_call" | custom-call | bytes 6291456 | tf_op jit(solution)/shard_map/query_up_grad/pallas_call | solution.py:288
  786.0 17.5 %all_gather.27 = bf16[640,512]{1,0:T(8,128)(2,1)S(1)} all-gather(bf16[160,512]{1,0:T(8,128)(2,1)S(1)} %copy-done.49), channel_id=1, replica_groups=mesh['dp'=8,'mp'=4] {'mp'}, dimensions={0}, use_global_device_ids=true | all-gather | bytes 819200 | tf_op jit(solution)/shard_map/all_gather | solution.py:387
  877.2 11.5 %attn_out_grad.1 = f32[1024,2048]{1,0:T(8,128)} custom-call(s32[16]{0:T(128)S(1)} %pad_add_fusion.row_of.column_of, s32[16]{0:T(128)S(1)} %compare_convert_fusion.column_of.row_of, bf16[512,1024]{1,0:T(8,128)(2,1)S(1)} %pad_maximum_fusion.6.refs_0_, bf16[512,1024]{1,0:T(8,128)(2,1)} %collective-permute-done.52.refs_1_, ...), custom_call_target="tpu_custom_call" | custom-call | bytes 12582912 | tf_op jit(solution)/shard_map/attn_out_grad/pallas_call | solution.py:288
  888.6 8.3 key_value_grad.1
  897.0 9.2 %query_down_grad.1 = f32[512,1024]{1,0:T(8,128)} custom-call(s32[16]{0:T(128)S(1)} %pad_add_fusion.row_of.column_of, s32[16]{0:T(128)S(1)} %compare_convert_fusion.column_of.row_of, bf16[256,512]{1,0:T(8,128)(2,1)S(1)} %pad_maximum_fusion.15.refs_0_, bf16[256,512]{1,0:T(8,128)(2,1)} %collective-permute-done.16.refs_1_, ...), custom_call_target="tpu_custom_call" | custom-call | bytes 3145728 | tf_op jit(solution)/shard_map/query_down_grad/pallas_call | solution.py:288
  (542 shorter events, 332.8 us)
Async XLA Ops:
  7.2 57.2 %all-gather.7.cloned.1.call-start = ((), (), s32[]{:S(2)}) async-start(), calls=%async_computation.6 | async-start | bytes 1638400 | tf_op jit(solution)/shard_map/all_gather | solution.py:387
  14.9 117.4 %all-gather.9.cloned.1.call-start = ((), (), s32[]{:S(2)}) async-start(), calls=%async_computation.7 | async-start | bytes 5406720 | tf_op jit(solution)/shard_map/all_gather | solution.py:397
  17.7 169.8 %all-gather.11.cloned.1.call-start = ((), (), s32[]{:S(2)}) async-start(), calls=%async_computation.8 | async-start | bytes 3276800 | tf_op jit(solution)/shard_map/all_gather | solution.py:387
  19.4 121.6 %all-to-all-start = ((bf16[160,4,512]{2,0,1:T(8,128)(2,1)}), bf16[160,4,512]{2,0,1:T(8,128)(2,1)}, u32[]{:S(2)}, u32[]{:S(2)}) async-start(bf16[160,4,512]{2,0,1:T(8,128)(2,1)} %bitcast.80), calls=%async_computation | async-start | bytes 1310720 | tf_op jit(solution)/shard_map/all_to_all | solution.py:399
  25.7 219.9 %reduce-scatter.6.cloned.1.call-start = ((), (), s32[]{:S(2)}) async-start(), calls=%async_computation.9 | async-start | bytes 3276800 | tf_op jit(solution)/shard_map/reduce_scatter | solution.py:390
  194.5 109.3 %all-gather.13.cloned.1.call-start = ((), (), s32[]{:S(2)}) async-start(), calls=%async_computation.10 | async-start | bytes 3276800 | tf_op jit(solution)/shard_map/all_gather | solution.py:387
  249.2 186.7 %reduce-scatter.10.cloned.1.call-start = ((), (), s32[]{:S(2)}) async-start(), calls=%async_computation.12 | async-start | bytes 3276800 | tf_op jit(solution)/shard_map/reduce_scatter | solution.py:390
  343.1 35.6 %collective-permute-start.82 = (bf16[704,1024]{1,0:T(8,128)(2,1)}, bf16[704,1024]{1,0:T(8,128)(2,1)}, u32[]{:S(2)}, u32[]{:S(2)}) collective-permute-start(bf16[704,1024]{1,0:T(8,128)(2,1)} %constant_dynamic-slice_fusion.2), channel_id=1, source_target_pairs={{0,4},{4,0},{8,12},{12,8},{16,20},{20,16},{24,28},{28,24},{1,5},{5... | collective-permute-start | bytes 4325384 | tf_op jit(solution)/shard_map/ppermute | solution.py:226
  374.5 164.8 %all-gather.15.cloned.1.call-start = ((), (), s32[]{:S(2)}) async-start(), calls=%async_computation.13 | async-start | bytes 3276800 | tf_op jit(solution)/shard_map/all_gather | solution.py:387
  386.2 44.9 %collective-permute-start.71 = (bf16[512,1408]{1,0:T(8,128)(2,1)S(1)}, bf16[512,1408]{1,0:T(8,128)(2,1)S(1)}, u32[]{:S(2)}, u32[]{:S(2)}) collective-permute-start(bf16[512,1408]{1,0:T(8,128)(2,1)S(1)} %constant_dynamic-slice_fusion.7), channel_id=1, source_target_pairs={{0,16},{4,20},{8,24},{12,28},{16,0},{20,4},{24,8},{28,12},{1,17},{... | collective-permute-start | bytes 4325384 | tf_op jit(solution)/shard_map/ppermute | solution.py:226
  389.8 42.9 %collective-permute-start.65 = (bf16[512,1408]{1,0:T(8,128)(2,1)S(1)}, bf16[512,1408]{1,0:T(8,128)(2,1)S(1)}, u32[]{:S(2)}, u32[]{:S(2)}) collective-permute-start(bf16[512,1408]{1,0:T(8,128)(2,1)S(1)} %constant_dynamic-slice_fusion.10), channel_id=1, source_target_pairs={{0,8},{4,12},{8,0},{12,4},{16,24},{20,28},{24,16},{28,20},{1,9},{5... | collective-permute-start | bytes 4325384 | tf_op jit(solution)/shard_map/ppermute | solution.py:226
  397.4 60.4 %collective-permute-start.78 = (bf16[704,256]{1,0:T(8,128)(2,1)}, bf16[704,256]{1,0:T(8,128)(2,1)}, u32[]{:S(2)}, u32[]{:S(2)}) collective-permute-start(bf16[704,256]{1,0:T(8,128)(2,1)} %constant_dynamic-slice_fusion.3), channel_id=1, source_target_pairs={{0,16},{4,20},{8,24},{12,28},{16,0},{20,4},{24,8},{28,12},{1,17},{... | collective-permute-start | bytes 1081352 | tf_op jit(solution)/shard_map/ppermute | solution.py:226
  439.9 256.1 %reduce-scatter.12.cloned.1.call-start = ((), (), s32[]{:S(2)}) async-start(), calls=%async_computation.14 | async-start | bytes 1638400 | tf_op jit(solution)/shard_map/reduce_scatter | solution.py:390
  474.9 58.0 %collective-permute-start.68 = (bf16[512,1408]{1,0:T(8,128)(2,1)}, bf16[512,1408]{1,0:T(8,128)(2,1)}, u32[]{:S(2)}, u32[]{:S(2)}) collective-permute-start(bf16[512,1408]{1,0:T(8,128)(2,1)} %pad_maximum_fusion.2), channel_id=1, source_target_pairs={{0,8},{4,12},{8,0},{12,4},{16,24},{20,28},{24,16},{28,20},{1,9},{5... | collective-permute-start | bytes 4325384 | tf_op jit(solution)/shard_map/ppermute | solution.py:226
  475.5 41.9 %collective-permute-start.85 = (bf16[704,256]{1,0:T(8,128)(2,1)S(1)}, bf16[704,256]{1,0:T(8,128)(2,1)S(1)}, u32[]{:S(2)}, u32[]{:S(2)}) collective-permute-start(bf16[704,256]{1,0:T(8,128)(2,1)S(1)} %add_convert_fusion.18), channel_id=1, source_target_pairs={{0,8},{4,12},{8,0},{12,4},{16,24},{20,28},{24,16},{28,20},{1,9},{5... | collective-permute-start | bytes 1081352 | tf_op jit(solution)/shard_map/ppermute | solution.py:226
  478.4 57.6 %collective-permute-start.74 = (bf16[512,1408]{1,0:T(8,128)(2,1)}, bf16[512,1408]{1,0:T(8,128)(2,1)}, u32[]{:S(2)}, u32[]{:S(2)}) collective-permute-start(bf16[512,1408]{1,0:T(8,128)(2,1)} %pad_maximum_fusion.3), channel_id=1, source_target_pairs={{0,16},{4,20},{8,24},{12,28},{16,0},{20,4},{24,8},{28,12},{1,17},{... | collective-permute-start | bytes 4325384 | tf_op jit(solution)/shard_map/ppermute | solution.py:226
  481.4 46.3 %collective-permute-start.80 = (bf16[704,512]{1,0:T(8,128)(2,1)S(1)}, bf16[704,512]{1,0:T(8,128)(2,1)}, u32[]{:S(2)}, u32[]{:S(2)}) collective-permute-start(bf16[704,512]{1,0:T(8,128)(2,1)S(1)} %pad_maximum_fusion.8), channel_id=1, source_target_pairs={{0,8},{4,12},{8,0},{12,4},{16,24},{20,28},{24,16},{28,20},{1,9},{5... | collective-permute-start | bytes 2162696 | tf_op jit(solution)/shard_map/ppermute | solution.py:226
  532.4 137.3 %collective-permute-start.62 = (f32[2048]{0:T(1024)S(1)}, f32[2048]{0:T(1024)}, u32[]{:S(2)}, u32[]{:S(2)}) collective-permute-start(f32[2048]{0:T(1024)S(1)} %add.512), channel_id=1, source_target_pairs={{0,8},{4,12},{8,0},{12,4},{16,24},{20,28},{24,16},{28,20},{1,9},{5... | collective-permute-start | bytes 24584 | tf_op jit(solution)/shard_map/ppermute | solution.py:337
  536.0 186.0 %collective-permute-start.69 = (bf16[1024,1408]{1,0:T(8,128)(2,1)}, bf16[1024,1408]{1,0:T(8,128)(2,1)}, u32[]{:S(2)}, u32[]{:S(2)}) collective-permute-start(bf16[1024,1408]{1,0:T(8,128)(2,1)} %pad_maximum_fusion.refs_0_), channel_id=1, source_target_pairs={{0,4},{4,0},{8,12},{12,8},{16,20},{20,16},{24,28},{28,24},{1,5},{5... | collective-permute-start | bytes 8650760 | tf_op jit(solution)/shard_map/ppermute | solution.py:226
  577.4 204.4 %reduce-scatter.14.cloned.1.call-start = ((), (), s32[]{:S(2)}) async-start(), calls=%async_computation.15 | async-start | bytes 819200 | tf_op jit(solution)/shard_map/reduce_scatter | solution.py:390
  586.8 43.3 %collective-permute-start = (bf16[4,320,512]{2,1,0:T(8,128)(2,1)S(1)}, bf16[4,320,512]{2,1,0:T(8,128)(2,1)S(1)}, u32[]{:S(2)}, u32[]{:S(2)}) collective-permute-start(bf16[4,320,512]{2,1,0:T(8,128)(2,1)S(1)} %dynamic-slice_bitcast_fusion.1), channel_id=1, source_target_pairs={{0,4},{4,0},{8,12},{12,8},{16,20},{20,16},{24,28},{28,24},{1,5},{5... | collective-permute-start | bytes 3932168 | tf_op jit(solution)/shard_map/ppermute | solution.py:226
  588.4 43.5 %collective-permute-start.3 = (bf16[4,320,512]{2,1,0:T(8,128)(2,1)S(1)}, bf16[4,320,512]{2,1,0:T(8,128)(2,1)S(1)}, u32[]{:S(2)}, u32[]{:S(2)}) collective-permute-start(bf16[4,320,512]{2,1,0:T(8,128)(2,1)S(1)} %dynamic-slice_bitcast_fusion), channel_id=1, source_target_pairs={{0,4},{4,0},{8,12},{12,8},{16,20},{20,16},{24,28},{28,24},{1,5},{5... | collective-permute-start | bytes 3932168 | tf_op jit(solution)/shard_map/ppermute | solution.py:226
  664.0 166.6 %all-gather.17.cloned.1.call-start = ((), (), s32[]{:S(2)}) async-start(), calls=%async_computation.16 | async-start | bytes 1638400 | tf_op jit(solution)/shard_map/all_gather | solution.py:387
  668.6 85.9 %collective-permute-start.75 = (bf16[1024,1408]{1,0:T(8,128)(2,1)}, bf16[1024,1408]{1,0:T(8,128)(2,1)}, u32[]{:S(2)}, u32[]{:S(2)}) collective-permute-start(bf16[1024,1408]{1,0:T(8,128)(2,1)} %pad_maximum_fusion.1.refs_0_), channel_id=1, source_target_pairs={{0,4},{4,0},{8,12},{12,8},{16,20},{20,16},{24,28},{28,24},{1,5},{5... | collective-permute-start | bytes 8650760 | tf_op jit(solution)/shard_map/ppermute | solution.py:226
  696.0 175.3 %reduce-scatter.8.cloned.1.call-start = ((), (), s32[]{:S(2)}) async-start(), calls=%async_computation.11 | async-start | bytes 3276800 | tf_op jit(solution)/shard_map/reduce_scatter | solution.py:390
  718.6 45.5 %collective-permute-start.28 = (bf16[512,512]{1,0:T(8,128)(2,1)}, bf16[512,512]{1,0:T(8,128)(2,1)}, u32[]{:S(2)}, u32[]{:S(2)}) collective-permute-start(bf16[512,512]{1,0:T(8,128)(2,1)} %pad_maximum_fusion.11.refs_0_), channel_id=1, source_target_pairs={{0,4},{4,0},{8,12},{12,8},{16,20},{20,16},{24,28},{28,24},{1,5},{5... | collective-permute-start | bytes 1572872 | tf_op jit(solution)/shard_map/ppermute | solution.py:226
  718.7 45.4 %collective-permute-start.34 = (bf16[512,512]{1,0:T(8,128)(2,1)}, bf16[512,512]{1,0:T(8,128)(2,1)}, u32[]{:S(2)}, u32[]{:S(2)}) collective-permute-start(bf16[512,512]{1,0:T(8,128)(2,1)} %pad_maximum_fusion.12.refs_2_), channel_id=1, source_target_pairs={{0,4},{4,0},{8,12},{12,8},{16,20},{20,16},{24,28},{28,24},{1,5},{5... | collective-permute-start | bytes 1572872 | tf_op jit(solution)/shard_map/ppermute | solution.py:226
  721.2 53.9 %collective-permute-start.51 = (bf16[256,1024]{1,0:T(8,128)(2,1)}, bf16[256,1024]{1,0:T(8,128)(2,1)}, u32[]{:S(2)}, u32[]{:S(2)}) collective-permute-start(bf16[256,1024]{1,0:T(8,128)(2,1)} %pad_maximum_fusion.13), channel_id=1, source_target_pairs={{0,8},{4,12},{8,0},{12,4},{16,24},{20,28},{24,16},{28,20},{1,9},{5... | collective-permute-start | bytes 1572872 | tf_op jit(solution)/shard_map/ppermute | solution.py:226
  722.0 54.5 %collective-permute-start.57 = (bf16[256,1024]{1,0:T(8,128)(2,1)}, bf16[256,1024]{1,0:T(8,128)(2,1)}, u32[]{:S(2)}, u32[]{:S(2)}) collective-permute-start(bf16[256,1024]{1,0:T(8,128)(2,1)} %pad_maximum_fusion.14), channel_id=1, source_target_pairs={{0,16},{4,20},{8,24},{12,28},{16,0},{20,4},{24,8},{28,12},{1,17},{... | collective-permute-start | bytes 1572872 | tf_op jit(solution)/shard_map/ppermute | solution.py:226
  776.5 94.7 %collective-permute-start.52 = (bf16[512,1024]{1,0:T(8,128)(2,1)S(1)}, bf16[512,1024]{1,0:T(8,128)(2,1)}, u32[]{:S(2)}, u32[]{:S(2)}) collective-permute-start(bf16[512,1024]{1,0:T(8,128)(2,1)S(1)} %pad_maximum_fusion.6.refs_0_), channel_id=1, source_target_pairs={{0,4},{4,0},{8,12},{12,8},{16,20},{20,16},{24,28},{28,24},{1,5},{5... | collective-permute-start | bytes 3145736 | tf_op jit(solution)/shard_map/ppermute | solution.py:226
  778.7 98.5 %collective-permute-start.58 = (bf16[512,1024]{1,0:T(8,128)(2,1)}, bf16[512,1024]{1,0:T(8,128)(2,1)}, u32[]{:S(2)}, u32[]{:S(2)}) collective-permute-start(bf16[512,1024]{1,0:T(8,128)(2,1)} %pad_maximum_fusion.7.refs_2_), channel_id=1, source_target_pairs={{0,4},{4,0},{8,12},{12,8},{16,20},{20,16},{24,28},{28,24},{1,5},{5... | collective-permute-start | bytes 3145736 | tf_op jit(solution)/shard_map/ppermute | solution.py:226
  815.4 55.3 %collective-permute-start.10 = (f32[2048]{0:T(1024)}, f32[2048]{0:T(1024)}, u32[]{:S(2)}, u32[]{:S(2)}) collective-permute-start(f32[2048]{0:T(1024)} %add.459), channel_id=1, source_target_pairs={{0,16},{4,20},{8,24},{12,28},{16,0},{20,4},{24,8},{28,12},{1,17},{... | collective-permute-start | bytes 24584 | tf_op jit(solution)/shard_map/ppermute | solution.py:337
  (159 other events, 2066.6 us)
Sparse Core Ops, SparseCore 0:
  15.0 49.3 all-gather.6
  67.8 64.3 all-gather.8
  133.8 53.6 all-gather.10
  194.7 50.8 reduce-scatter.5
  249.3 54.4 all-gather.12
  374.6 50.8 reduce-scatter.9
  440.0 52.6 all-gather.14
  577.5 52.8 reduce-scatter.11
  664.1 19.6 reduce-scatter.13
  696.1 30.1 all-gather.16
  731.0 50.6 reduce-scatter.7

commit v2 on v1

v2 whole, which is shorter than its diff:
```python
import functools

import jax
import jax.numpy as jnp
from jax import lax
from jax.experimental import pallas as pl
from jax.experimental.pallas import tpu as pltpu
from jax.sharding import PartitionSpec as P

HEAD_DIM = 256
EPS = 1e-06
SHORT_PART = 128
LONG_PART = 512
BLOCK = SHORT_PART + LONG_PART
LOG2E = 1.4426950408889634


def dotf(left, right):
    return jnp.dot(left, right, preferred_element_type=jnp.float32)


def turned_bits(value, count):
    return sum(((value >> b) & 1) << (count - 1 - b) for b in range(count))


def bits_of(count):
    return max(count.bit_length() - 1, 0)


def chunks_of(heads):
    short = [(0, heads * SHORT_PART)]
    long = [(heads * SHORT_PART + h * LONG_PART, LONG_PART) for h in range(heads)]
    return ((0, SHORT_PART, short), (SHORT_PART, LONG_PART, long))


def spread(heads, head_dim, source, turned):
    for h in range(heads):
        cols = slice(h * head_dim, (h + 1) * head_dim)
        turned[:, h * SHORT_PART : (h + 1) * SHORT_PART] = source[:SHORT_PART, cols].T
        first = heads * SHORT_PART + h * LONG_PART
        turned[:, first : first + LONG_PART] = source[SHORT_PART:, cols].T


def visible_in(extent, width):
    key_pos = lax.broadcasted_iota(jnp.int32, (extent, width), 0)
    query_pos = lax.broadcasted_iota(jnp.int32, (extent, width), 1) & (extent - 1)
    return key_pos <= query_pos


def block_copies(own, sources, all_keys, all_values, sems):
    copies = []
    for kind, (parts, target) in enumerate(((sources[:4], all_keys), (sources[4:], all_values))):
        held = parts[0].shape[0] // BLOCK
        bits = bits_of(2 * held)
        for place, part in enumerate(parts):
            for i in range(held):
                relative = place % 2 * held + i
                if kind == 1:
                    relative = turned_bits(relative, bits)
                index = own ^ (2 * relative + place // 2)
                first = pl.multiple_of(index * BLOCK, BLOCK)
                copies.append(
                    pltpu.make_async_copy(
                        part.at[pl.ds(i * BLOCK, BLOCK), :],
                        target.at[pl.ds(first, BLOCK), :],
                        sems.at[len(copies)],
                    )
                )
    return copies


def forward_kernel(
    heads, head_dim, group, query, *refs
):
    sources, (out, kept, logs, turned, maxima, totals, all_keys, all_values, sems) = (
        refs[:8],
        refs[8:],
    )
    factor = head_dim ** (-0.5) * LOG2E
    own = group[0]
    copies = block_copies(own, sources, all_keys, all_values, sems)
    for copy in copies:
        copy.start()
    spread(heads, head_dim, query, turned)
    kept[...] = jnp.zeros_like(kept)
    maxima[...] = jnp.full_like(maxima, -jnp.inf)
    totals[...] = jnp.zeros_like(totals)
    for copy in copies:
        copy.wait()

    def one_block(index, masked):
        for offset, extent, chunks in chunks_of(heads):
            first = pl.multiple_of(index * BLOCK + offset, SHORT_PART)
            keys = all_keys[pl.ds(first, extent), :]
            values = all_values[pl.ds(first, extent), :].T
            for column, width in chunks:
                at = slice(column, column + width)
                scores = dotf(keys, turned[:, at]) * factor
                if masked:
                    scores = jnp.where(visible_in(extent, width), scores, -jnp.inf)
                old = maxima[:, at]
                new = jnp.maximum(old, jnp.max(scores, axis=0, keepdims=True))
                rescale = jnp.exp2(old - new)
                weights = jnp.exp2(scores - new)
                maxima[:, at] = new
                totals[:, at] = totals[:, at] * rescale + jnp.sum(weights, axis=0, keepdims=True)
                kept[:, at] = kept[:, at] * rescale + dotf(values, weights.astype(jnp.bfloat16))

    def step(index, carry):
        one_block(index, False)
        return carry

    lax.fori_loop(0, own, step, 0)
    one_block(own, True)
    logs[...] = maxima[...] + jnp.log2(totals[...])
    for h in range(heads):
        cols = slice(h * head_dim, (h + 1) * head_dim)
        for rows, first, width in (
            (slice(0, SHORT_PART), h * SHORT_PART, SHORT_PART),
            (slice(SHORT_PART, BLOCK), heads * SHORT_PART + h * LONG_PART, LONG_PART),
        ):
            at = slice(first, first + width)
            exact = kept[:, at] * (1.0 / totals[:, at])
            kept[:, at] = exact
            out[rows, cols] = exact.T.astype(jnp.bfloat16)


def backward_kernel(heads, head_dim, group, query, grad, kept, logs, *refs):
    sources = refs[:8]
    query_grad, key_grad, value_grad = refs[8:11]
    turned, grad_turned, total, delta, short_query, short_grad = refs[11:17]
    all_keys, all_values, sems = refs[17:]
    scale = head_dim ** (-0.5)
    factor = scale * LOG2E
    own = group[0]
    count = all_keys.shape[0] // BLOCK
    bits = bits_of(count) - 1
    copies = block_copies(own, sources, all_keys, all_values, sems)
    for copy in copies:
        copy.start()
    spread(heads, head_dim, query, turned)
    spread(heads, head_dim, grad, grad_turned)
    for h in range(heads):
        cols = slice(h * head_dim, (h + 1) * head_dim)
        rows = slice(h * SHORT_PART, (h + 1) * SHORT_PART)
        short_query[rows, :] = query[:SHORT_PART, cols]
        short_grad[rows, :] = grad[:SHORT_PART, cols]
    delta[...] = jnp.sum(grad_turned[...].astype(jnp.float32) * kept[...], axis=0, keepdims=True)
    total[...] = jnp.zeros_like(total)
    for copy in copies:
        copy.wait()

    def places(index):
        relative = index ^ own
        core, rest = relative & 1, relative >> 1
        key_place = core * (count // 2) + turned_bits(rest, bits)
        return key_place * BLOCK, (core * (count // 2) + rest) * BLOCK

    def one_block(index, masked):
        key_first, value_first = places(index)
        for offset, extent, chunks in chunks_of(heads):
            first = pl.multiple_of(index * BLOCK + offset, SHORT_PART)
            keys = all_keys[pl.ds(first, extent), :]
            values = all_values[pl.ds(first, extent), :]
            keys_turned = keys.T
            key_sum = None
            value_sum = None
            for h, (column, width) in enumerate(chunks):
                at = slice(column, column + width)
                if offset == 0:
                    rows_query, rows_grad = short_query[...], short_grad[...]
                else:
                    cols = slice(h * head_dim, (h + 1) * head_dim)
                    rows_query, rows_grad = query[SHORT_PART:, cols], grad[SHORT_PART:, cols]
                scores = dotf(keys, turned[:, at]) * factor
                chance = jnp.exp2(scores - logs[:, at])
                if masked:
                    chance = jnp.where(visible_in(extent, width), chance, 0.0)
                chance_grad = dotf(values, grad_turned[:, at])
                score_low = (chance * (chance_grad - delta[:, at])).astype(jnp.bfloat16)
                key_part = dotf(score_low, rows_query)
                value_part = dotf(chance.astype(jnp.bfloat16), rows_grad)
                key_sum = key_part if key_sum is None else key_sum + key_part
                value_sum = value_part if value_sum is None else value_sum + value_part
                total[:, at] += dotf(keys_turned, score_low)
            key_rows = pl.ds(pl.multiple_of(key_first + offset, SHORT_PART), extent)
            value_rows = pl.ds(pl.multiple_of(value_first + offset, SHORT_PART), extent)
            key_grad[key_rows, :] = (key_sum * scale).astype(jnp.bfloat16)
            value_grad[value_rows, :] = value_sum.astype(jnp.bfloat16)

    def step(index, carry):
        one_block(index, False)
        return carry

    def clear(index, carry):
        nothing = jnp.zeros((BLOCK, head_dim), jnp.bfloat16)
        key_first, value_first = places(index)
        key_grad[pl.ds(pl.multiple_of(key_first, SHORT_PART), BLOCK), :] = nothing
        value_grad[pl.ds(pl.multiple_of(value_first, SHORT_PART), BLOCK), :] = nothing
        return carry

    lax.fori_loop(0, own, step, 0)
    one_block(own, True)
    lax.fori_loop(own + 1, count, clear, 0)
    for h in range(heads):
        cols = slice(h * head_dim, (h + 1) * head_dim)
        for rows, first, width in (
            (slice(0, SHORT_PART), h * SHORT_PART, SHORT_PART),
            (slice(SHORT_PART, BLOCK), heads * SHORT_PART + h * LONG_PART, LONG_PART),
        ):
            query_grad[rows, cols] = (total[:, first : first + width] * scale).T.astype(jnp.bfloat16)


def in_vmem(count):
    return [pl.BlockSpec(memory_space=pltpu.VMEM)] * count


def gathered_scratch(sources, head_dim):
    rows = sum(part.shape[0] for part in sources[:4])
    return [
        pltpu.VMEM((rows, head_dim), jnp.bfloat16),
        pltpu.VMEM((rows, head_dim), jnp.bfloat16),
        pltpu.SemaphoreType.DMA((2 * rows // BLOCK,)),
    ], rows


def attention_forward(group, query, sources, heads, head_dim):
    columns = heads * BLOCK
    scratch, rows = gathered_scratch(sources, head_dim)
    return pl.pallas_call(
        functools.partial(forward_kernel, heads, head_dim),
        out_shape=(
            jax.ShapeDtypeStruct(query.shape, jnp.bfloat16),
            jax.ShapeDtypeStruct((head_dim, columns), jnp.float32),
            jax.ShapeDtypeStruct((1, columns), jnp.float32),
        ),
        in_specs=[pl.BlockSpec(memory_space=pltpu.SMEM)]
        + in_vmem(1)
        + [pl.BlockSpec(memory_space=pl.ANY)] * 8,
        out_specs=tuple(in_vmem(3)),
        scratch_shapes=[
            pltpu.VMEM((head_dim, columns), jnp.bfloat16),
            pltpu.VMEM((1, columns), jnp.float32),
            pltpu.VMEM((1, columns), jnp.float32),
        ]
        + scratch,
        compiler_params=pltpu.CompilerParams(vmem_limit_bytes=50 << 20),
        cost_estimate=pl.CostEstimate(
            flops=2 * columns * rows * head_dim * 2,
            bytes_accessed=4 * rows * head_dim + 8 * query.size,
            transcendentals=columns * rows // 2,
        ),
        name="attention_forward",
    )(group, query, *sources)


def attention_backward(group, query, grad, sources, kept, logs, heads, head_dim):
    columns = heads * BLOCK
    scratch, rows = gathered_scratch(sources, head_dim)
    return pl.pallas_call(
        functools.partial(backward_kernel, heads, head_dim),
        out_shape=(
            jax.ShapeDtypeStruct(query.shape, jnp.bfloat16),
            jax.ShapeDtypeStruct((rows, head_dim), jnp.bfloat16),
            jax.ShapeDtypeStruct((rows, head_dim), jnp.bfloat16),
        ),
        in_specs=[pl.BlockSpec(memory_space=pltpu.SMEM)]
        + in_vmem(4)
        + [pl.BlockSpec(memory_space=pl.ANY)] * 8,
        out_specs=tuple(in_vmem(3)),
        scratch_shapes=[
            pltpu.VMEM((head_dim, columns), jnp.bfloat16),
            pltpu.VMEM((head_dim, columns), jnp.bfloat16),
            pltpu.VMEM((head_dim, columns), jnp.float32),
            pltpu.VMEM((1, columns), jnp.float32),
            pltpu.VMEM((heads * SHORT_PART, head_dim), jnp.bfloat16),
            pltpu.VMEM((heads * SHORT_PART, head_dim), jnp.bfloat16),
        ]
        + scratch,
        compiler_params=pltpu.CompilerParams(vmem_limit_bytes=56 << 20),
        cost_estimate=pl.CostEstimate(
            flops=2 * columns * rows * head_dim * 5,
            bytes_accessed=8 * rows * head_dim + 10 * query.size,
            transcendentals=columns * rows // 2,
        ),
        name="attention_backward",
    )(group, query, grad, kept, logs, *sources)


def normalize(rows, gain):
    return rows * lax.rsqrt(jnp.mean(rows * rows, axis=-1, keepdims=True) + EPS) * gain


def gated(gate_in, up_in):
    return jax.nn.silu(gate_in) * up_in


class Order:
    def __init__(self):
        self.last = ()

    def take(self, *values):
        out = lax.optimization_barrier(values + self.last)[: len(values)]
        return out if len(values) > 1 else out[0]

    def mark(self, *values):
        self.last = tuple(jax.tree.leaves(values))


def add_low(left, right):
    return (left.astype(jnp.float32) + right.astype(jnp.float32)).astype(jnp.bfloat16)


def ring_of(count):
    return [0] + list(range(1, count, 2)) + list(range(2, count, 2))[::-1]


def ring_place(back):
    ring = ring_of(lax.axis_size("mp"))
    count = len(ring)
    table = [ring[(ring.index(i) - back) % count] for i in range(count)]
    return jnp.asarray(table, jnp.int32)[lax.axis_index("mp")]


def ring_pass(array):
    ring = ring_of(lax.axis_size("mp"))
    pairs = [(ring[i], ring[(i + 1) % len(ring)]) for i in range(len(ring))]
    return lax.ppermute(array, "mp", pairs)


def put_rows(whole_rows, rows, place):
    return lax.dynamic_update_slice_in_dim(whole_rows, rows, place * rows.shape[0], 0)


def take_rows(whole_rows, place):
    count = whole_rows.shape[0] // lax.axis_size("mp")
    return lax.dynamic_slice_in_dim(whole_rows, place * count, count, 0)


def ring_rows(parts):
    out = jnp.zeros((parts[0].shape[0] * len(parts),) + parts[0].shape[1:], parts[0].dtype)
    for step, rows in enumerate(parts):
        out = put_rows(out, rows, ring_place(step))
    return out


class RingGather:
    def __init__(self, rows):
        self.parts = [rows]
        self.start()

    def start(self):
        if len(self.parts) < lax.axis_size("mp"):
            self.flying = ring_pass(self.parts[-1])

    def step(self, order):
        if len(self.parts) < lax.axis_size("mp"):
            rows = order.take(self.flying)
            order.mark(rows)
            self.parts.append(rows)
            self.start()

    def steps_left(self):
        return lax.axis_size("mp") - len(self.parts)

    def rows(self):
        return ring_rows(self.parts)


class RingScatter:
    def __init__(self, partial):
        self.partial, self.steps = partial, 1
        self.held = take_rows(partial, ring_place(1))
        self.flying = ring_pass(self.held)

    def step(self, order):
        if self.steps_left():
            got, partial = order.take(self.flying, self.partial)
            self.steps += 1
            self.held = add_low(take_rows(partial, ring_place(self.steps)), got)
            order.mark(self.held)
            if self.steps_left():
                self.flying = ring_pass(self.held)

    def steps_left(self):
        return lax.axis_size("mp") - self.steps


def trade(array, bit):
    count = lax.axis_size("dp")
    return lax.ppermute(array, "dp", [(i, i ^ (1 << bit)) for i in range(count)])


def bit_here(bit):
    return (lax.axis_index("dp") >> bit) & 1


def orders():
    rest = list(range(1, bits_of(lax.axis_size("dp"))))
    return [0] + rest, [0] + rest[::-1]


class Lane:
    def __init__(self, partial, order, axis):
        self.bits, self.axis = order, axis
        self.steps = [("halve", bit) for bit in order]
        self.steps += [("double", bit) for bit in order[:0:-1]] + [("core", 0)]
        self.cut_and_start(lambda which, half: self.cut(partial, which, half), partial.shape[axis])

    def cut(self, array, which, half):
        return lax.dynamic_slice_in_dim(array, which * half, half, self.axis)

    def cut_and_start(self, part, extent):
        bit = self.steps[0][1]
        mine = bit_here(bit)
        self.sent, self.held = part(1 - mine, extent // 2), part(mine, extent // 2)
        self.flying = trade(self.sent, bit)

    def step(self, order):
        kind, _ = self.steps.pop(0)
        got, held = order.take(self.flying, self.held)
        if not self.steps:
            self.pieces = [held, got]
            order.mark(self.pieces)
            return
        following, bit = self.steps[0]
        if kind == "halve" and following == "halve":
            self.cut_and_start(
                lambda which, half: add_low(self.cut(held, which, half), self.cut(got, which, half)),
                held.shape[self.axis],
            )
        else:
            if kind == "halve":
                self.held = add_low(held, got)
            else:
                self.held = jnp.concatenate([held, got], axis=self.axis)
            self.sent = self.held
            self.flying = trade(self.sent, bit)
        order.mark(self.sent, self.held)

    def places(self):
        own = jnp.int32(0)
        for bit in self.bits[1:]:
            own = own * 2 + bit_here(bit)
        count = 1 << (len(self.bits) - 1)
        relative = jnp.arange(count, dtype=jnp.int32) ^ own
        core = bit_here(0)
        return jnp.concatenate([core * count + relative, (1 - core) * count + relative])


def lay_kernel(sets, pieces, axis, split, places, *refs):
    sources, out = refs[:sets], refs[sets]
    landed, raised, in_sems, out_sems = refs[sets + 1 :]
    total, slots = sets * pieces, raised.shape[0]
    rows, columns = landed.shape[1:]

    def fetch(i):
        first = i % pieces * (rows, columns)[axis]
        source = sources[i // pieces]
        window = (
            source.at[pl.ds(first, rows), :] if axis == 0 else source.at[:, pl.ds(first, columns)]
        )
        return pltpu.make_async_copy(window, landed.at[i], in_sems.at[i])

    def store(i):
        along = places[i]
        across = i * split // total
        if axis == 0:
            window = out.at[
                pl.ds(pl.multiple_of(along * rows, rows), rows), pl.ds(across * columns, columns)
            ]
        else:
            window = out.at[
                pl.ds(across * rows, rows), pl.ds(pl.multiple_of(along * columns, 128), columns)
            ]
        return pltpu.make_async_copy(raised.at[i % slots], window, out_sems.at[i])

    for i in range(total):
        fetch(i).start()
    for i in range(total):
        fetch(i).wait()
        if i >= slots:
            store(i - slots).wait()
        raised[i % slots] = landed[i].astype(jnp.float32)
        store(i).start()
    for i in range(max(total - slots, 0), total):
        store(i).wait()


def lay_out(lanes, shape, name):
    sets = [piece for lane in lanes for piece in lane.pieces]
    axis = lanes[0].axis
    places = jnp.concatenate([lane.places() for lane in lanes])
    pieces = places.shape[0] // len(sets)
    block = list(sets[0].shape)
    block[axis] //= pieces
    total = len(sets) * pieces
    anywhere = pl.BlockSpec(memory_space=pl.ANY)
    return pl.pallas_call(
        functools.partial(lay_kernel, len(sets), pieces, axis, len(lanes)),
        in_specs=[pl.BlockSpec(memory_space=pltpu.SMEM)] + [anywhere] * len(sets),
        out_specs=anywhere,
        out_shape=jax.ShapeDtypeStruct(shape, jnp.float32),
        scratch_shapes=[
            pltpu.VMEM((total, *block), jnp.bfloat16),
            pltpu.VMEM((min(total, 6), *block), jnp.float32),
            pltpu.SemaphoreType.DMA((total,)),
            pltpu.SemaphoreType.DMA((total,)),
        ],
        compiler_params=pltpu.CompilerParams(vmem_limit_bytes=40 << 20),
        cost_estimate=pl.CostEstimate(
            flops=0, bytes_accessed=6 * shape[0] * shape[1], transcendentals=0
        ),
        name=name,
    )(places, *sets)


def sum_halves(partial, axis):
    first, second = orders()
    half = partial.shape[1 - axis] // 2
    low = lax.slice_in_dim(partial, 0, half, axis=1 - axis)
    high = lax.slice_in_dim(partial, half, 2 * half, axis=1 - axis)
    return [Lane(low, first, axis), Lane(high, second, axis)]


def sum_ranks(array):
    count = lax.axis_size("mp")
    for bit in range(bits_of(count)):
        array = array + lax.ppermute(array, "mp", [(i, i ^ (1 << bit)) for i in range(count)])
    return array


def own_share(array):
    share = array.shape[0] // lax.axis_size("mp")
    return lax.dynamic_slice_in_dim(array, lax.axis_index("mp") * share, share)


class BlockSum:
    def __init__(self, blocks, order):
        self.bits = list(order)
        half = blocks.shape[0] // 2
        self.held, self.sent = blocks[:half], blocks[half:]
        self.flying = trade(self.sent, self.bits[0])

    def step(self, order):
        self.bits.pop(0)
        got, held = order.take(self.flying, self.held)
        if self.bits:
            half = held.shape[0] // 2
            self.sent = add_low(held[half:], got[half:])
            self.held = add_low(held[:half], got[:half])
            self.flying = trade(self.sent, self.bits[0])
        else:
            self.held = self.sent = add_low(held, got)
        order.mark(self.sent, self.held)


class BlockGather:
    def __init__(self, rows, order):
        self.bits, self.held = list(order), rows
        self.flying = trade(rows, self.bits[0])

    def step(self, order):
        if not self.bits:
            got = order.take(*self.flying)
            order.mark(got)
            self.parts = self.held + list(got)
            return
        self.bits.pop(0)
        got, held = order.take(self.flying, self.held)
        if self.bits:
            self.held = jnp.concatenate([held, got], axis=0)
            self.flying = trade(self.held, self.bits[0])
        else:
            self.held = [held, got]
            self.flying = [trade(part, 0) for part in self.held]
        order.mark(self.held)


class SmallSum:
    def __init__(self, array, axis):
        self.axis, self.held = axis, array
        self.bits = list(range(bits_of(lax.axis_size(axis))))
        self.start()

    def start(self):
        if self.bits:
            count = lax.axis_size(self.axis)
            pairs = [(i, i ^ (1 << self.bits[0])) for i in range(count)]
            self.flying = lax.ppermute(self.held, self.axis, pairs)

    def step(self, order):
        if self.bits:
            self.bits.pop(0)
            got, held = order.take(self.flying, self.held)
            self.held = held + got
            order.mark(self.held)
            self.start()


def column_share(rows):
    ring = ring_of(lax.axis_size("mp"))
    count = len(ring)
    width = rows.shape[1] // count
    parts = []
    for step in range(count):
        part = lax.dynamic_slice_in_dim(rows, ring_place(-step) * width, width, 1)
        pairs = [(ring[i], ring[(i + step) % count]) for i in range(count)]
        parts.append(lax.ppermute(part, "mp", pairs) if step else part)
    return parts


def shards(
    tokens,
    attn_gain,
    query_down,
    query_up,
    key_value,
    attn_out,
    mlp_gain,
    gate_weight,
    up_weight,
    down_weight,
    out_grad,
):
    head_dim = HEAD_DIM
    local_heads = query_up.shape[1] // head_dim
    ranks = lax.axis_size("mp")
    group = lax.axis_index("dp").reshape(1)
    first, second = orders()

    def gather(rows):
        return lax.all_gather(rows, "mp", axis=0, tiled=True)

    def scatter(rows):
        return lax.psum_scatter(rows, "mp", scatter_dimension=0, tiled=True)

    def weight_grad(left, right):
        return jnp.einsum("tk,td->kd", left, right, preferred_element_type=jnp.float32).astype(
            jnp.bfloat16
        )

    def steps(*moving):
        for one in moving:
            one.step(order)

    def finish(*lanes):
        while lanes[0].steps:
            steps(*lanes)

    order = Order()
    inputs = tokens.astype(jnp.float32)
    normal_one = normalize(inputs, attn_gain).astype(jnp.bfloat16)
    pair_local = dotf(normal_one, key_value).astype(jnp.bfloat16)
    order.mark(pair_local)
    pair_ring = RingGather(pair_local)
    latent = dotf(order.take(normal_one), query_down).astype(jnp.bfloat16)
    order.mark(latent)
    latent_ring = RingGather(latent)
    while pair_ring.steps_left() > 1:
        steps(pair_ring, latent_ring)
    steps(pair_ring)
    pair_own = pair_ring.rows()
    order.mark(pair_own)
    keys = BlockGather(pair_own[:, :head_dim], first[1:])
    values = BlockGather(pair_own[:, head_dim:], second[1:])
    while latent_ring.steps_left():
        steps(latent_ring)
    grad_ring = RingGather(order.take(out_grad))
    latent_full = order.take(latent_ring.rows())
    query_full = dotf(latent_full, query_up).astype(jnp.bfloat16)
    order.mark(query_full)
    steps(keys, values, grad_ring)
    while keys.bits:
        steps(keys, values)
    steps(grad_ring, keys, values)
    sources = order.take(*keys.parts, *values.parts)
    attended, kept, logs = attention_forward(group, query_full, sources, local_heads, head_dim)
    order.mark(attended)
    steps(grad_ring)
    share_parts = column_share(order.take(normal_one))
    attn_partial = dotf(order.take(attended), attn_out).astype(jnp.bfloat16)
    order.mark(attn_partial)
    attn_sum = scatter(attn_partial)
    while grad_ring.steps_left():
        steps(grad_ring)
    share_parts = order.take(*share_parts)
    order.mark(*share_parts)
    grad_full = order.take(grad_ring.rows())
    act_grad = jnp.einsum("td,fd->tf", grad_full, down_weight, preferred_element_type=jnp.float32)
    normal_share = ring_rows(share_parts)
    order.mark(act_grad, normal_share)
    hidden_res = inputs + order.take(attn_sum).astype(jnp.float32)
    normal_two = normalize(hidden_res, mlp_gain).astype(jnp.bfloat16)
    order.mark(normal_two)
    normal_full = order.take(gather(normal_two))
    gate = dotf(normal_full, gate_weight)
    upward = dotf(normal_full, up_weight)
    activated = gated(gate, upward).astype(jnp.bfloat16)
    _, gated_pull = jax.vjp(gated, gate, upward)
    gate_grad32, up_grad32 = gated_pull(act_grad)
    gate_low = gate_grad32.astype(jnp.bfloat16)
    up_low = up_grad32.astype(jnp.bfloat16)
    two_partial = (
        jnp.einsum("tf,df->td", gate_low, gate_weight, preferred_element_type=jnp.float32)
        + jnp.einsum("tf,df->td", up_low, up_weight, preferred_element_type=jnp.float32)
    ).astype(jnp.bfloat16)
    order.mark(two_partial)
    two_sum = scatter(two_partial)
    down_part = weight_grad(order.take(activated), grad_full)
    order.mark(down_part)
    down = sum_halves(order.take(down_part), 1)
    order.mark([lane.sent for lane in down])
    gate_part = weight_grad(order.take(normal_full), gate_low)
    order.mark(gate_part)
    gate_lane = Lane(order.take(gate_part), first, 0)
    order.mark(gate_lane.sent)
    steps(*down)
    up_part = weight_grad(order.take(normal_full), up_low)
    order.mark(up_part)
    up_lane = Lane(order.take(up_part), second, 0)
    order.mark(up_lane.sent)
    steps(gate_lane, up_lane)
    steps(*down)
    result_partial = dotf(order.take(activated), down_weight).astype(jnp.bfloat16)
    order.mark(result_partial)
    normal_two_grad = order.take(two_sum).astype(jnp.float32)
    _, norm_pull_two = jax.vjp(normalize, hidden_res, mlp_gain)
    resid_from_norm, mlp_gain_part = norm_pull_two(normal_two_grad)
    hidden_grad = out_grad.astype(jnp.float32) + resid_from_norm
    branch = hidden_grad.astype(jnp.bfloat16)
    order.mark(branch)
    branch_full = gather(branch)
    steps(gate_lane, up_lane)
    steps(*down)
    mlp_gain_sum = SmallSum(order.take(mlp_gain_part), "mp")
    steps(gate_lane, up_lane)
    steps(mlp_gain_sum)
    steps(*down)
    while mlp_gain_sum.bits:
        steps(mlp_gain_sum)
    branch_full = order.take(branch_full)
    attended_low = jnp.einsum(
        "td,kd->tk", branch_full, attn_out, preferred_element_type=jnp.float32
    ).astype(jnp.bfloat16)
    order.mark(attended_low)
    result_sum = scatter(order.take(result_partial))
    steps(gate_lane, up_lane)
    query_low, key_grads, value_grads = attention_backward(
        group, query_full, order.take(attended_low), sources, kept, logs, local_heads, head_dim
    )
    beside = [lane.flying for lane in down + [gate_lane, up_lane]]
    query_low, key_grads, value_grads = lax.optimization_barrier(
        (query_low, key_grads, value_grads, *beside)
    )[:3]
    order.mark(query_low)
    key_sum = BlockSum(order.take(key_grads), first)
    value_sum = BlockSum(order.take(value_grads), second)
    order.mark(key_sum.sent, value_sum.sent)
    latent_partial = jnp.einsum(
        "tk,rk->tr", order.take(query_low), query_up, preferred_element_type=jnp.float32
    ).astype(jnp.bfloat16)
    order.mark(latent_partial)
    latent_sum = RingScatter(latent_partial)
    up_query_part = weight_grad(latent_full, order.take(query_low))
    order.mark(up_query_part)
    steps(key_sum, value_sum)
    out_part = weight_grad(order.take(attended), branch_full)
    order.mark(out_part)
    steps(*down)
    steps(latent_sum)
    out_part, up_query_part, result_sum = order.take(out_part, up_query_part, result_sum)
    order.mark(out_part, up_query_part)
    out_sum, up_query_sum = lax.psum((out_part, up_query_part), "dp")
    finish(*down)
    down_sum = lay_out(down, (activated.shape[1], grad_full.shape[1]), "down_grad")
    order.mark(down_sum)
    steps(key_sum, value_sum)
    steps(latent_sum)
    steps(gate_lane, up_lane)
    while len(key_sum.bits) > 1:
        steps(key_sum, value_sum)
    while latent_sum.steps_left():
        steps(latent_sum)
    latent_low = latent_sum.held
    low_ring = RingGather(latent_low)
    finish(gate_lane, up_lane)
    while key_sum.bits:
        steps(key_sum, value_sum)
    pair_partial = jnp.concatenate([key_sum.held, value_sum.held], axis=1)
    order.mark(pair_partial)
    pair_low_sum = RingScatter(pair_partial)
    gate_sum = lay_out([gate_lane], gate_weight.shape, "gate_grad")
    order.mark(gate_sum)
    steps(pair_low_sum, low_ring)
    up_sum = lay_out([up_lane], up_weight.shape, "up_grad")
    order.mark(up_sum)
    while pair_low_sum.steps_left():
        steps(pair_low_sum, low_ring)
    pair_low = pair_low_sum.held
    low_pair_ring = RingGather(pair_low)
    normal_one_grad = jnp.einsum(
        "tr,dr->td", latent_low, query_down, preferred_element_type=jnp.float32
    ) + jnp.einsum("tp,dp->td", order.take(pair_low), key_value, preferred_element_type=jnp.float32)
    _, norm_pull_one = jax.vjp(normalize, inputs, attn_gain)
    input_from_norm, attn_gain_part = norm_pull_one(normal_one_grad)
    input_grad = hidden_grad + input_from_norm
    order.mark(input_grad, attn_gain_part)
    attn_gain_sum = SmallSum(order.take(attn_gain_part), "mp")
    while low_ring.steps_left():
        steps(low_ring)
    steps(low_pair_ring)
    down_query_part = weight_grad(normal_share, order.take(low_ring.rows()))
    order.mark(down_query_part)
    down_query = Lane(order.take(down_query_part), first, 0)
    order.mark(down_query.sent)
    steps(attn_gain_sum)
    steps(low_pair_ring)
    while low_pair_ring.steps_left() > 1:
        steps(low_pair_ring, attn_gain_sum)
    while attn_gain_sum.bits:
        steps(attn_gain_sum)
    gains = jnp.stack([own_share(attn_gain_sum.held), own_share(mlp_gain_sum.held)])
    order.mark(gains)
    gains = SmallSum(gains, "dp")
    steps(low_pair_ring)
    pair_weight_part = weight_grad(normal_share, order.take(low_pair_ring.rows()))
    order.mark(pair_weight_part)
    pair_weight = Lane(order.take(pair_weight_part), second, 0)
    order.mark(pair_weight.sent)
    result = (hidden_res + order.take(result_sum).astype(jnp.float32)).astype(jnp.bfloat16)
    order.mark(result)
    while down_query.steps or gains.bits:
        if down_query.steps:
            steps(down_query, pair_weight)
        steps(gains)
    down_query_sum = lay_out(
        [down_query], (normal_share.shape[1], query_down.shape[1]), "query_down_grad"
    )
    pair_weight_sum = lay_out(
        [pair_weight], (normal_share.shape[1], key_value.shape[1]), "key_value_grad"
    )
    out_sum, up_query_sum = out_sum.astype(jnp.float32), up_query_sum.astype(jnp.float32)
    attn_gain_sum, mlp_gain_sum = gains.held[0], gains.held[1]
    return (
        result,
        input_grad,
        attn_gain_sum,
        down_query_sum,
        up_query_sum,
        pair_weight_sum,
        out_sum,
        mlp_gain_sum,
        gate_sum,
        up_sum,
        down_sum,
    )


def solution(mesh):
    return jax.shard_map(
        shards,
        mesh=mesh,
        in_specs=(
            P(("dp", "mp"), None),
            P(),
            P(),
            P(None, "mp"),
            P(),
            P("mp", None),
            P(),
            P(None, "mp"),
            P(None, "mp"),
            P("mp", None),
            P(("dp", "mp"), None),
        ),
        out_specs=(
            P(("dp", "mp"), None),
            P(("dp", "mp"), None),
            P("mp"),
            P("mp", None),
            P(None, "mp"),
            P("mp", None),
            P("mp", None),
            P("mp"),
            P(None, "mp"),
            P(None, "mp"),
            P("mp", None),
        ),
        check_vma=False,
    )
```

time: 924 us -> 693 us (0.75)
  waiting for transfers between devices: 465 us -> 312 us
  Pallas kernels: 90.7 us -> 49 us
  local copies, waits for them, and re-layouts: 40.7 us -> 58.4 us
  blocking collectives: 17.5 us -> 0 us
  other arithmetic: 73.6 us -> 57.1 us
  matrix products: 109 us -> 96.7 us
  starting transfers between devices: 101 us -> 88.8 us
    ppermute x78 -> x50, waiting for transfers between devices: 197 us -> 104 us  [trade(): return lax.ppermute(array, 'dp', [(i, i ^ 1 << bit) for i in range(count)])]
    ppermute x10 -> x31, waiting for transfers between devices: 11.5 us -> 85.9 us  [the longest x21 76.2 us: ring_pass(): return lax.ppermute(array, 'mp', pairs)]
    all_gather x5 -> x2, waiting for transfers between devices: 139 us -> 65.1 us  [gather(): return lax.all_gather(rows, 'mp', axis=0, tiled=True)]
    all_gather x1 -> x0, waiting for transfers between devices: 65 us -> none  [shards(): pair_all = lax.all_gather(pair_local, ('dp', 'mp'), axis=0, tiled=True)]
    pallas_call x7 -> x5, Pallas kernels: 71.9 us -> 28.3 us  [lay_out(): pl.pallas_call(functools.partial(lay_kernel, len(sets), pieces, axis, len...]
    ppermute x78 -> x50, starting transfers between devices: 86.6 us -> 44.4 us  [trade(): return lax.ppermute(array, 'dp', [(i, i ^ 1 << bit) for i in range(count)])]
    ppermute x10 -> x31, starting transfers between devices: 6.07 us -> 43.8 us  [the longest x21 29.1 us: ring_pass(): return lax.ppermute(array, 'mp', pairs)]
    concatenate x26 -> x3, other arithmetic: 28.7 us -> 0.14 us  [the longest x1 0.08 us: lay_out(): places = jnp.concatenate([lane.places() for lane in lanes])]
  transfers between devices with their start and end apart: 100 -> 87, of which waited for: 47 -> 36; matrix products, arithmetic and copies ran while one was open for 17% -> 22% of each run, Pallas kernels for 9% -> 7%
where the time goes in v2:
time: 693 us; the launch traced here: 682 us
  waiting for transfers between devices  312 us (45%)
  matrix products  96.7 us (14%)
  starting transfers between devices  88.8 us (13%)
  local copies, waits for them, and re-layouts  58.4 us (8%)
  other arithmetic  57.1 us (8%)
  Pallas kernels  49 us (7%)
  between operations  19.9 us (3%)
    ppermute x50, waiting for transfers between devices, trade(): return lax.ppermute(array, 'dp', [(i, i ^ 1 << bit) for i in range(count)])  104 us
    ppermute x21, waiting for transfers between devices, ring_pass(): return lax.ppermute(array, 'mp', pairs)  76.2 us
    all_gather x2, waiting for transfers between devices, gather(): return lax.all_gather(rows, 'mp', axis=0, tiled=True)  65.1 us
    ppermute x50, starting transfers between devices, trade(): return lax.ppermute(array, 'dp', [(i, i ^ 1 << bit) for i in range(count)])  44.4 us
    reduce_scatter x3, waiting for transfers between devices, scatter(): return lax.psum_scatter(rows, 'mp', scatter_dimension=0, tiled=True)  37.8 us
    convert_element_type x28, other arithmetic, add_low(): (left.astype(jnp.float32) + right.astype(jnp.float32)).astype(jnp.bfloat16)  34.3 us
    dot_general x7, matrix products, dotf(): return jnp.dot(left, right, preferred_element_type=jnp.float32)  33.9 us
    dot_general x7, matrix products, weight_grad(): jnp.einsum('tk,td->kd', left, right, preferred_element_type=jnp.float32)  31.5 us
  transfers between devices with their start and end apart: 87, of which 36 were waited for; matrix products, arithmetic and copies ran while one was open for 22% of the time, Pallas kernels for 7%

profile of v2, /device:TPU:0, one launch (start us, length us, event | category | flops | bytes accessed | tf_op | source)
XLA Modules:
  0.0 681.7 jit_solution(547530466320361857)
XLA Ops:
  21.8 9.7 %collective-permute-done.1 = bf16[160,512]{1,0:T(8,128)(2,1)} collective-permute-done((bf16[160,512]{1,0:T(8,128)(2,1)S(1)}, bf16[160,512]{1,0:T(8,128)(2,1)}, u32[]{:S(2)}, u32[]{:S(2)}) %collective-permute-start.1) | collective-permute-done | bytes 163872 | tf_op jit(solution)/shard_map/ppermute | solution.py:328
  64.4 11.4 %collective-permute-done.8 = bf16[160,2048]{1,0:T(8,128)(2,1)} collective-permute-done((bf16[160,2048]{1,0:T(8,128)(2,1)S(1)}, bf16[160,2048]{1,0:T(8,128)(2,1)}, u32[]{:S(2)}, u32[]{:S(2)}) %collective-permute-start.8) | collective-permute-done | bytes 655392 | tf_op jit(solution)/shard_map/ppermute | solution.py:328
  79.1 11.6 %collective-permute-done.12 = bf16[160,2048]{1,0:T(8,128)(2,1)} collective-permute-done((bf16[160,2048]{1,0:T(8,128)(2,1)}, bf16[160,2048]{1,0:T(8,128)(2,1)}, u32[]{:S(2)}, u32[]{:S(2)}) %collective-permute-start.12) | collective-permute-done | bytes 655392 | tf_op jit(solution)/shard_map/ppermute | solution.py:328
  93.0 8.4 %attention_forward.1 = (bf16[640,1024]{1,0:T(8,128)(2,1)}, f32[256,2560]{1,0:T(8,128)}, f32[1,2560]{1,0:T(1,128)S(1)}) custom-call(s32[1]{0:T(128)} %bitcast.group, bf16[640,1024]{1,0:T(8,128)(2,1)} %convolution_convert_fusion.9.query, bf16[1280,256]{1,0:T(8,128)(2,1)S(1)} %constant_dynamic-update-slice_fusion.refs_0_, ...), custom_call_target="tpu_custom_call" | custom-call | flops 13421772800 | bytes 10485760 | tf_op jit(solution)/shard_map/attention_forward/pallas_call | solution.py:230
  104.1 5.4 convolution_convert_fusion.5
  128.7 9.1 %fusion.29 = f32[640,1408]{1,0:T(8,128)} fusion(bf16[640,2048]{1,0:T(8,128)(2,1)S(1)} %constant_dynamic-update-slice_fusion.37, bf16[1408,2048]{1,0:T(8,128)(2,1)} %param.56), kind=kOutput, calls=%fused_computation.190 | convolution fusion | flops 3690987520 | bytes 11993088 | tf_op jit(solution)/shard_map/td,fd->tf/dot_general | solution.py:690
  137.8 37.8 %reduce-scatter.4.cloned.1.call-done = bf16[160,2048]{1,0:T(8,128)(2,1)} async-done(((bf16[640,2048]{1,0:T(8,128)(2,1)}), bf16[160,2048]{1,0:T(8,128)(2,1)}) %reduce-scatter.4.cloned.1.call-update) | async-done | bytes 655376 | tf_op jit(solution)/shard_map/reduce_scatter | solution.py:636
  178.3 65.1 %all-gather.3.cloned.1.call-done = bf16[640,2048]{1,0:T(8,128)(2,1)} async-done(((bf16[160,2048]{1,0:T(8,128)(2,1)}), bf16[640,2048]{1,0:T(8,128)(2,1)}) %all-gather.3.cloned.1.call-update) | async-done | bytes 2621456 | tf_op jit(solution)/shard_map/all_gather | solution.py:633
  243.4 7.6 %fusion.30 = f32[640,1408]{1,0:T(8,128)S(1)} fusion(bf16[640,2048]{1,0:T(8,128)(2,1)} %all-gather.3.cloned.1.call-done, bf16[2048,1408]{1,0:T(8,128)(2,1)} %param.54), kind=kOutput, calls=%fused_computation.191 | convolution fusion | flops 3690987520 | bytes 11993088 | tf_op jit(solution)/shard_map/dot_general | solution.py:19
  251.0 9.4 %multiply_convert_fusion = (bf16[640,1408]{1,0:T(8,128)(2,1)}, bf16[640,1408]{1,0:T(8,128)(2,1)S(1)}, bf16[640,1408]{1,0:T(8,128)(2,1)S(1)}) fusion(f32[640,1408]{1,0:T(8,128)S(1)} %fusion.30, f32[640,1408]{1,0:T(8,128)S(1)} %copy-done.75, bf16[640,2048]{1,0:T(8,128)(2,1)S(1)} %copy-done.68, bf16[2048,1408]{1,0:T(8,128)(2,1)} %param.55), kind=kOutput, calls=%fused_computation.9 | convolution fusion | flops 3705405440 | bytes 21004288 | tf_op jit(solution)/shard_map/dot_general | solution.py:19
  264.7 5.6 add_convert_fusion
  270.3 7.0 %convolution_convert_fusion.2 = bf16[1408,2048]{1,0:T(8,128)(2,1)S(1)} fusion(bf16[640,1408]{1,0:T(8,128)(2,1)} %get-tuple-element.256, bf16[640,2048]{1,0:T(8,128)(2,1)} %copy-done.33), kind=kOutput, calls=%fused_computation.2 | convolution fusion | flops 3693871104 | bytes 10190848 | tf_op jit(solution)/shard_map/tk,td->kd/dot_general | solution.py:639
  282.7 7.3 %convolution_convert_fusion.1 = bf16[2048,1408]{1,0:T(8,128)(2,1)S(1)} fusion(bf16[640,2048]{1,0:T(8,128)(2,1)} %all-gather.3.cloned.1.call-done, bf16[640,1408]{1,0:T(8,128)(2,1)} %copy-done.76), kind=kOutput, calls=%fused_computation.1 | convolution fusion | flops 3693871104 | bytes 10190848 | tf_op jit(solution)/shard_map/tk,td->kd/dot_general | solution.py:639
  321.0 6.4 collective-permute-done.23
  331.3 5.7 convolution_convert_fusion.4
  344.7 13.6 %collective-permute-done.29 = bf16[512,1408]{1,0:T(8,128)(2,1)} collective-permute-done((bf16[512,1408]{1,0:T(8,128)(2,1)}, bf16[512,1408]{1,0:T(8,128)(2,1)}, u32[]{:S(2)}, u32[]{:S(2)}) %collective-permute-start.29) | collective-permute-done | bytes 1441824 | tf_op jit(solution)/shard_map/ppermute | solution.py:391
  362.0 14.0 %collective-permute-done.28 = bf16[512,1408]{1,0:T(8,128)(2,1)S(1)} collective-permute-done((bf16[512,1408]{1,0:T(8,128)(2,1)}, bf16[512,1408]{1,0:T(8,128)(2,1)S(1)}, u32[]{:S(2)}, u32[]{:S(2)}) %collective-permute-start.28) | collective-permute-done | bytes 1441824 | tf_op jit(solution)/shard_map/ppermute | solution.py:391
  377.8 5.8 collective-permute-done.27
  386.9 12.2 %collective-permute-done.32 = bf16[256,1408]{1,0:T(8,128)(2,1)S(1)} collective-permute-done((bf16[256,1408]{1,0:T(8,128)(2,1)S(1)}, bf16[256,1408]{1,0:T(8,128)(2,1)S(1)}, u32[]{:S(2)}, u32[]{:S(2)}) %collective-permute-start.32) | collective-permute-done | bytes 720928 | tf_op jit(solution)/shard_map/ppermute | solution.py:391
  413.6 7.0 %convolution_convert_fusion.7.grad = bf16[640,1024]{1,0:T(8,128)(2,1)} fusion(bf16[640,2048]{1,0:T(8,128)(2,1)} %all-gather.5.cloned.1.call-done, bf16[1024,2048]{1,0:T(8,128)(2,1)} %param.52), kind=kOutput, calls=%fused_computation.30 | convolution fusion | flops 2685009920 | bytes 8126464 | tf_op jit(solution)/shard_map/td,kd->tk/dot_general | solution.py:743
  431.3 12.3 %attention_backward.1 = (bf16[640,1024]{1,0:T(8,128)(2,1)}, bf16[5120,256]{1,0:T(8,128)(2,1)}, bf16[5120,256]{1,0:T(8,128)(2,1)}) custom-call(s32[1]{0:T(128)} %bitcast.group, bf16[640,1024]{1,0:T(8,128)(2,1)} %convolution_convert_fusion.9.query, bf16[640,1024]{1,0:T(8,128)(2,1)} %convolution_convert_fusion.7.grad, f32[256,2560]{1,0:T(8,128)} %get-tuple-element.285.kept, ...), custom_call_target="tpu_custom_call" | custom-call | flops 33554432000 | bytes 17039360 | tf_op jit(solution)/shard_map/attention_backward/pallas_call | solution.py:260
  443.6 22.3 %collective-permute-done.41 = bf16[512,1408]{1,0:T(8,128)(2,1)} collective-permute-done((bf16[512,1408]{1,0:T(8,128)(2,1)}, bf16[512,1408]{1,0:T(8,128)(2,1)}, u32[]{:S(2)}, u32[]{:S(2)}) %collective-permute-start.41) | collective-permute-done | bytes 1441824 | tf_op jit(solution)/shard_map/ppermute | solution.py:391
  496.0 8.1 %collective-permute-done.44 = bf16[160,1024]{1,0:T(8,128)(2,1)S(1)} collective-permute-done((bf16[160,1024]{1,0:T(8,128)(2,1)S(1)}, bf16[160,1024]{1,0:T(8,128)(2,1)S(1)}, u32[]{:S(2)}, u32[]{:S(2)}) %collective-permute-start.44) | collective-permute-done | bytes 327712 | tf_op jit(solution)/shard_map/ppermute | solution.py:328
  506.2 7.2 %down_grad.1 = f32[1408,2048]{1,0:T(8,128)} custom-call(s32[16]{0:T(128)S(1)} %pad_add_fusion.places, bf16[704,1024]{1,0:T(8,128)(2,1)S(1)} %constant_dynamic-update-slice_fusion.12.refs_0_, bf16[704,1024]{1,0:T(8,128)(2,1)} %collective-permute-done.46.refs_1_, bf16[704,1024]{1,0:T(8,128)(2,1)} %constant_dynamic-update-slice_fusion.14.refs_2_, ...), custom_call_target="tpu_custom_call" | custom-call | bytes 17301504 | tf_op jit(solution)/shard_map/down_grad/pallas_call | solution.py:499
  526.5 7.1 %collective-permute-done.53 = bf16[160,1024]{1,0:T(8,128)(2,1)S(1)} collective-permute-done((bf16[160,1024]{1,0:T(8,128)(2,1)S(1)}, bf16[160,1024]{1,0:T(8,128)(2,1)S(1)}, u32[]{:S(2)}, u32[]{:S(2)}) %collective-permute-start.53) | collective-permute-done | bytes 327712 | tf_op jit(solution)/shard_map/ppermute | solution.py:328
  538.5 7.3 %gate_grad.1 = f32[2048,1408]{1,0:T(8,128)} custom-call(s32[8]{0:T(128)S(1)} %pad_add_fusion.1.places, bf16[1024,1408]{1,0:T(8,128)(2,1)S(1)} %constant_dynamic-update-slice_fusion.16.refs_0_, bf16[1024,1408]{1,0:T(8,128)(2,1)S(1)} %collective-permute-done.52.refs_1_), custom_call_target="tpu_custom_call" | custom-call | bytes 17301504 | tf_op jit(solution)/shard_map/gate_grad/pallas_call | solution.py:499
  551.5 7.3 %up_grad.1 = f32[2048,1408]{1,0:T(8,128)} custom-call(s32[8]{0:T(128)S(1)} %pad_add_fusion.2.places, bf16[1024,1408]{1,0:T(8,128)(2,1)S(1)} %copy-done.2, bf16[1024,1408]{1,0:T(8,128)(2,1)S(1)} %copy-done.4), custom_call_target="tpu_custom_call" | custom-call | bytes 17301504 | tf_op jit(solution)/shard_map/up_grad/pallas_call | solution.py:499
  563.5 6.8 collective-permute-done.59
  604.7 11.2 %collective-permute-done.71 = bf16[128,1024]{1,0:T(8,128)(2,1)S(1)} collective-permute-done((bf16[128,1024]{1,0:T(8,128)(2,1)}, bf16[128,1024]{1,0:T(8,128)(2,1)S(1)}, u32[]{:S(2)}, u32[]{:S(2)}) %collective-permute-start.71) | collective-permute-done | bytes 262176 | tf_op jit(solution)/shard_map/ppermute | solution.py:391
  629.4 9.6 %collective-permute-done.76 = bf16[128,1024]{1,0:T(8,128)(2,1)S(1)} collective-permute-done((bf16[128,1024]{1,0:T(8,128)(2,1)S(1)}, bf16[128,1024]{1,0:T(8,128)(2,1)S(1)}, u32[]{:S(2)}, u32[]{:S(2)}) %collective-permute-start.76) | collective-permute-done | bytes 262176 | tf_op jit(solution)/shard_map/ppermute | solution.py:391
  639.7 18.7 %all-reduce.3.cloned.1.call-done = (bf16[1024,1024]{1,0:T(8,128)(2,1)}, bf16[1024,2048]{1,0:T(8,128)(2,1)}) async-done(((bf16[1024,1024]{1,0:T(8,128)(2,1)}, bf16[1024,2048]{1,0:T(8,128)(2,1)}), (bf16[1024,1024]{1,0:T(8,128)(2,1)}, bf16[1024,2048]{1,0:T(8,128)(2,1)})) %all-reduce.3.cloned.1.call-update) | async-done | bytes 6291472 | tf_op jit(solution)/shard_map/psum | solution.py:774
  658.3 6.8 convert_element_type.667
  (480 shorter events, 276.9 us)
Async XLA Ops:
  7.2 168.4 %reduce-scatter.4.cloned.1.call-start = ((), (), s32[]{:S(2)}) async-start(), calls=%async_computation.3 | async-start | bytes 3276800 | tf_op jit(solution)/shard_map/reduce_scatter | solution.py:636
  16.1 19.9 %collective-permute-start = (bf16[160,1024]{1,0:T(8,128)(2,1)S(1)}, bf16[160,1024]{1,0:T(8,128)(2,1)S(1)}, u32[]{:S(2)}, u32[]{:S(2)}) collective-permute-start(bf16[160,1024]{1,0:T(8,128)(2,1)S(1)} %get-tuple-element.459), channel_id=1, source_target_pairs={{0,1},{1,3},{3,2},{2,0},{4,5},{5,7},{7,6},{6,4},{8,9},{9,11},{11,1... | collective-permute-start | bytes 983048 | tf_op jit(solution)/shard_map/ppermute | solution.py:328
  58.6 19.5 %collective-permute-start.7 = (bf16[1280,256]{1,0:T(8,128)(2,1)S(1)}, bf16[1280,256]{1,0:T(8,128)(2,1)}, u32[]{:S(2)}, u32[]{:S(2)}) collective-permute-start(bf16[1280,256]{1,0:T(8,128)(2,1)S(1)} %constant_dynamic-update-slice_fusion.refs_0_), channel_id=1, source_target_pairs={{0,16},{4,20},{8,24},{12,28},{16,0},{20,4},{24,8},{28,12},{1,17},{... | collective-permute-start | bytes 1966088 | tf_op jit(solution)/shard_map/ppermute | solution.py:391
  109.6 133.8 %all-gather.3.cloned.1.call-start = ((), (), s32[]{:S(2)}) async-start(), calls=%async_computation.4 | async-start | bytes 3276800 | tf_op jit(solution)/shard_map/all_gather | solution.py:633
  178.2 158.9 %reduce-scatter.6.cloned.1.call-start = ((), (), s32[]{:S(2)}) async-start(), calls=%async_computation.5 | async-start | bytes 3276800 | tf_op jit(solution)/shard_map/reduce_scatter | solution.py:636
  282.6 131.0 %all-gather.5.cloned.1.call-start = ((), (), s32[]{:S(2)}) async-start(), calls=%async_computation.6 | async-start | bytes 3276800 | tf_op jit(solution)/shard_map/all_gather | solution.py:633
  293.0 18.1 %collective-permute-start.25 = (bf16[1024,1408]{1,0:T(8,128)(2,1)}, bf16[1024,1408]{1,0:T(8,128)(2,1)}, u32[]{:S(2)}, u32[]{:S(2)}) collective-permute-start(bf16[1024,1408]{1,0:T(8,128)(2,1)} %get-tuple-element.405), channel_id=1, source_target_pairs={{0,4},{4,0},{8,12},{12,8},{16,20},{20,16},{24,28},{28,24},{1,5},{5... | collective-permute-start | bytes 8650760 | tf_op jit(solution)/shard_map/ppermute | solution.py:391
  308.1 19.3 %collective-permute-start.23 = (bf16[704,512]{1,0:T(8,128)(2,1)}, bf16[704,512]{1,0:T(8,128)(2,1)}, u32[]{:S(2)}, u32[]{:S(2)}) collective-permute-start(bf16[704,512]{1,0:T(8,128)(2,1)} %get-tuple-element.417), channel_id=1, source_target_pairs={{0,8},{4,12},{8,0},{12,4},{16,24},{20,28},{24,16},{28,20},{1,9},{5... | collective-permute-start | bytes 2162696 | tf_op jit(solution)/shard_map/ppermute | solution.py:391
  309.6 20.0 %collective-permute-start.22 = (bf16[704,512]{1,0:T(8,128)(2,1)}, bf16[704,512]{1,0:T(8,128)(2,1)S(1)}, u32[]{:S(2)}, u32[]{:S(2)}) collective-permute-start(bf16[704,512]{1,0:T(8,128)(2,1)} %get-tuple-element.415), channel_id=1, source_target_pairs={{0,16},{4,20},{8,24},{12,28},{16,0},{20,4},{24,8},{28,12},{1,17},{... | collective-permute-start | bytes 2162696 | tf_op jit(solution)/shard_map/ppermute | solution.py:391
  316.2 42.1 %collective-permute-start.29 = (bf16[512,1408]{1,0:T(8,128)(2,1)}, bf16[512,1408]{1,0:T(8,128)(2,1)}, u32[]{:S(2)}, u32[]{:S(2)}) collective-permute-start(bf16[512,1408]{1,0:T(8,128)(2,1)} %get-tuple-element.403), channel_id=1, source_target_pairs={{0,8},{4,12},{8,0},{12,4},{16,24},{20,28},{24,16},{28,20},{1,9},{5... | collective-permute-start | bytes 4325384 | tf_op jit(solution)/shard_map/ppermute | solution.py:391
  341.1 165.0 %reduce-scatter.8.cloned.1.call-start = ((), (), s32[]{:S(2)}) async-start(), calls=%async_computation.7 | async-start | bytes 3276800 | tf_op jit(solution)/shard_map/reduce_scatter | solution.py:636
  341.1 34.8 %collective-permute-start.28 = (bf16[512,1408]{1,0:T(8,128)(2,1)}, bf16[512,1408]{1,0:T(8,128)(2,1)S(1)}, u32[]{:S(2)}, u32[]{:S(2)}) collective-permute-start(bf16[512,1408]{1,0:T(8,128)(2,1)} %get-tuple-element.401), channel_id=1, source_target_pairs={{0,16},{4,20},{8,24},{12,28},{16,0},{20,4},{24,8},{28,12},{1,17},{... | collective-permute-start | bytes 4325384 | tf_op jit(solution)/shard_map/ppermute | solution.py:391
  342.7 41.0 %collective-permute-start.27 = (bf16[704,256]{1,0:T(8,128)(2,1)}, bf16[704,256]{1,0:T(8,128)(2,1)S(1)}, u32[]{:S(2)}, u32[]{:S(2)}) collective-permute-start(bf16[704,256]{1,0:T(8,128)(2,1)} %get-tuple-element.433), channel_id=1, source_target_pairs={{0,16},{4,20},{8,24},{12,28},{16,0},{20,4},{24,8},{28,12},{1,17},{... | collective-permute-start | bytes 1081352 | tf_op jit(solution)/shard_map/ppermute | solution.py:391
  343.2 42.1 %collective-permute-start.26 = (bf16[704,256]{1,0:T(8,128)(2,1)}, bf16[704,256]{1,0:T(8,128)(2,1)S(1)}, u32[]{:S(2)}, u32[]{:S(2)}) collective-permute-start(bf16[704,256]{1,0:T(8,128)(2,1)} %get-tuple-element.431), channel_id=1, source_target_pairs={{0,8},{4,12},{8,0},{12,4},{16,24},{20,28},{24,16},{28,20},{1,9},{5... | collective-permute-start | bytes 1081352 | tf_op jit(solution)/shard_map/ppermute | solution.py:391
  360.4 38.7 %collective-permute-start.32 = (bf16[256,1408]{1,0:T(8,128)(2,1)S(1)}, bf16[256,1408]{1,0:T(8,128)(2,1)S(1)}, u32[]{:S(2)}, u32[]{:S(2)}) collective-permute-start(bf16[256,1408]{1,0:T(8,128)(2,1)S(1)} %get-tuple-element.413), channel_id=1, source_target_pairs={{0,16},{4,20},{8,24},{12,28},{16,0},{20,4},{24,8},{28,12},{1,17},{... | collective-permute-start | bytes 2162696 | tf_op jit(solution)/shard_map/ppermute | solution.py:391
  376.3 24.5 %collective-permute-start.31 = (bf16[256,1408]{1,0:T(8,128)(2,1)S(1)}, bf16[256,1408]{1,0:T(8,128)(2,1)S(1)}, u32[]{:S(2)}, u32[]{:S(2)}) collective-permute-start(bf16[256,1408]{1,0:T(8,128)(2,1)S(1)} %get-tuple-element.411), channel_id=1, source_target_pairs={{0,8},{4,12},{8,0},{12,4},{16,24},{20,28},{24,16},{28,20},{1,9},{5... | collective-permute-start | bytes 2162696 | tf_op jit(solution)/shard_map/ppermute | solution.py:391
  383.8 23.1 %collective-permute-start.35 = (bf16[704,256]{1,0:T(8,128)(2,1)S(1)}, bf16[704,256]{1,0:T(8,128)(2,1)S(1)}, u32[]{:S(2)}, u32[]{:S(2)}) collective-permute-start(bf16[704,256]{1,0:T(8,128)(2,1)S(1)} %add_convert_fusion.21), channel_id=1, source_target_pairs={{0,16},{4,20},{8,24},{12,28},{16,0},{20,4},{24,8},{28,12},{1,17},{... | collective-permute-start | bytes 1081352 | tf_op jit(solution)/shard_map/ppermute | solution.py:391
  385.4 24.6 %collective-permute-start.34 = (bf16[704,256]{1,0:T(8,128)(2,1)S(1)}, bf16[704,256]{1,0:T(8,128)(2,1)S(1)}, u32[]{:S(2)}, u32[]{:S(2)}) collective-permute-start(bf16[704,256]{1,0:T(8,128)(2,1)S(1)} %add_convert_fusion.20), channel_id=1, source_target_pairs={{0,8},{4,12},{8,0},{12,4},{16,24},{20,28},{24,16},{28,20},{1,9},{5... | collective-permute-start | bytes 1081352 | tf_op jit(solution)/shard_map/ppermute | solution.py:391
  386.9 16.4 %collective-permute-start.30 = (f32[2048]{0:T(1024)S(1)}, f32[2048]{0:T(1024)S(1)}, u32[]{:S(2)}, u32[]{:S(2)}) collective-permute-start(f32[2048]{0:T(1024)S(1)} %copy-done.51), channel_id=1, source_target_pairs={{0,1},{1,0},{2,3},{3,2},{4,5},{5,4},{6,7},{7,6},{8,9},{9,8},{10,11... | collective-permute-start | bytes 24584 | tf_op jit(solution)/shard_map/ppermute | solution.py:590
  399.3 23.1 %collective-permute-start.37 = (bf16[256,1408]{1,0:T(8,128)(2,1)S(1)}, bf16[256,1408]{1,0:T(8,128)(2,1)}, u32[]{:S(2)}, u32[]{:S(2)}) collective-permute-start(bf16[256,1408]{1,0:T(8,128)(2,1)S(1)} %add_convert_fusion.6), channel_id=1, source_target_pairs={{0,16},{4,20},{8,24},{12,28},{16,0},{20,4},{24,8},{28,12},{1,17},{... | collective-permute-start | bytes 2162696 | tf_op jit(solution)/shard_map/ppermute | solution.py:391
  401.9 21.8 %collective-permute-start.36 = (bf16[256,1408]{1,0:T(8,128)(2,1)}, bf16[256,1408]{1,0:T(8,128)(2,1)}, u32[]{:S(2)}, u32[]{:S(2)}) collective-permute-start(bf16[256,1408]{1,0:T(8,128)(2,1)} %add_convert_fusion.5), channel_id=1, source_target_pairs={{0,8},{4,12},{8,0},{12,4},{16,24},{20,28},{24,16},{28,20},{1,9},{5... | collective-permute-start | bytes 2162696 | tf_op jit(solution)/shard_map/ppermute | solution.py:391
  408.5 35.1 %collective-permute-start.38 = (bf16[704,512]{1,0:T(8,128)(2,1)}, bf16[704,512]{1,0:T(8,128)(2,1)}, u32[]{:S(2)}, u32[]{:S(2)}) collective-permute-start(bf16[704,512]{1,0:T(8,128)(2,1)} %constant_dynamic-update-slice_fusion.4), channel_id=1, source_target_pairs={{0,8},{4,12},{8,0},{12,4},{16,24},{20,28},{24,16},{28,20},{1,9},{5... | collective-permute-start | bytes 2162696 | tf_op jit(solution)/shard_map/ppermute | solution.py:391
  411.5 32.1 %collective-permute-start.39 = (bf16[704,512]{1,0:T(8,128)(2,1)}, bf16[704,512]{1,0:T(8,128)(2,1)}, u32[]{:S(2)}, u32[]{:S(2)}) collective-permute-start(bf16[704,512]{1,0:T(8,128)(2,1)} %constant_dynamic-update-slice_fusion.6), channel_id=1, source_target_pairs={{0,16},{4,20},{8,24},{12,28},{16,0},{20,4},{24,8},{28,12},{1,17},{... | collective-permute-start | bytes 2162696 | tf_op jit(solution)/shard_map/ppermute | solution.py:391
  428.3 37.6 %collective-permute-start.41 = (bf16[512,1408]{1,0:T(8,128)(2,1)}, bf16[512,1408]{1,0:T(8,128)(2,1)}, u32[]{:S(2)}, u32[]{:S(2)}) collective-permute-start(bf16[512,1408]{1,0:T(8,128)(2,1)} %constant_dynamic-update-slice_fusion.10), channel_id=1, source_target_pairs={{0,16},{4,20},{8,24},{12,28},{16,0},{20,4},{24,8},{28,12},{1,17},{... | collective-permute-start | bytes 4325384 | tf_op jit(solution)/shard_map/ppermute | solution.py:391
  429.8 36.1 %collective-permute-start.40 = (bf16[512,1408]{1,0:T(8,128)(2,1)S(1)}, bf16[512,1408]{1,0:T(8,128)(2,1)}, u32[]{:S(2)}, u32[]{:S(2)}) collective-permute-start(bf16[512,1408]{1,0:T(8,128)(2,1)S(1)} %constant_dynamic-update-slice_fusion.8), channel_id=1, source_target_pairs={{0,8},{4,12},{8,0},{12,4},{16,24},{20,28},{24,16},{28,20},{1,9},{5... | collective-permute-start | bytes 4325384 | tf_op jit(solution)/shard_map/ppermute | solution.py:391
  431.3 227.1 %all-reduce.3.cloned.1.call-start = ((), (), s32[]{:S(2)}) async-start(), calls=%async_computation.8 | async-start | bytes 12582912 | tf_op jit(solution)/shard_map/psum | solution.py:774
  486.7 19.5 %collective-permute-start.46 = (bf16[704,1024]{1,0:T(8,128)(2,1)S(1)}, bf16[704,1024]{1,0:T(8,128)(2,1)}, u32[]{:S(2)}, u32[]{:S(2)}) collective-permute-start(bf16[704,1024]{1,0:T(8,128)(2,1)S(1)} %constant_dynamic-update-slice_fusion.12.refs_0_), channel_id=1, source_target_pairs={{0,4},{4,0},{8,12},{12,8},{16,20},{20,16},{24,28},{28,24},{1,5},{5... | collective-permute-start | bytes 4325384 | tf_op jit(solution)/shard_map/ppermute | solution.py:391
  491.3 22.1 %collective-permute-start.45 = (bf16[1280,256]{1,0:T(8,128)(2,1)}, bf16[1280,256]{1,0:T(8,128)(2,1)}, u32[]{:S(2)}, u32[]{:S(2)}) collective-permute-start(bf16[1280,256]{1,0:T(8,128)(2,1)} %get-tuple-element.425), channel_id=1, source_target_pairs={{0,8},{4,12},{8,0},{12,4},{16,24},{20,28},{24,16},{28,20},{1,9},{5... | collective-permute-start | bytes 1966088 | tf_op jit(solution)/shard_map/ppermute | solution.py:391
  493.8 20.9 %collective-permute-start.50 = (bf16[1280,256]{1,0:T(8,128)(2,1)}, bf16[1280,256]{1,0:T(8,128)(2,1)}, u32[]{:S(2)}, u32[]{:S(2)}) collective-permute-start(bf16[1280,256]{1,0:T(8,128)(2,1)} %get-tuple-element.423), channel_id=1, source_target_pairs={{0,16},{4,20},{8,24},{12,28},{16,0},{20,4},{24,8},{28,12},{1,17},{... | collective-permute-start | bytes 1966088 | tf_op jit(solution)/shard_map/ppermute | solution.py:391
  535.8 23.0 %collective-permute-start.58 = (bf16[160,1024]{1,0:T(8,128)(2,1)S(1)}, bf16[160,1024]{1,0:T(8,128)(2,1)S(1)}, u32[]{:S(2)}, u32[]{:S(2)}) collective-permute-start(bf16[160,1024]{1,0:T(8,128)(2,1)S(1)} %get-tuple-element.394), channel_id=1, source_target_pairs={{0,1},{1,3},{3,2},{2,0},{4,5},{5,7},{7,6},{6,4},{8,9},{9,11},{11,1... | collective-permute-start | bytes 983048 | tf_op jit(solution)/shard_map/ppermute | solution.py:328
  639.0 29.2 %collective-permute-start.78 = (bf16[256,1024]{1,0:T(8,128)(2,1)S(1)}, bf16[256,1024]{1,0:T(8,128)(2,1)S(1)}, u32[]{:S(2)}, u32[]{:S(2)}) collective-permute-start(bf16[256,1024]{1,0:T(8,128)(2,1)S(1)} %constant_dynamic-update-slice_fusion.24.refs_0_), channel_id=1, source_target_pairs={{0,4},{4,0},{8,12},{12,8},{16,20},{20,16},{24,28},{28,24},{1,5},{5... | collective-permute-start | bytes 1572872 | tf_op jit(solution)/shard_map/ppermute | solution.py:391
  639.1 32.7 %collective-permute-start.80 = (bf16[256,512]{1,0:T(8,128)(2,1)S(1)}, bf16[256,512]{1,0:T(8,128)(2,1)}, u32[]{:S(2)}, u32[]{:S(2)}) collective-permute-start(bf16[256,512]{1,0:T(8,128)(2,1)S(1)} %constant_dynamic-update-slice_fusion.26.refs_0_), channel_id=1, source_target_pairs={{0,4},{4,0},{8,12},{12,8},{16,20},{20,16},{24,28},{28,24},{1,5},{5... | collective-permute-start | bytes 786440 | tf_op jit(solution)/shard_map/ppermute | solution.py:391
  (141 other events, 1324.4 us)
Sparse Core Ops, SparseCore 0:
  109.7 65.8 reduce-scatter.3
  178.3 64.9 all-gather.2
  282.8 50.8 reduce-scatter.5
  341.2 53.5 all-gather.4
  431.4 48.9 reduce-scatter.7
  548.0 110.3 all-reduce.2

commit v3 on v2

--- a/solution.py
+++ b/solution.py
@@ -13,6 +13,7 @@
 LONG_PART = 512
 BLOCK = SHORT_PART + LONG_PART
 LOG2E = 1.4426950408889634
+FREE = pl.CostEstimate(flops=0, bytes_accessed=0, transcendentals=0)
 
 
 def dotf(left, right):
@@ -245,11 +246,7 @@
         ]
         + scratch,
         compiler_params=pltpu.CompilerParams(vmem_limit_bytes=50 << 20),
-        cost_estimate=pl.CostEstimate(
-            flops=2 * columns * rows * head_dim * 2,
-            bytes_accessed=4 * rows * head_dim + 8 * query.size,
-            transcendentals=columns * rows // 2,
-        ),
+        cost_estimate=pl.CostEstimate(flops=2 * columns * rows * head_dim * 2, bytes_accessed=4 * rows * head_dim, transcendentals=0),
         name="attention_forward",
     )(group, query, *sources)
 
@@ -278,11 +275,7 @@
         ]
         + scratch,
         compiler_params=pltpu.CompilerParams(vmem_limit_bytes=56 << 20),
-        cost_estimate=pl.CostEstimate(
-            flops=2 * columns * rows * head_dim * 5,
-            bytes_accessed=8 * rows * head_dim + 10 * query.size,
-            transcendentals=columns * rows // 2,
-        ),
+        cost_estimate=pl.CostEstimate(flops=2 * columns * rows * head_dim * 2, bytes_accessed=4 * rows * head_dim, transcendentals=0),
         name="attention_backward",
     )(group, query, grad, kept, logs, *sources)
 
@@ -293,6 +286,10 @@
 
 def gated(gate_in, up_in):
     return jax.nn.silu(gate_in) * up_in
+
+
+def after(value, *others):
+    return lax.optimization_barrier((value,) + others)[0]
 
 
 class Order:
@@ -309,6 +306,117 @@
 
 def add_low(left, right):
     return (left.astype(jnp.float32) + right.astype(jnp.float32)).astype(jnp.bfloat16)
+
+
+def plus_kernel(held, got, *outs):
+    value = held[...].astype(jnp.float32) + got[...].astype(jnp.float32)
+    if len(outs) == 1:
+        outs[0][...] = value.astype(jnp.bfloat16)
+        return
+    half = pl.num_programs(0) // 2
+
+    @pl.when(pl.program_id(0) < half)
+    def _():
+        outs[0][...] = value.astype(jnp.bfloat16)
+
+    @pl.when(pl.program_id(0) >= half)
+    def _():
+        outs[1][...] = value.astype(jnp.bfloat16)
+
+
+def plus(held, got, halves):
+    rows, width = held.shape
+    steps = 4 if rows % 64 == 0 else 2
+    block = (rows // steps, width)
+    if halves:
+        half = steps // 2
+        source = lambda i: (lax.rem(i + half, steps), 0)
+        out_specs = [
+            pl.BlockSpec(block, lambda i: (jnp.minimum(i, half - 1), 0)),
+            pl.BlockSpec(block, lambda i: (jnp.maximum(i - half, 0), 0)),
+        ]
+        out_shape = [jax.ShapeDtypeStruct((rows // 2, width), jnp.bfloat16)] * 2
+    else:
+        source = lambda i: (i, 0)
+        out_specs = [pl.BlockSpec(block, source)]
+        out_shape = [jax.ShapeDtypeStruct((rows, width), jnp.bfloat16)]
+    out = pl.pallas_call(
+        plus_kernel,
+        grid=(steps,),
+        in_specs=[pl.BlockSpec(block, source)] * 2,
+        out_specs=out_specs,
+        out_shape=out_shape,
+        compiler_params=pltpu.CompilerParams(vmem_limit_bytes=24 << 20),
+        cost_estimate=FREE,
+        name="plus",
+    )(held, got)
+    return out if halves else out[0]
+
+
+def join_kernel(axis, *refs):
+    *parts, out, inside, in_sems, out_sems = refs
+    arriving, leaving, first = [], [], 0
+    for i, part in enumerate(parts):
+        extent = part.shape[axis]
+        cut = (pl.ds(first, extent), slice(None)) if axis == 0 else (slice(None), pl.ds(first, extent))
+        arriving.append(pltpu.make_async_copy(part, inside.at[cut], in_sems.at[i]))
+        leaving.append(pltpu.make_async_copy(inside.at[cut], out.at[cut], out_sems.at[i]))
+        first += extent
+    for copy in arriving:
+        copy.start()
+    for arrived, left in zip(arriving, leaving):
+        arrived.wait()
+        left.start()
+    for copy in leaving:
+        copy.wait()
+
+
+def join(parts, axis):
+    shape = list(parts[0].shape)
+    shape[axis] = sum(part.shape[axis] for part in parts)
+    anywhere = pl.BlockSpec(memory_space=pl.ANY)
+    return pl.pallas_call(
+        functools.partial(join_kernel, axis),
+        in_specs=[anywhere] * len(parts),
+        out_specs=anywhere,
+        out_shape=jax.ShapeDtypeStruct(tuple(shape), parts[0].dtype),
+        scratch_shapes=[
+            pltpu.VMEM(tuple(shape), parts[0].dtype),
+            pltpu.SemaphoreType.DMA((len(parts),)),
+            pltpu.SemaphoreType.DMA((len(parts),)),
+        ],
+        compiler_params=pltpu.CompilerParams(vmem_limit_bytes=24 << 20),
+        cost_estimate=FREE,
+        name="join",
+    )(*parts)
+
+
+def rows_kernel(contract, count, places, *refs):
+    parts, (weight, out) = refs[:count], refs[count:]
+    for i, part in enumerate(parts):
+        rows = part.shape[contract[0] ^ 1]
+        out[pl.ds(pl.multiple_of(places[i] * rows, 16), rows), :] = lax.dot_general(
+            part[...],
+            weight[...],
+            (((contract[0],), (contract[1],)), ((), ())),
+            preferred_element_type=jnp.float32,
+        ).astype(jnp.bfloat16)
+
+
+def rows_product(parts, weight, contract, name, places=None):
+    count = len(parts)
+    if places is None:
+        places = jnp.arange(count, dtype=jnp.int32)
+    rows, width = parts[0].shape[contract[0] ^ 1], weight.shape[contract[1] ^ 1]
+    return pl.pallas_call(
+        functools.partial(rows_kernel, contract, count),
+        in_specs=[pl.BlockSpec(memory_space=pltpu.SMEM)] + in_vmem(count + 1),
+        out_specs=pl.BlockSpec(memory_space=pltpu.VMEM),
+        out_shape=jax.ShapeDtypeStruct((rows * count, width), jnp.bfloat16),
+        compiler_params=pltpu.CompilerParams(vmem_limit_bytes=40 << 20),
+        cost_estimate=FREE,
+        name=name,
+    )(places, *parts, weight)
 
 
 def ring_of(count):
@@ -368,16 +476,16 @@
 
 
 class RingScatter:
-    def __init__(self, partial):
-        self.partial, self.steps = partial, 1
-        self.held = take_rows(partial, ring_place(1))
+    def __init__(self, part):
+        self.part, self.steps = part, 1
+        self.held = part(1)
         self.flying = ring_pass(self.held)
 
     def step(self, order):
         if self.steps_left():
-            got, partial = order.take(self.flying, self.partial)
             self.steps += 1
-            self.held = add_low(take_rows(partial, ring_place(self.steps)), got)
+            got, own = order.take(self.flying, self.part(self.steps % lax.axis_size("mp")))
+            self.held = add_low(own, got)
             order.mark(self.held)
             if self.steps_left():
                 self.flying = ring_pass(self.held)
@@ -448,86 +556,339 @@
         return jnp.concatenate([core * count + relative, (1 - core) * count + relative])
 
 
-def lay_kernel(sets, pieces, axis, split, places, *refs):
-    sources, out = refs[:sets], refs[sets]
-    landed, raised, in_sems, out_sems = refs[sets + 1 :]
-    total, slots = sets * pieces, raised.shape[0]
-    rows, columns = landed.shape[1:]
+def kept_first(first_bit_first):
+    count = lax.axis_size("dp")
+    bits = bits_of(count) - 1
+    order = [turned_bits(i, bits) if first_bit_first else i for i in range(count // 2)]
+    own = lax.axis_index("dp").astype(jnp.int32)
+    relative = jnp.asarray([2 * i for i in order] + [2 * i + 1 for i in order], jnp.int32)
+    return relative ^ own
+
+
+def product_kernel(groups, split, places, *refs):
+    inputs, at = [], 0
+    for parts, beside in groups:
+        inputs.append((refs[at : at + parts], refs[at + parts : at + parts * (1 + beside)]))
+        at += parts * (1 + beside)
+    scratch = refs[len(refs) - 2 * len(groups) :]
+    values = []
+    for g, ((lefts, rights), (parts, _)) in enumerate(zip(inputs, groups)):
+        left, right = scratch[2 * g : 2 * g + 2]
+        count, width = rights[0].shape
+
+        @pl.when(pl.program_id(0) == 0)
+        def _(rights=rights, right=right, count=count, width=width, parts=parts):
+            for i, part in enumerate(rights):
+                row, column = i % parts * count, i // parts * width
+                right[row : row + count, column : column + width] = part[...]
+
+        for i, part in enumerate(lefts):
+            left[i * count : (i + 1) * count, :] = part[...]
+        values.append(
+            lax.dot_general(
+                left[...], right[...], (((0,), (0,)), ((), ())), preferred_element_type=jnp.float32
+            ).astype(jnp.bfloat16)
+        )
+    first = 0
+    for value in values:
+        cut = (slice(None), slice(first, first + value.shape[1]))
+        first += value.shape[1]
+        if split is None:
+            refs[at][cut] = value
+            continue
+        other, sent, held = refs[at : at + 3]
+        total = (value.astype(jnp.float32) + other[cut].astype(jnp.float32)).astype(jnp.bfloat16)
+
+        @pl.when(pl.program_id(0) < split)
+        def _(total=total, cut=cut):
+            sent[cut] = total
+
+        @pl.when(pl.program_id(0) >= split)
+        def _(total=total, cut=cut):
+            held[cut] = total
+
+
+def product_blocks(products, places, rows, name, other=None):
+    blocks = places.shape[0]
+    if other is None:
+        split, order, inputs = None, lambda i: i, ()
+    else:
+        split, order, inputs = blocks // 2, lambda i: lax.rem(i + blocks // 2, blocks), (other,)
+    arrays, in_specs, scratch, groups, total = [], [], [], [], 0
+    for lefts, rights in products:
+        tokens = lefts[0].shape[0]
+        moving = pl.BlockSpec((tokens, rows), lambda i, places: (0, places[order(i)]))
+        arrays += list(lefts)
+        in_specs += [moving] * len(lefts)
+        width = sum(right[0].shape[1] for right in rights)
+        for right in rights:
+            arrays += list(right)
+            in_specs += [pl.BlockSpec(right[0].shape, lambda i, places: (0, 0))] * len(right)
+        scratch += [
+            pltpu.VMEM((tokens * len(lefts), rows), jnp.bfloat16),
+            pltpu.VMEM((tokens * len(lefts), width), jnp.bfloat16),
+        ]
+        groups.append((len(lefts), len(rights)))
+        total += width
+    block = (rows, total)
+    if other is None:
+        out_specs = pl.BlockSpec(block, lambda i, places: (i, 0))
+        out_shape = jax.ShapeDtypeStruct((blocks * rows, total), jnp.bfloat16)
+    else:
+        in_specs.append(pl.BlockSpec(block, lambda i, places: (order(i), 0)))
+        out_specs = [
+            pl.BlockSpec(block, lambda i, places: (jnp.minimum(i, split - 1), 0)),
+            pl.BlockSpec(block, lambda i, places: (jnp.maximum(i - split, 0), 0)),
+        ]
+        out_shape = [jax.ShapeDtypeStruct((split * rows, total), jnp.bfloat16)] * 2
+    return pl.pallas_call(
+        functools.partial(product_kernel, tuple(groups), split),
+        grid_spec=pltpu.PrefetchScalarGridSpec(
+            num_scalar_prefetch=1,
+            grid=(blocks,),
+            in_specs=in_specs,
+            out_specs=out_specs,
+            scratch_shapes=scratch,
+        ),
+        out_shape=out_shape,
+        compiler_params=pltpu.CompilerParams(vmem_limit_bytes=48 << 20),
+        cost_estimate=FREE,
+        name=name,
+    )(places, *arrays, *inputs)
+
+
+class BlockLane:
+    def __init__(self, order, products, bits, name, first_row=0, rows=None):
+        self.bits, self.name, self.products = list(bits), name, products
+        self.rows = rows or products[0][0][0].shape[1] // lax.axis_size("dp")
+        self.first_row = first_row
+        self.places = kept_first(bits[1] == 1)
+        self.table = self.places + first_row // self.rows
+        half = self.places.shape[0] // 2
+        self.sent = product_blocks(self.taken(order), self.table[half:], self.rows, name + "_sent")
+        order.mark(self.sent)
+        self.flying = trade(self.sent, 0)
+        self.steps = ["product"] + ["halve"] * (len(bits) - 1) + ["double"] * (len(bits) - 1)
+        self.steps += ["core"]
+
+    def taken(self, order):
+        leaves, shape = jax.tree.flatten(self.products)
+        return jax.tree.unflatten(shape, order.take(*leaves))
+
+    def step(self, order):
+        kind = self.steps.pop(0)
+        if kind == "product":
+            self.bits.pop(0)
+            got = order.take(self.flying)
+            half = self.places.shape[0] // 2
+            self.sent, self.held = product_blocks(
+                self.taken(order), self.table[:half], self.rows, self.name + "_kept", got
+            )
+            self.done_bits = []
+            self.flying = trade(self.sent, self.bits[0])
+            order.mark(self.sent, self.held)
+            return
+        if kind == "both":
+            near, far, own = order.take(*self.flying, self.held)
+            self.held = self.sent = (own, near, far)
+            self.flying = trade(near, self.done_bits[0])
+            order.mark(self.held)
+            return
+        if kind == "rest":
+            self.held = self.sent = join(order.take(*self.held, self.flying), 0)
+            self.flying = trade(self.held, 0)
+            order.mark(self.held)
+            return
+        got, held = order.take(self.flying, self.held)
+        if kind == "core":
+            self.pieces = [held, got]
+            order.mark(self.pieces)
+            return
+        if kind == "halve":
+            self.done_bits.append(self.bits.pop(0))
+            if self.bits:
+                self.sent, self.held = plus(held, got, True)
+                self.flying = trade(self.sent, self.bits[0])
+                order.mark(self.sent, self.held)
+                return
+            held = plus(held, got, False)
+            if len(self.done_bits) == 2:
+                self.steps = ["both", "rest", "core"]
+                self.held = self.sent = held
+                self.flying = (trade(held, self.done_bits[1]), trade(held, self.done_bits[0]))
+                order.mark(held)
+                return
+        else:
+            self.done_bits.pop()
+            held = join([held, got], 0)
+        self.held = self.sent = held
+        self.flying = trade(held, self.done_bits[-1] if self.done_bits else 0)
+        order.mark(self.held)
+
+
+def block_lanes(order, products, name):
+    first, second = orders()
+    total = products[0][0][0].shape[1]
+    rows = total // lax.axis_size("dp")
+    if rows % 256:
+        return [BlockLane(order, products, first, name)]
+    return [
+        BlockLane(order, products, first, name + "_low", 0, rows // 2),
+        BlockLane(order, products, second, name + "_high", total // 2, rows // 2),
+    ]
+
+
+def unfold_kernel(firsts, pieces, targets, places, *refs):
+    sets = 2 * len(firsts)
+    sources, outs = refs[:sets], refs[sets : sets + len(targets)]
+    landed = refs[sets + len(targets)]
+    raised = refs[sets + len(targets) + 1 : -2]
+    in_sems, out_sems = refs[-2:]
+    rows = landed.shape[1]
+    slots = raised[0].shape[0]
+    total = sets * pieces
 
     def fetch(i):
-        first = i % pieces * (rows, columns)[axis]
         source = sources[i // pieces]
-        window = (
-            source.at[pl.ds(first, rows), :] if axis == 0 else source.at[:, pl.ds(first, columns)]
+        return pltpu.make_async_copy(
+            source.at[pl.ds(i % pieces * rows, rows), :], landed.at[i], in_sems.at[i]
         )
-        return pltpu.make_async_copy(window, landed.at[i], in_sems.at[i])
 
     def store(i):
-        along = places[i]
-        across = i * split // total
-        if axis == 0:
-            window = out.at[
-                pl.ds(pl.multiple_of(along * rows, rows), rows), pl.ds(across * columns, columns)
-            ]
-        else:
-            window = out.at[
-                pl.ds(across * rows, rows), pl.ds(pl.multiple_of(along * columns, 128), columns)
-            ]
-        return pltpu.make_async_copy(raised.at[i % slots], window, out_sems.at[i])
+        along = pl.multiple_of(firsts[i // (2 * pieces)] + places[i] * rows, rows)
+        copies = []
+        for k, ((_, turned), out) in enumerate(zip(targets, outs)):
+            window = out.at[:, pl.ds(along, rows)] if turned else out.at[pl.ds(along, rows), :]
+            copies.append(
+                pltpu.make_async_copy(
+                    raised[k].at[i % slots], window, out_sems.at[i * len(targets) + k]
+                )
+            )
+        return copies
 
     for i in range(total):
         fetch(i).start()
     for i in range(total):
         fetch(i).wait()
         if i >= slots:
-            store(i - slots).wait()
-        raised[i % slots] = landed[i].astype(jnp.float32)
-        store(i).start()
+            for copy in store(i - slots):
+                copy.wait()
+        first = 0
+        for k, (width, turned) in enumerate(targets):
+            value = landed[i, :, first : first + width].astype(jnp.float32)
+            raised[k][i % slots] = value.T if turned else value
+            first += width
+        for copy in store(i):
+            copy.start()
     for i in range(max(total - slots, 0), total):
-        store(i).wait()
-
-
-def lay_out(lanes, shape, name):
+        for copy in store(i):
+            copy.wait()
+
+
+def unfold(lanes, targets, name):
+    sets = [piece for lane in lanes for piece in lane.pieces]
+    rows, width = lanes[0].rows, sets[0].shape[1]
+    pieces = sets[0].shape[0] // rows
+    total, slots = len(sets) * pieces, 4
+    height = total * rows
+    anywhere = pl.BlockSpec(memory_space=pl.ANY)
+    return pl.pallas_call(
+        functools.partial(
+            unfold_kernel, tuple(lane.first_row for lane in lanes), pieces, tuple(targets)
+        ),
+        in_specs=[pl.BlockSpec(memory_space=pltpu.SMEM)] + [anywhere] * len(sets),
+        out_specs=[anywhere] * len(targets),
+        out_shape=[
+            jax.ShapeDtypeStruct((w, height) if turned else (height, w), jnp.float32)
+            for w, turned in targets
+        ],
+        scratch_shapes=[pltpu.VMEM((total, rows, width), jnp.bfloat16)]
+        + [
+            pltpu.VMEM((slots, w, rows) if turned else (slots, rows, w), jnp.float32)
+            for w, turned in targets
+        ]
+        + [
+            pltpu.SemaphoreType.DMA((total,)),
+            pltpu.SemaphoreType.DMA((total * len(targets),)),
+        ],
+        compiler_params=pltpu.CompilerParams(vmem_limit_bytes=48 << 20),
+        cost_estimate=FREE,
+        name=name,
+    )(jnp.concatenate([lane.places for lane in lanes]), *sets)
+
+
+def lay_kernel(lanes, sets, pieces, axis, cuts, places, *refs):
+    outs = refs[lanes * sets : -4]
+    landed, raised, in_sems, out_sems = refs[-4:]
+    rows, columns = landed.shape[1:]
+    slots = raised.shape[0]
+    total = lanes * sets * pieces
+
+    def window(ref, along, across, extent):
+        if axis == 0:
+            return ref.at[pl.ds(along, rows), pl.ds(across, extent)]
+        return ref.at[pl.ds(across, extent), pl.ds(along, columns)]
+
+    def fetch(i):
+        first = i % pieces * (rows, columns)[axis]
+        source = refs[i // pieces]
+        across = source.shape[1 - axis]
+        return pltpu.make_async_copy(
+            window(source, first, 0, across), window(landed.at[i], 0, 0, across), in_sems.at[i]
+        )
+
+    def store(i):
+        along = pl.multiple_of(places[i] * (rows, columns)[axis], (rows, columns)[axis])
+        return [
+            pltpu.make_async_copy(
+                window(raised.at[i % slots], 0, first, extent),
+                window(outs[out], along, target, extent),
+                out_sems.at[2 * i + k],
+            )
+            for k, (out, first, extent, target) in enumerate(cuts[i // (sets * pieces)])
+        ]
+
+    for i in range(total):
+        fetch(i).start()
+    for i in range(total):
+        fetch(i).wait()
+        if i >= slots:
+            for copy in store(i - slots):
+                copy.wait()
+        extent = refs[i // pieces].shape[1 - axis]
+        filled = (slice(None), slice(extent)) if axis == 0 else (slice(extent), slice(None))
+        raised[(i % slots, *filled)] = landed[(i, *filled)].astype(jnp.float32)
+        for copy in store(i):
+            copy.start()
+    for i in range(max(total - slots, 0), total):
+        for copy in store(i):
+            copy.wait()
+
+
+def lay_out(lanes, cuts, shapes, name):
     sets = [piece for lane in lanes for piece in lane.pieces]
     axis = lanes[0].axis
     places = jnp.concatenate([lane.places() for lane in lanes])
     pieces = places.shape[0] // len(sets)
-    block = list(sets[0].shape)
+    block = [max(piece.shape[d] for piece in sets) for d in (0, 1)]
     block[axis] //= pieces
     total = len(sets) * pieces
     anywhere = pl.BlockSpec(memory_space=pl.ANY)
     return pl.pallas_call(
-        functools.partial(lay_kernel, len(sets), pieces, axis, len(lanes)),
+        functools.partial(lay_kernel, len(lanes), len(lanes[0].pieces), pieces, axis, cuts),
         in_specs=[pl.BlockSpec(memory_space=pltpu.SMEM)] + [anywhere] * len(sets),
-        out_specs=anywhere,
-        out_shape=jax.ShapeDtypeStruct(shape, jnp.float32),
+        out_specs=[anywhere] * len(shapes),
+        out_shape=[jax.ShapeDtypeStruct(shape, jnp.float32) for shape in shapes],
         scratch_shapes=[
             pltpu.VMEM((total, *block), jnp.bfloat16),
             pltpu.VMEM((min(total, 6), *block), jnp.float32),
             pltpu.SemaphoreType.DMA((total,)),
-            pltpu.SemaphoreType.DMA((total,)),
+            pltpu.SemaphoreType.DMA((2 * total,)),
         ],
-        compiler_params=pltpu.CompilerParams(vmem_limit_bytes=40 << 20),
-        cost_estimate=pl.CostEstimate(
-            flops=0, bytes_accessed=6 * shape[0] * shape[1], transcendentals=0
-        ),
+        compiler_params=pltpu.CompilerParams(vmem_limit_bytes=44 << 20),
+        cost_estimate=FREE,
         name=name,
     )(places, *sets)
-
-
-def sum_halves(partial, axis):
-    first, second = orders()
-    half = partial.shape[1 - axis] // 2
-    low = lax.slice_in_dim(partial, 0, half, axis=1 - axis)
-    high = lax.slice_in_dim(partial, half, 2 * half, axis=1 - axis)
-    return [Lane(low, first, axis), Lane(high, second, axis)]
-
-
-def sum_ranks(array):
-    count = lax.axis_size("mp")
-    for bit in range(bits_of(count)):
-        array = array + lax.ppermute(array, "mp", [(i, i ^ (1 << bit)) for i in range(count)])
-    return array
 
 
 def own_share(array):
@@ -546,12 +907,10 @@
         self.bits.pop(0)
         got, held = order.take(self.flying, self.held)
         if self.bits:
-            half = held.shape[0] // 2
-            self.sent = add_low(held[half:], got[half:])
-            self.held = add_low(held[:half], got[:half])
+            self.sent, self.held = plus(held, got, True)
             self.flying = trade(self.sent, self.bits[0])
         else:
-            self.held = self.sent = add_low(held, got)
+            self.held = self.sent = plus(held, got, False)
         order.mark(self.sent, self.held)
 
 
@@ -626,14 +985,16 @@
     head_dim = HEAD_DIM
     local_heads = query_up.shape[1] // head_dim
     ranks = lax.axis_size("mp")
-    group = lax.axis_index("dp").reshape(1)
+    group = lax.axis_index("dp").reshape(1).astype(jnp.int32)
+    ring_places = jnp.stack([ring_place(i) for i in range(lax.axis_size("mp"))])
     first, second = orders()
 
-    def gather(rows):
-        return lax.all_gather(rows, "mp", axis=0, tiled=True)
-
-    def scatter(rows):
-        return lax.psum_scatter(rows, "mp", scatter_dimension=0, tiled=True)
+    def rows_of(array):
+        return lambda back: take_rows(array, ring_place(back))
+
+    def parts_of(array):
+        count = array.shape[0] // ranks
+        return lambda back: array[back * count : (back + 1) * count]
 
     def weight_grad(left, right):
         return jnp.einsum("tk,td->kd", left, right, preferred_element_type=jnp.float32).astype(
@@ -674,173 +1035,196 @@
     while keys.bits:
         steps(keys, values)
     steps(grad_ring, keys, values)
+    share_parts = column_share(order.take(normal_one))
     sources = order.take(*keys.parts, *values.parts)
     attended, kept, logs = attention_forward(group, query_full, sources, local_heads, head_dim)
     order.mark(attended)
+    share_parts = order.take(*share_parts)
+    order.mark(*share_parts)
     steps(grad_ring)
-    share_parts = column_share(order.take(normal_one))
     attn_partial = dotf(order.take(attended), attn_out).astype(jnp.bfloat16)
     order.mark(attn_partial)
-    attn_sum = scatter(attn_partial)
+    attn_ring = RingScatter(rows_of(attn_partial))
     while grad_ring.steps_left():
         steps(grad_ring)
-    share_parts = order.take(*share_parts)
-    order.mark(*share_parts)
-    grad_full = order.take(grad_ring.rows())
-    act_grad = jnp.einsum("td,fd->tf", grad_full, down_weight, preferred_element_type=jnp.float32)
+    grad_ringed = jnp.concatenate(order.take(*grad_ring.parts), axis=0)
+    act_grad = jnp.einsum("td,fd->tf", grad_ringed, down_weight, preferred_element_type=jnp.float32)
     normal_share = ring_rows(share_parts)
     order.mark(act_grad, normal_share)
-    hidden_res = inputs + order.take(attn_sum).astype(jnp.float32)
+    while attn_ring.steps_left():
+        steps(attn_ring)
+    hidden_res = inputs + attn_ring.held.astype(jnp.float32)
     normal_two = normalize(hidden_res, mlp_gain).astype(jnp.bfloat16)
     order.mark(normal_two)
-    normal_full = order.take(gather(normal_two))
-    gate = dotf(normal_full, gate_weight)
-    upward = dotf(normal_full, up_weight)
-    activated = gated(gate, upward).astype(jnp.bfloat16)
-    _, gated_pull = jax.vjp(gated, gate, upward)
-    gate_grad32, up_grad32 = gated_pull(act_grad)
-    gate_low = gate_grad32.astype(jnp.bfloat16)
-    up_low = up_grad32.astype(jnp.bfloat16)
-    two_partial = (
-        jnp.einsum("tf,df->td", gate_low, gate_weight, preferred_element_type=jnp.float32)
-        + jnp.einsum("tf,df->td", up_low, up_weight, preferred_element_type=jnp.float32)
-    ).astype(jnp.bfloat16)
-    order.mark(two_partial)
-    two_sum = scatter(two_partial)
-    down_part = weight_grad(order.take(activated), grad_full)
-    order.mark(down_part)
-    down = sum_halves(order.take(down_part), 1)
-    order.mark([lane.sent for lane in down])
-    gate_part = weight_grad(order.take(normal_full), gate_low)
-    order.mark(gate_part)
-    gate_lane = Lane(order.take(gate_part), first, 0)
-    order.mark(gate_lane.sent)
-    steps(*down)
-    up_part = weight_grad(order.take(normal_full), up_low)
-    order.mark(up_part)
-    up_lane = Lane(order.take(up_part), second, 0)
-    order.mark(up_lane.sent)
-    steps(gate_lane, up_lane)
-    steps(*down)
-    result_partial = dotf(order.take(activated), down_weight).astype(jnp.bfloat16)
-    order.mark(result_partial)
-    normal_two_grad = order.take(two_sum).astype(jnp.float32)
+    two_ring = RingGather(normal_two)
+    act_parts = parts_of(act_grad)
+    activated, gate_low, up_low, two_terms = [], [], [], []
+    two_sum = None
+    for block in range(ranks):
+        steps(*([two_ring] if block else []))
+        rows = order.take(two_ring.parts[block])
+        gate = dotf(rows, gate_weight)
+        upward = dotf(rows, up_weight)
+        _, gated_pull = jax.vjp(gated, gate, upward)
+        gate_grad32, up_grad32 = gated_pull(act_parts(block))
+        activated.append(gated(gate, upward).astype(jnp.bfloat16))
+        gate_low.append(gate_grad32.astype(jnp.bfloat16))
+        up_low.append(up_grad32.astype(jnp.bfloat16))
+        two_terms.append(
+            (
+                jnp.einsum("tf,df->td", gate_low[-1], gate_weight, preferred_element_type=jnp.float32)
+                + jnp.einsum("tf,df->td", up_low[-1], up_weight, preferred_element_type=jnp.float32)
+            ).astype(jnp.bfloat16)
+        )
+        order.mark(two_terms[-1], activated[-1])
+        if block == 1:
+            two_sum = RingScatter(lambda back: two_terms[back])
+        elif block > 1:
+            steps(two_sum)
+    while two_sum.steps_left():
+        steps(two_sum)
+    normal_two_grad = two_sum.held.astype(jnp.float32)
     _, norm_pull_two = jax.vjp(normalize, hidden_res, mlp_gain)
     resid_from_norm, mlp_gain_part = norm_pull_two(normal_two_grad)
     hidden_grad = out_grad.astype(jnp.float32) + resid_from_norm
     branch = hidden_grad.astype(jnp.bfloat16)
     order.mark(branch)
-    branch_full = gather(branch)
-    steps(gate_lane, up_lane)
-    steps(*down)
-    mlp_gain_sum = SmallSum(order.take(mlp_gain_part), "mp")
-    steps(gate_lane, up_lane)
-    steps(mlp_gain_sum)
-    steps(*down)
-    while mlp_gain_sum.bits:
-        steps(mlp_gain_sum)
-    branch_full = order.take(branch_full)
-    attended_low = jnp.einsum(
-        "td,kd->tk", branch_full, attn_out, preferred_element_type=jnp.float32
-    ).astype(jnp.bfloat16)
+    branch_ring = RingGather(branch)
+    def part_sent(*lanes):
+        order.mark([lane.sent for lane in lanes])
+
+    low_parts = []
+
+    def low_part():
+        rows = order.take(branch_ring.parts[len(low_parts)])
+        low_parts.append(rows_product([rows], attn_out, (1, 1), "attended_low"))
+        order.mark(low_parts[-1])
+
+    mlp = block_lanes(
+        order,
+        [(grad_ring.parts, [activated]), (two_ring.parts, [gate_low, up_low])],
+        "mlp_grads",
+    )
+    steps(branch_ring)
+    low_part()
+    low_part()
+    steps(mlp[0])
+    steps(branch_ring)
+    low_part()
+    steps(*mlp[1:])
+    while branch_ring.steps_left():
+        steps(branch_ring)
+        low_part()
+    while len(low_parts) < ranks:
+        low_part()
+    attended_low = ring_rows(low_parts)
     order.mark(attended_low)
-    result_sum = scatter(order.take(result_partial))
-    steps(gate_lane, up_lane)
     query_low, key_grads, value_grads = attention_backward(
         group, query_full, order.take(attended_low), sources, kept, logs, local_heads, head_dim
     )
-    beside = [lane.flying for lane in down + [gate_lane, up_lane]]
     query_low, key_grads, value_grads = lax.optimization_barrier(
-        (query_low, key_grads, value_grads, *beside)
+        (query_low, key_grads, value_grads, mlp[0].flying)
     )[:3]
     order.mark(query_low)
     key_sum = BlockSum(order.take(key_grads), first)
     value_sum = BlockSum(order.take(value_grads), second)
-    order.mark(key_sum.sent, value_sum.sent)
-    latent_partial = jnp.einsum(
-        "tk,rk->tr", order.take(query_low), query_up, preferred_element_type=jnp.float32
-    ).astype(jnp.bfloat16)
+    part_sent(key_sum, value_sum)
+    steps(*mlp)
+    latent_partial = rows_product([order.take(query_low)], query_up, (1, 1), "latent_low")
     order.mark(latent_partial)
-    latent_sum = RingScatter(latent_partial)
-    up_query_part = weight_grad(latent_full, order.take(query_low))
-    order.mark(up_query_part)
+    latent_low = lax.psum_scatter(latent_partial, "mp", scatter_dimension=0, tiled=True)
     steps(key_sum, value_sum)
-    out_part = weight_grad(order.take(attended), branch_full)
-    order.mark(out_part)
-    steps(*down)
-    steps(latent_sum)
-    out_part, up_query_part, result_sum = order.take(out_part, up_query_part, result_sum)
-    order.mark(out_part, up_query_part)
+    up_query_part = rows_product([latent_full], order.take(query_low), (0, 0), "query_up_grad")
+    out_part = weight_grad(attended, ring_rows(order.take(*branch_ring.parts)))
+    order.mark(up_query_part, out_part)
     out_sum, up_query_sum = lax.psum((out_part, up_query_part), "dp")
-    finish(*down)
-    down_sum = lay_out(down, (activated.shape[1], grad_full.shape[1]), "down_grad")
-    order.mark(down_sum)
     steps(key_sum, value_sum)
-    steps(latent_sum)
-    steps(gate_lane, up_lane)
-    while len(key_sum.bits) > 1:
-        steps(key_sum, value_sum)
-    while latent_sum.steps_left():
-        steps(latent_sum)
-    latent_low = latent_sum.held
-    low_ring = RingGather(latent_low)
-    finish(gate_lane, up_lane)
+    steps(*mlp)
     while key_sum.bits:
         steps(key_sum, value_sum)
-    pair_partial = jnp.concatenate([key_sum.held, value_sum.held], axis=1)
+    pair_partial = join(order.take(key_sum.held, value_sum.held), 1)
     order.mark(pair_partial)
-    pair_low_sum = RingScatter(pair_partial)
-    gate_sum = lay_out([gate_lane], gate_weight.shape, "gate_grad")
-    order.mark(gate_sum)
-    steps(pair_low_sum, low_ring)
-    up_sum = lay_out([up_lane], up_weight.shape, "up_grad")
-    order.mark(up_sum)
+    pair_low_sum = RingScatter(rows_of(pair_partial))
+    steps(pair_low_sum)
+    latent_low = order.take(latent_low)
+    order.mark(latent_low)
+    low_full = lax.all_gather(latent_low, "mp", axis=0, tiled=True)
     while pair_low_sum.steps_left():
-        steps(pair_low_sum, low_ring)
+        steps(pair_low_sum)
     pair_low = pair_low_sum.held
     low_pair_ring = RingGather(pair_low)
-    normal_one_grad = jnp.einsum(
-        "tr,dr->td", latent_low, query_down, preferred_element_type=jnp.float32
-    ) + jnp.einsum("tp,dp->td", order.take(pair_low), key_value, preferred_element_type=jnp.float32)
+    result_partial = rows_product(
+        order.take(*activated), down_weight, (1, 0), "result", ring_places
+    )
+    order.mark(result_partial)
+    steps(low_pair_ring)
+    steps(*mlp)
+    while low_pair_ring.steps_left():
+        steps(low_pair_ring)
+    pair_weight_part = rows_product(
+        [normal_share], order.take(low_pair_ring.rows()), (0, 0), "key_value_grad"
+    )
+    order.mark(pair_weight_part)
+    pair_weight = Lane(order.take(pair_weight_part), first, 0)
+    part_sent(pair_weight)
+    down_query_part = rows_product(
+        [normal_share], order.take(low_full), (0, 0), "query_down_grad"
+    )
+    order.mark(down_query_part)
+    down_query = Lane(order.take(down_query_part), second, 0)
+    part_sent(down_query)
+    result_sum = lax.psum_scatter(
+        after(result_partial, low_full), "mp", scatter_dimension=0, tiled=True
+    )
+    steps(pair_weight, down_query)
+    latent_term = jnp.einsum(
+        "tr,dr->td", order.take(latent_low), query_down, preferred_element_type=jnp.float32
+    )
+    order.mark(latent_term)
+    normal_one_grad = latent_term + jnp.einsum(
+        "tp,dp->td", order.take(pair_low), key_value, preferred_element_type=jnp.float32
+    )
     _, norm_pull_one = jax.vjp(normalize, inputs, attn_gain)
     input_from_norm, attn_gain_part = norm_pull_one(normal_one_grad)
     input_grad = hidden_grad + input_from_norm
     order.mark(input_grad, attn_gain_part)
     attn_gain_sum = SmallSum(order.take(attn_gain_part), "mp")
-    while low_ring.steps_left():
-        steps(low_ring)
-    steps(low_pair_ring)
-    down_query_part = weight_grad(normal_share, order.take(low_ring.rows()))
-    order.mark(down_query_part)
-    down_query = Lane(order.take(down_query_part), first, 0)
-    order.mark(down_query.sent)
-    steps(attn_gain_sum)
-    steps(low_pair_ring)
-    while low_pair_ring.steps_left() > 1:
-        steps(low_pair_ring, attn_gain_sum)
-    while attn_gain_sum.bits:
-        steps(attn_gain_sum)
+    mlp_gain_sum = SmallSum(order.take(mlp_gain_part), "mp")
+    steps(pair_weight, down_query)
+    while attn_gain_sum.bits or mlp_gain_sum.bits:
+        steps(attn_gain_sum, mlp_gain_sum)
     gains = jnp.stack([own_share(attn_gain_sum.held), own_share(mlp_gain_sum.held)])
     order.mark(gains)
-    gains = SmallSum(gains, "dp")
-    steps(low_pair_ring)
-    pair_weight_part = weight_grad(normal_share, order.take(low_pair_ring.rows()))
-    order.mark(pair_weight_part)
-    pair_weight = Lane(order.take(pair_weight_part), second, 0)
-    order.mark(pair_weight.sent)
+    steps(pair_weight, down_query)
+    gains = SmallSum(order.take(gains), "dp")
+    while len(down_query.steps) > 2:
+        steps(pair_weight, down_query)
+        steps(gains)
+    out_sum, up_query_sum = order.take(out_sum, up_query_sum)
+    order.mark(out_sum, up_query_sum)
+    while len(mlp[0].steps) > 1:
+        steps(*mlp)
+    steps(pair_weight, down_query)
+    out_sum = order.take(out_sum).astype(jnp.float32)
+    up_query_sum = up_query_sum.astype(jnp.float32)
+    order.mark(out_sum, up_query_sum)
+    finish(pair_weight, down_query)
+    while gains.bits:
+        steps(gains)
+    cuts = tuple(((i, 0, part.shape[1], 0),) for i, part in enumerate((query_down, key_value)))
+    down_query_sum, pair_weight_sum = lay_out(
+        [down_query, pair_weight],
+        cuts,
+        [(normal_share.shape[1], part.shape[1]) for part in (query_down, key_value)],
+        "query_down_key_value_laid",
+    )
+    order.mark(down_query_sum)
+    finish(*mlp)
+    down_sum, gate_sum, up_sum = unfold(
+        mlp, [(down_weight.shape[0], True)] + [(gate_weight.shape[1], False)] * 2, "mlp_grads_laid"
+    )
+    order.mark(down_sum)
     result = (hidden_res + order.take(result_sum).astype(jnp.float32)).astype(jnp.bfloat16)
-    order.mark(result)
-    while down_query.steps or gains.bits:
-        if down_query.steps:
-            steps(down_query, pair_weight)
-        steps(gains)
-    down_query_sum = lay_out(
-        [down_query], (normal_share.shape[1], query_down.shape[1]), "query_down_grad"
-    )
-    pair_weight_sum = lay_out(
-        [pair_weight], (normal_share.shape[1], key_value.shape[1]), "key_value_grad"
-    )
-    out_sum, up_query_sum = out_sum.astype(jnp.float32), up_query_sum.astype(jnp.float32)
     attn_gain_sum, mlp_gain_sum = gains.held[0], gains.held[1]
     return (
         result,

time: 693 us -> 674 us (0.973)
  Pallas kernels: 49 us -> 130 us
  matrix products: 96.7 us -> 57 us
  other arithmetic: 57.1 us -> 24.8 us
  waiting for transfers between devices: 312 us -> 283 us
  starting transfers between devices: 88.8 us -> 99.3 us
    pallas_call x5 -> x28, Pallas kernels: 28.3 us -> 110 us  [the longest x4 40.2 us: product_blocks(): pl.pallas_call(functools.partial(product_kernel, tuple(groups), split), g...]
    ppermute x21 -> x27, waiting for transfers between devices: 76.2 us -> 142 us  [ring_pass(): return lax.ppermute(array, 'mp', pairs)]
    all_gather x2 -> x1, waiting for transfers between devices: 65.1 us -> 0.01 us  [shards(): low_full = lax.all_gather(latent_low, 'mp', axis=0, tiled=True)]
    reduce_scatter x3 -> x2, waiting for transfers between devices: 37.8 us -> 0.02 us  [the longest x1 0.02 us: shards(): lax.psum_scatter(after(result_partial, low_full), 'mp', scatter_dimension...]
    convert_element_type x28 -> x12, other arithmetic: 34.3 us -> 3.97 us  [add_low(): (left.astype(jnp.float32) + right.astype(jnp.float32)).astype(jnp.bfloat16)]
    dot_general x7 -> x1, matrix products: 31.5 us -> 5.01 us  [weight_grad(): jnp.einsum('tk,td->kd', left, right, preferred_element_type=jnp.float32)]
    ppermute x21 -> x27, starting transfers between devices: 29.1 us -> 53.8 us  [ring_pass(): return lax.ppermute(array, 'mp', pairs)]
    concatenate x12 -> x4, local copies, waits for them, and re-layouts: 11.3 us -> 0.05 us  [step(): self.held = jnp.concatenate([held, got], axis=self.axis)]
  transfers between devices with their start and end apart: 87 -> 81, of which waited for: 36 -> 40; matrix products, arithmetic and copies ran while one was open for 22% -> 14% of each run, Pallas kernels for 7% -> 18%
where the time goes in v3:
time: 674 us; the launch traced here: 667 us
  waiting for transfers between devices  283 us (42%)
  Pallas kernels  130 us (19%)
  starting transfers between devices  99.3 us (15%)
  matrix products  57 us (8%)
  local copies, waits for them, and re-layouts  51.8 us (8%)
  other arithmetic  24.8 us (4%)
  between operations  21 us (3%)
    ppermute x27, waiting for transfers between devices, ring_pass(): return lax.ppermute(array, 'mp', pairs)  142 us
    ppermute x40, waiting for transfers between devices, trade(): return lax.ppermute(array, 'dp', [(i, i ^ 1 << bit) for i in range(count)])  103 us
    ppermute x27, starting transfers between devices, ring_pass(): return lax.ppermute(array, 'mp', pairs)  53.8 us
    pallas_call x4, Pallas kernels, product_blocks(): pl.pallas_call(functools.partial(product_kernel, tuple(groups), split), g...  40.2 us
    ppermute x40, starting transfers between devices, trade(): return lax.ppermute(array, 'dp', [(i, i ^ 1 << bit) for i in range(count)])  33.7 us
    unnamed x206, local copies, waits for them, and re-layouts  27.3 us
    psum x1, waiting for transfers between devices, shards(): out_sum, up_query_sum = lax.psum((out_part, up_query_part), 'dp')  23.7 us
    dot_general x12, matrix products, dotf(): return jnp.dot(left, right, preferred_element_type=jnp.float32)  23 us
  transfers between devices with their start and end apart: 81, of which 40 were waited for; matrix products, arithmetic and copies ran while one was open for 14% of the time, Pallas kernels for 18%

profile of v3, /device:TPU:0, one launch (start us, length us, event | category | flops | bytes accessed | tf_op | source)
XLA Modules:
  0.0 666.8 jit_solution(13901466959245658561)
XLA Ops:
  22.2 9.9 %collective-permute-done.1 = bf16[160,512]{1,0:T(8,128)(2,1)S(1)} collective-permute-done((bf16[160,512]{1,0:T(8,128)(2,1)S(1)}, bf16[160,512]{1,0:T(8,128)(2,1)S(1)}, u32[]{:S(2)}, u32[]{:S(2)}) %collective-permute-start.1) | collective-permute-done | bytes 163872 | tf_op jit(solution)/shard_map/ppermute | solution.py:436
  41.2 7.3 %collective-permute-done.2 = bf16[160,1024]{1,0:T(8,128)(2,1)S(1)} collective-permute-done((bf16[160,1024]{1,0:T(8,128)(2,1)S(1)}, bf16[160,1024]{1,0:T(8,128)(2,1)S(1)}, u32[]{:S(2)}, u32[]{:S(2)}) %collective-permute-start.2) | collective-permute-done | bytes 327712 | tf_op jit(solution)/shard_map/ppermute | solution.py:436
  94.5 8.8 %attention_forward.1 = (bf16[640,1024]{1,0:T(8,128)(2,1)}, f32[256,2560]{1,0:T(8,128)}, f32[1,2560]{1,0:T(1,128)S(1)}) custom-call(s32[1]{0:T(128)} %bitcast.group, bf16[640,1024]{1,0:T(8,128)(2,1)} %convolution_convert_fusion.2.query, bf16[1280,256]{1,0:T(8,128)(2,1)S(1)} %constant_dynamic-update-slice_fusion.refs_0_, ...), custom_call_target="tpu_custom_call" | custom-call | flops 13421772800 | bytes 5242880 | tf_op jit(solution)/shard_map/attention_forward/pallas_call | solution.py:231
  109.9 5.5 collective-permute-done.17
  120.1 7.8 %fusion = f32[640,1408]{1,0:T(8,128)} fusion(bf16[1408,2048]{1,0:T(8,128)(2,1)S(1)} %bitcast.62, bf16[160,2048]{1,0:T(8,128)(2,1)} %copy-done.60, bf16[160,2048]{1,0:T(8,128)(2,1)} %collective-permute-done.12.refs_2_, bf16[160,2048]{1,0:T(8,128)(2,1)} %collective-permute-done.8.refs_1_, bf16[160,2048]{1,0:T(8,128)(2,1)S(1)} %copy-done.2), kind=kOutput, calls=%fused_computation.2 | convolution fusion | flops 3701473280 | bytes 11993088 | tf_op jit(solution)/shard_map/td,fd->tf/dot_general | solution.py:1051
  127.9 6.7 %collective-permute-done.20 = bf16[160,2048]{1,0:T(8,128)(2,1)S(1)} collective-permute-done((bf16[160,2048]{1,0:T(8,128)(2,1)S(1)}, bf16[160,2048]{1,0:T(8,128)(2,1)S(1)}, u32[]{:S(2)}, u32[]{:S(2)}) %collective-permute-start.20) | collective-permute-done | bytes 655392 | tf_op jit(solution)/shard_map/ppermute | solution.py:436
  135.9 13.6 %collective-permute-done.21 = bf16[160,2048]{1,0:T(8,128)(2,1)S(1)} collective-permute-done((bf16[160,2048]{1,0:T(8,128)(2,1)S(1)}, bf16[160,2048]{1,0:T(8,128)(2,1)S(1)}, u32[]{:S(2)}, u32[]{:S(2)}) %collective-permute-start.21) | collective-permute-done | bytes 655392 | tf_op jit(solution)/shard_map/ppermute | solution.py:436
  152.8 12.7 %collective-permute-done.22 = bf16[160,2048]{1,0:T(8,128)(2,1)S(1)} collective-permute-done((bf16[160,2048]{1,0:T(8,128)(2,1)S(1)}, bf16[160,2048]{1,0:T(8,128)(2,1)S(1)}, u32[]{:S(2)}, u32[]{:S(2)}) %collective-permute-start.22) | collective-permute-done | bytes 655392 | tf_op jit(solution)/shard_map/ppermute | solution.py:436
  177.8 8.8 %collective-permute-done.23.refs_9_ = bf16[160,2048]{1,0:T(8,128)(2,1)S(1)} collective-permute-done((bf16[160,2048]{1,0:T(8,128)(2,1)S(1)}, bf16[160,2048]{1,0:T(8,128)(2,1)S(1)}, u32[]{:S(2)}, u32[]{:S(2)}) %collective-permute-start.23) | collective-permute-done | bytes 655392 | tf_op jit(solution)/shard_map/ppermute | solution.py:436
  199.6 5.8 collective-permute-done.24.refs_10_
  222.1 6.9 %collective-permute-done.25.refs_11_ = bf16[160,2048]{1,0:T(8,128)(2,1)S(1)} collective-permute-done((bf16[160,2048]{1,0:T(8,128)(2,1)S(1)}, bf16[160,2048]{1,0:T(8,128)(2,1)S(1)}, u32[]{:S(2)}, u32[]{:S(2)}) %collective-permute-start.25) | collective-permute-done | bytes 655392 | tf_op jit(solution)/shard_map/ppermute | solution.py:436
  237.1 5.6 collective-permute-done.27
  245.4 9.2 %collective-permute-done.28 = bf16[160,2048]{1,0:T(8,128)(2,1)S(1)} collective-permute-done((bf16[160,2048]{1,0:T(8,128)(2,1)S(1)}, bf16[160,2048]{1,0:T(8,128)(2,1)S(1)}, u32[]{:S(2)}, u32[]{:S(2)}) %collective-permute-start.28) | collective-permute-done | bytes 655392 | tf_op jit(solution)/shard_map/ppermute | solution.py:436
  256.3 8.7 %mlp_grads_low_sent.1 = bf16[512,4224]{1,0:T(8,128)(2,1)} custom-call(s32[4]{0:T(128)S(1)} %get-tuple-element.654.places, bf16[160,2048]{1,0:T(8,128)(2,1)S(1)} %copy-done.2, bf16[160,2048]{1,0:T(8,128)(2,1)} %collective-permute-done.8.refs_1_, bf16[160,2048]{1,0:T(8,128)(2,1)} %collective-permute-done.12.refs_2_, bf16[160,2048]{1,0:T(8,128)(2,1)} %copy-done.60, ...), custom_call_target="tpu_custom_call" | custom-call | tf_op jit(solution)/shard_map/mlp_grads_low_sent/pallas_call | solution.py:644
  265.6 8.7 %mlp_grads_high_sent.1 = bf16[512,4224]{1,0:T(8,128)(2,1)} custom-call(s32[4]{0:T(128)S(1)} %get-tuple-element.652.places, bf16[160,2048]{1,0:T(8,128)(2,1)S(1)} %copy-done.2, bf16[160,2048]{1,0:T(8,128)(2,1)} %collective-permute-done.8.refs_1_, bf16[160,2048]{1,0:T(8,128)(2,1)} %collective-permute-done.12.refs_2_, bf16[160,2048]{1,0:T(8,128)(2,1)} %copy-done.60, ...), custom_call_target="tpu_custom_call" | custom-call | tf_op jit(solution)/shard_map/mlp_grads_high_sent/pallas_call | solution.py:644
  277.0 15.4 %collective-permute-done.29.refs_0_ = bf16[160,2048]{1,0:T(8,128)(2,1)S(1)} collective-permute-done((bf16[160,2048]{1,0:T(8,128)(2,1)S(1)}, bf16[160,2048]{1,0:T(8,128)(2,1)S(1)}, u32[]{:S(2)}, u32[]{:S(2)}) %collective-permute-start.29) | collective-permute-done | bytes 655392 | tf_op jit(solution)/shard_map/ppermute | solution.py:436
  297.7 11.4 %mlp_grads_low_kept.1 = (bf16[256,4224]{1,0:T(8,128)(2,1)}, bf16[256,4224]{1,0:T(8,128)(2,1)}) custom-call(s32[4]{0:T(128)S(1)} %get-tuple-element.653.places, bf16[160,2048]{1,0:T(8,128)(2,1)S(1)} %copy-done.2, bf16[160,2048]{1,0:T(8,128)(2,1)} %collective-permute-done.8.refs_1_, bf16[160,2048]{1,0:T(8,128)(2,1)} %collective-permute-done.12.refs_2_, ...), custom_call_target="tpu_custom_call" | custom-call | tf_op jit(solution)/shard_map/mlp_grads_low_kept/pallas_call | solution.py:644
  318.7 11.4 %mlp_grads_high_kept.1 = (bf16[256,4224]{1,0:T(8,128)(2,1)}, bf16[256,4224]{1,0:T(8,128)(2,1)}) custom-call(s32[4]{0:T(128)S(1)} %get-tuple-element.651.places, bf16[160,2048]{1,0:T(8,128)(2,1)S(1)} %copy-done.2, bf16[160,2048]{1,0:T(8,128)(2,1)} %collective-permute-done.8.refs_1_, bf16[160,2048]{1,0:T(8,128)(2,1)} %collective-permute-done.12.refs_2_, ...), custom_call_target="tpu_custom_call" | custom-call | tf_op jit(solution)/shard_map/mlp_grads_high_kept/pallas_call | solution.py:644
  333.2 11.8 %attention_backward.1 = (bf16[640,1024]{1,0:T(8,128)(2,1)}, bf16[5120,256]{1,0:T(8,128)(2,1)}, bf16[5120,256]{1,0:T(8,128)(2,1)}) custom-call(s32[1]{0:T(128)} %bitcast.group, bf16[640,1024]{1,0:T(8,128)(2,1)} %convolution_convert_fusion.2.query, bf16[640,1024]{1,0:T(8,128)(2,1)} %constant_dynamic-update-slice_fusion.20.grad, ...), custom_call_target="tpu_custom_call" | custom-call | flops 13421772800 | bytes 5242880 | tf_op jit(solution)/shard_map/attention_backward/pallas_call | solution.py:257
  345.0 12.2 %collective-permute-done.34.got = bf16[256,4224]{1,0:T(8,128)(2,1)} collective-permute-done((bf16[256,4224]{1,0:T(8,128)(2,1)}, bf16[256,4224]{1,0:T(8,128)(2,1)}, u32[]{:S(2)}, u32[]{:S(2)}) %collective-permute-start.34) | collective-permute-done | bytes 2162720 | tf_op jit(solution)/shard_map/ppermute | solution.py:499
  357.2 5.1 fusion.48
  368.0 9.7 %collective-permute-done.36.got = bf16[256,4224]{1,0:T(8,128)(2,1)} collective-permute-done((bf16[256,4224]{1,0:T(8,128)(2,1)}, bf16[256,4224]{1,0:T(8,128)(2,1)}, u32[]{:S(2)}, u32[]{:S(2)}) %collective-permute-start.36) | collective-permute-done | bytes 2162720 | tf_op jit(solution)/shard_map/ppermute | solution.py:499
  406.9 5.0 convolution_convert_fusion
  411.9 11.3 %collective-permute-done.37.got = bf16[1280,256]{1,0:T(8,128)(2,1)} collective-permute-done((bf16[1280,256]{1,0:T(8,128)(2,1)}, bf16[1280,256]{1,0:T(8,128)(2,1)}, u32[]{:S(2)}, u32[]{:S(2)}) %collective-permute-start.37) | collective-permute-done | bytes 655392 | tf_op jit(solution)/shard_map/ppermute | solution.py:499
  456.3 14.6 %collective-permute-done.46 = bf16[160,512]{1,0:T(8,128)(2,1)S(1)} collective-permute-done((bf16[160,512]{1,0:T(8,128)(2,1)S(1)}, bf16[160,512]{1,0:T(8,128)(2,1)S(1)}, u32[]{:S(2)}, u32[]{:S(2)}) %collective-permute-start.46) | collective-permute-done | bytes 163872 | tf_op jit(solution)/shard_map/ppermute | solution.py:436
  476.5 4.8 result.1
  486.8 16.0 %collective-permute-done.53.refs_2_ = bf16[128,4224]{1,0:T(8,128)(2,1)} collective-permute-done((bf16[128,4224]{1,0:T(8,128)(2,1)}, bf16[128,4224]{1,0:T(8,128)(2,1)}, u32[]{:S(2)}, u32[]{:S(2)}) %collective-permute-start.53) | collective-permute-done | bytes 1081376 | tf_op jit(solution)/shard_map/ppermute | solution.py:499
  540.6 31.2 %collective-permute-done.64 = bf16[64,512]{1,0:T(8,128)(2,1)S(1)} collective-permute-done((bf16[64,512]{1,0:T(8,128)(2,1)S(1)}, bf16[64,512]{1,0:T(8,128)(2,1)S(1)}, u32[]{:S(2)}, u32[]{:S(2)}) %collective-permute-start.64) | collective-permute-done | bytes 65568 | tf_op jit(solution)/shard_map/ppermute | solution.py:499
  580.4 23.7 %all-reduce.3.cloned.1.call-done = (bf16[1024,2048]{1,0:T(8,128)(2,1)}, bf16[1024,1024]{1,0:T(8,128)(2,1)}) async-done(((bf16[1024,2048]{1,0:T(8,128)(2,1)}, bf16[1024,1024]{1,0:T(8,128)(2,1)}), (bf16[1024,2048]{1,0:T(8,128)(2,1)}, bf16[1024,1024]{1,0:T(8,128)(2,1)})) %all-reduce.3.cloned.1.call-update) | async-done | bytes 6291472 | tf_op jit(solution)/shard_map/psum | solution.py:1140
  628.2 4.4 convert_element_type.352
  634.3 4.5 query_down_key_value_laid.1
  639.5 17.4 %mlp_grads_laid.1 = (f32[1408,2048]{1,0:T(8,128)}, f32[2048,1408]{1,0:T(8,128)}, f32[2048,1408]{1,0:T(8,128)}) custom-call(s32[16]{0:T(128)S(1)} %get-tuple-element.660.places, bf16[512,4224]{1,0:T(8,128)(2,1)} %join.4.refs_0_, bf16[512,4224]{1,0:T(8,128)(2,1)} %collective-permute-done.68.refs_1_, bf16[512,4224]{1,0:T(8,128)(2,1)} %join.5.refs_2_, ...), custom_call_target="tpu_custom_call" | custom-call | tf_op jit(solution)/shard_map/mlp_grads_laid/pallas_call | solution.py:795
  (488 shorter events, 309.9 us)
Async XLA Ops:
  8.0 440.7 %reduce-scatter.3.cloned.1.call-start = ((), (), s32[]{:S(2)}) async-start(), calls=%async_computation.2 | async-start | bytes 1638400 | tf_op jit(solution)/shard_map/reduce_scatter | solution.py:1135
  16.6 20.3 %collective-permute-start = (bf16[160,1024]{1,0:T(8,128)(2,1)}, bf16[160,1024]{1,0:T(8,128)(2,1)S(1)}, u32[]{:S(2)}, u32[]{:S(2)}) collective-permute-start(bf16[160,1024]{1,0:T(8,128)(2,1)} %get-tuple-element.658), channel_id=1, source_target_pairs={{0,1},{1,3},{3,2},{2,0},{4,5},{5,7},{7,6},{6,4},{8,9},{9,11},{11,1... | collective-permute-start | bytes 983048 | tf_op jit(solution)/shard_map/ppermute | solution.py:436
  87.3 29.1 %collective-permute-start.16 = (bf16[160,2048]{1,0:T(8,128)(2,1)}, bf16[160,2048]{1,0:T(8,128)(2,1)S(1)}, u32[]{:S(2)}, u32[]{:S(2)}) collective-permute-start(bf16[160,2048]{1,0:T(8,128)(2,1)} %collective-permute-done.12.refs_2_), channel_id=1, source_target_pairs={{0,1},{1,3},{3,2},{2,0},{4,5},{5,7},{7,6},{6,4},{8,9},{9,11},{11,1... | collective-permute-start | bytes 1966088 | tf_op jit(solution)/shard_map/ppermute | solution.py:436
  94.5 20.9 %collective-permute-start.17 = (bf16[160,512]{1,0:T(8,128)(2,1)S(1)}, bf16[160,512]{1,0:T(8,128)(2,1)S(1)}, u32[]{:S(2)}, u32[]{:S(2)}) collective-permute-start(bf16[160,512]{1,0:T(8,128)(2,1)S(1)} %get-tuple-element.635), channel_id=1, source_target_pairs={{0,1},{1,3},{3,2},{2,0},{4,5},{5,7},{7,6},{6,4},{8,9},{9,11},{11,1... | collective-permute-start | bytes 491528 | tf_op jit(solution)/shard_map/ppermute | solution.py:968
  166.5 20.0 %collective-permute-start.23 = (bf16[160,2048]{1,0:T(8,128)(2,1)S(1)}, bf16[160,2048]{1,0:T(8,128)(2,1)S(1)}, u32[]{:S(2)}, u32[]{:S(2)}) collective-permute-start(bf16[160,2048]{1,0:T(8,128)(2,1)S(1)} %multiply_convert_fusion.refs_8_), channel_id=1, source_target_pairs={{0,1},{1,3},{3,2},{2,0},{4,5},{5,7},{7,6},{6,4},{8,9},{9,11},{11,1... | collective-permute-start | bytes 1966088 | tf_op jit(solution)/shard_map/ppermute | solution.py:436
  196.1 23.3 %collective-permute-start.26 = (bf16[160,2048]{1,0:T(8,128)(2,1)S(1)}, bf16[160,2048]{1,0:T(8,128)(2,1)S(1)}, u32[]{:S(2)}, u32[]{:S(2)}) collective-permute-start(bf16[160,2048]{1,0:T(8,128)(2,1)S(1)} %fusion.9), channel_id=1, source_target_pairs={{0,1},{1,3},{3,2},{2,0},{4,5},{5,7},{7,6},{6,4},{8,9},{9,11},{11,1... | collective-permute-start | bytes 1966088 | tf_op jit(solution)/shard_map/ppermute | solution.py:436
  205.4 23.6 %collective-permute-start.25 = (bf16[160,2048]{1,0:T(8,128)(2,1)S(1)}, bf16[160,2048]{1,0:T(8,128)(2,1)S(1)}, u32[]{:S(2)}, u32[]{:S(2)}) collective-permute-start(bf16[160,2048]{1,0:T(8,128)(2,1)S(1)} %collective-permute-done.24.refs_10_), channel_id=1, source_target_pairs={{0,1},{1,3},{3,2},{2,0},{4,5},{5,7},{7,6},{6,4},{8,9},{9,11},{11,1... | collective-permute-start | bytes 1966088 | tf_op jit(solution)/shard_map/ppermute | solution.py:436
  219.6 23.0 %collective-permute-start.27 = (bf16[160,2048]{1,0:T(8,128)(2,1)S(1)}, bf16[160,2048]{1,0:T(8,128)(2,1)S(1)}, u32[]{:S(2)}, u32[]{:S(2)}) collective-permute-start(bf16[160,2048]{1,0:T(8,128)(2,1)S(1)} %add_convert_fusion.3), channel_id=1, source_target_pairs={{0,1},{1,3},{3,2},{2,0},{4,5},{5,7},{7,6},{6,4},{8,9},{9,11},{11,1... | collective-permute-start | bytes 1966088 | tf_op jit(solution)/shard_map/ppermute | solution.py:436
  265.0 32.7 %collective-permute-start.31 = (bf16[512,4224]{1,0:T(8,128)(2,1)}, bf16[512,4224]{1,0:T(8,128)(2,1)}, u32[]{:S(2)}, u32[]{:S(2)}) collective-permute-start(bf16[512,4224]{1,0:T(8,128)(2,1)} %mlp_grads_low_sent.1), channel_id=1, source_target_pairs={{0,4},{4,0},{8,12},{12,8},{16,20},{20,16},{24,28},{28,24},{1,5},{5... | collective-permute-start | bytes 12976136 | tf_op jit(solution)/shard_map/ppermute | solution.py:499
  274.3 44.4 %collective-permute-start.33 = (bf16[512,4224]{1,0:T(8,128)(2,1)}, bf16[512,4224]{1,0:T(8,128)(2,1)}, u32[]{:S(2)}, u32[]{:S(2)}) collective-permute-start(bf16[512,4224]{1,0:T(8,128)(2,1)} %mlp_grads_high_sent.1), channel_id=1, source_target_pairs={{0,4},{4,0},{8,12},{12,8},{16,20},{20,16},{24,28},{28,24},{1,5},{5... | collective-permute-start | bytes 12976136 | tf_op jit(solution)/shard_map/ppermute | solution.py:499
  309.0 48.2 %collective-permute-start.34 = (bf16[256,4224]{1,0:T(8,128)(2,1)}, bf16[256,4224]{1,0:T(8,128)(2,1)}, u32[]{:S(2)}, u32[]{:S(2)}) collective-permute-start(bf16[256,4224]{1,0:T(8,128)(2,1)} %get-tuple-element.429), channel_id=1, source_target_pairs={{0,8},{4,12},{8,0},{12,4},{16,24},{20,28},{24,16},{28,20},{1,9},{5... | collective-permute-start | bytes 6488072 | tf_op jit(solution)/shard_map/ppermute | solution.py:499
  310.7 20.2 %collective-permute-start.32 = (bf16[160,2048]{1,0:T(8,128)(2,1)S(1)}, bf16[160,2048]{1,0:T(8,128)(2,1)S(1)}, u32[]{:S(2)}, u32[]{:S(2)}) collective-permute-start(bf16[160,2048]{1,0:T(8,128)(2,1)S(1)} %collective-permute-done.30.refs_0_), channel_id=1, source_target_pairs={{0,1},{1,3},{3,2},{2,0},{4,5},{5,7},{7,6},{6,4},{8,9},{9,11},{11,1... | collective-permute-start | bytes 1966088 | tf_op jit(solution)/shard_map/ppermute | solution.py:436
  330.1 47.6 %collective-permute-start.36 = (bf16[256,4224]{1,0:T(8,128)(2,1)}, bf16[256,4224]{1,0:T(8,128)(2,1)}, u32[]{:S(2)}, u32[]{:S(2)}) collective-permute-start(bf16[256,4224]{1,0:T(8,128)(2,1)} %get-tuple-element.454), channel_id=1, source_target_pairs={{0,16},{4,20},{8,24},{12,28},{16,0},{20,4},{24,8},{28,12},{1,17},{... | collective-permute-start | bytes 6488072 | tf_op jit(solution)/shard_map/ppermute | solution.py:499
  362.3 24.7 %collective-permute-start.35 = (bf16[2560,256]{1,0:T(8,128)(2,1)}, bf16[2560,256]{1,0:T(8,128)(2,1)}, u32[]{:S(2)}, u32[]{:S(2)}) collective-permute-start(bf16[2560,256]{1,0:T(8,128)(2,1)} %get-tuple-element.662), channel_id=1, source_target_pairs={{0,4},{4,0},{8,12},{12,8},{16,20},{20,16},{24,28},{28,24},{1,5},{5... | collective-permute-start | bytes 3932168 | tf_op jit(solution)/shard_map/ppermute | solution.py:499
  362.4 30.7 %collective-permute-start.38 = (bf16[2560,256]{1,0:T(8,128)(2,1)}, bf16[2560,256]{1,0:T(8,128)(2,1)}, u32[]{:S(2)}, u32[]{:S(2)}) collective-permute-start(bf16[2560,256]{1,0:T(8,128)(2,1)} %get-tuple-element.614), channel_id=1, source_target_pairs={{0,4},{4,0},{8,12},{12,8},{16,20},{20,16},{24,28},{28,24},{1,5},{5... | collective-permute-start | bytes 3932168 | tf_op jit(solution)/shard_map/ppermute | solution.py:499
  385.5 127.0 %all-gather.2.cloned.1.call-start = ((), (), s32[]{:S(2)}) async-start(), calls=%async_computation.3 | async-start | bytes 1638400 | tf_op jit(solution)/shard_map/all_gather | solution.py:1151
  385.6 51.9 %collective-permute-start.40 = (bf16[128,4224]{1,0:T(8,128)(2,1)}, bf16[128,4224]{1,0:T(8,128)(2,1)}, u32[]{:S(2)}, u32[]{:S(2)}) collective-permute-start(bf16[128,4224]{1,0:T(8,128)(2,1)} %copy-done.48), channel_id=1, source_target_pairs={{0,8},{4,12},{8,0},{12,4},{16,24},{20,28},{24,16},{28,20},{1,9},{5... | collective-permute-start | bytes 3244040 | tf_op jit(solution)/shard_map/ppermute | solution.py:499
  386.0 48.2 %collective-permute-start.41 = (bf16[128,4224]{1,0:T(8,128)(2,1)}, bf16[128,4224]{1,0:T(8,128)(2,1)}, u32[]{:S(2)}, u32[]{:S(2)}) collective-permute-start(bf16[128,4224]{1,0:T(8,128)(2,1)} %copy-done.47), channel_id=1, source_target_pairs={{0,16},{4,20},{8,24},{12,28},{16,0},{20,4},{24,8},{28,12},{1,17},{... | collective-permute-start | bytes 3244040 | tf_op jit(solution)/shard_map/ppermute | solution.py:499
  392.3 30.9 %collective-permute-start.37 = (bf16[1280,256]{1,0:T(8,128)(2,1)}, bf16[1280,256]{1,0:T(8,128)(2,1)}, u32[]{:S(2)}, u32[]{:S(2)}) collective-permute-start(bf16[1280,256]{1,0:T(8,128)(2,1)} %get-tuple-element.479), channel_id=1, source_target_pairs={{0,8},{4,12},{8,0},{12,4},{16,24},{20,28},{24,16},{28,20},{1,9},{5... | collective-permute-start | bytes 1966088 | tf_op jit(solution)/shard_map/ppermute | solution.py:499
  396.8 32.3 %collective-permute-start.42 = (bf16[1280,256]{1,0:T(8,128)(2,1)}, bf16[1280,256]{1,0:T(8,128)(2,1)}, u32[]{:S(2)}, u32[]{:S(2)}) collective-permute-start(bf16[1280,256]{1,0:T(8,128)(2,1)} %get-tuple-element.483), channel_id=1, source_target_pairs={{0,16},{4,20},{8,24},{12,28},{16,0},{20,4},{24,8},{28,12},{1,17},{... | collective-permute-start | bytes 1966088 | tf_op jit(solution)/shard_map/ppermute | solution.py:499
  448.8 155.3 %all-reduce.3.cloned.1.call-start = ((), (), s32[]{:S(2)}) async-start(), calls=%async_computation.5 | async-start | bytes 12582912 | tf_op jit(solution)/shard_map/psum | solution.py:1140
  449.8 37.0 %collective-permute-start.48 = (bf16[128,4224]{1,0:T(8,128)(2,1)}, bf16[128,4224]{1,0:T(8,128)(2,1)}, u32[]{:S(2)}, u32[]{:S(2)}) collective-permute-start(bf16[128,4224]{1,0:T(8,128)(2,1)} %copy-done.23), channel_id=1, source_target_pairs={{0,8},{4,12},{8,0},{12,4},{16,24},{20,28},{24,16},{28,20},{1,9},{5... | collective-permute-start | bytes 3244040 | tf_op jit(solution)/shard_map/ppermute | solution.py:499
  451.3 35.5 %collective-permute-start.47 = (bf16[128,4224]{1,0:T(8,128)(2,1)}, bf16[128,4224]{1,0:T(8,128)(2,1)}, u32[]{:S(2)}, u32[]{:S(2)}) collective-permute-start(bf16[128,4224]{1,0:T(8,128)(2,1)} %copy-done.23), channel_id=1, source_target_pairs={{0,16},{4,20},{8,24},{12,28},{16,0},{20,4},{24,8},{28,12},{1,17},{... | collective-permute-start | bytes 3244040 | tf_op jit(solution)/shard_map/ppermute | solution.py:499
  451.6 51.2 %collective-permute-start.53 = (bf16[128,4224]{1,0:T(8,128)(2,1)}, bf16[128,4224]{1,0:T(8,128)(2,1)}, u32[]{:S(2)}, u32[]{:S(2)}) collective-permute-start(bf16[128,4224]{1,0:T(8,128)(2,1)} %copy-done.21), channel_id=1, source_target_pairs={{0,16},{4,20},{8,24},{12,28},{16,0},{20,4},{24,8},{28,12},{1,17},{... | collective-permute-start | bytes 3244040 | tf_op jit(solution)/shard_map/ppermute | solution.py:499
  453.4 49.5 %collective-permute-start.52 = (bf16[128,4224]{1,0:T(8,128)(2,1)}, bf16[128,4224]{1,0:T(8,128)(2,1)}, u32[]{:S(2)}, u32[]{:S(2)}) collective-permute-start(bf16[128,4224]{1,0:T(8,128)(2,1)} %copy-done.21), channel_id=1, source_target_pairs={{0,8},{4,12},{8,0},{12,4},{16,24},{20,28},{24,16},{28,20},{1,9},{5... | collective-permute-start | bytes 3244040 | tf_op jit(solution)/shard_map/ppermute | solution.py:499
  486.8 170.1 %reduce-scatter.5.cloned.1.call-start = ((), (), s32[]{:S(2)}) async-start(), calls=%async_computation.4 | async-start | bytes 3276800 | tf_op jit(solution)/shard_map/reduce_scatter | solution.py:1176
  536.2 73.0 %collective-permute-start.71 = (bf16[128,4224]{1,0:T(8,128)(2,1)}, bf16[128,4224]{1,0:T(8,128)(2,1)}, u32[]{:S(2)}, u32[]{:S(2)}) collective-permute-start(bf16[128,4224]{1,0:T(8,128)(2,1)} %collective-permute-done.52.refs_1_), channel_id=1, source_target_pairs={{0,16},{4,20},{8,24},{12,28},{16,0},{20,4},{24,8},{28,12},{1,17},{... | collective-permute-start | bytes 3244040 | tf_op jit(solution)/shard_map/ppermute | solution.py:499
  537.2 66.9 %collective-permute-start.50 = (bf16[128,4224]{1,0:T(8,128)(2,1)}, bf16[128,4224]{1,0:T(8,128)(2,1)}, u32[]{:S(2)}, u32[]{:S(2)}) collective-permute-start(bf16[128,4224]{1,0:T(8,128)(2,1)} %collective-permute-done.47.refs_1_), channel_id=1, source_target_pairs={{0,8},{4,12},{8,0},{12,4},{16,24},{20,28},{24,16},{28,20},{1,9},{5... | collective-permute-start | bytes 3244040 | tf_op jit(solution)/shard_map/ppermute | solution.py:499
  539.0 32.7 %collective-permute-start.64 = (bf16[64,512]{1,0:T(8,128)(2,1)S(1)}, bf16[64,512]{1,0:T(8,128)(2,1)S(1)}, u32[]{:S(2)}, u32[]{:S(2)}) collective-permute-start(bf16[64,512]{1,0:T(8,128)(2,1)S(1)} %get-tuple-element.646), channel_id=1, source_target_pairs={{0,16},{4,20},{8,24},{12,28},{16,0},{20,4},{24,8},{28,12},{1,17},{... | collective-permute-start | bytes 196616 | tf_op jit(solution)/shard_map/ppermute | solution.py:499
  540.4 32.8 %collective-permute-start.63 = (bf16[64,1024]{1,0:T(8,128)(2,1)S(1)}, bf16[64,1024]{1,0:T(8,128)(2,1)S(1)}, u32[]{:S(2)}, u32[]{:S(2)}) collective-permute-start(bf16[64,1024]{1,0:T(8,128)(2,1)S(1)} %get-tuple-element.640), channel_id=1, source_target_pairs={{0,8},{4,12},{8,0},{12,4},{16,24},{20,28},{24,16},{28,20},{1,9},{5... | collective-permute-start | bytes 393224 | tf_op jit(solution)/shard_map/ppermute | solution.py:499
  609.2 30.3 %collective-permute-start.68 = (bf16[512,4224]{1,0:T(8,128)(2,1)}, bf16[512,4224]{1,0:T(8,128)(2,1)}, u32[]{:S(2)}, u32[]{:S(2)}) collective-permute-start(bf16[512,4224]{1,0:T(8,128)(2,1)} %join.4.refs_0_), channel_id=1, source_target_pairs={{0,4},{4,0},{8,12},{12,8},{16,20},{20,16},{24,28},{28,24},{1,5},{5... | collective-permute-start | bytes 12976136 | tf_op jit(solution)/shard_map/ppermute | solution.py:499
  612.8 26.7 %collective-permute-start.74 = (bf16[512,4224]{1,0:T(8,128)(2,1)}, bf16[512,4224]{1,0:T(8,128)(2,1)}, u32[]{:S(2)}, u32[]{:S(2)}) collective-permute-start(bf16[512,4224]{1,0:T(8,128)(2,1)} %join.5.refs_2_), channel_id=1, source_target_pairs={{0,4},{4,0},{8,12},{12,8},{16,20},{20,16},{24,28},{28,24},{1,5},{5... | collective-permute-start | bytes 12976136 | tf_op jit(solution)/shard_map/ppermute | solution.py:499
  (149 other events, 1842.8 us)
Sparse Core Ops, SparseCore 0:
  385.6 28.9 reduce-scatter.2
  448.9 37.9 all-gather.1
  539.1 50.0 reduce-scatter.4
Sparse Core Ops, SparseCore 1:
  486.8 117.2 all-reduce.2

commit v4 on v3

--- a/solution.py
+++ b/solution.py
@@ -1200,14 +1200,6 @@
     while len(down_query.steps) > 2:
         steps(pair_weight, down_query)
         steps(gains)
-    out_sum, up_query_sum = order.take(out_sum, up_query_sum)
-    order.mark(out_sum, up_query_sum)
-    while len(mlp[0].steps) > 1:
-        steps(*mlp)
-    steps(pair_weight, down_query)
-    out_sum = order.take(out_sum).astype(jnp.float32)
-    up_query_sum = up_query_sum.astype(jnp.float32)
-    order.mark(out_sum, up_query_sum)
     finish(pair_weight, down_query)
     while gains.bits:
         steps(gains)
@@ -1219,6 +1211,13 @@
         "query_down_key_value_laid",
     )
     order.mark(down_query_sum)
+    out_sum, up_query_sum = order.take(out_sum, up_query_sum)
+    order.mark(out_sum, up_query_sum)
+    while len(mlp[0].steps) > 1:
+        steps(*mlp)
+    out_sum = order.take(out_sum).astype(jnp.float32)
+    up_query_sum = up_query_sum.astype(jnp.float32)
+    order.mark(out_sum, up_query_sum)
     finish(*mlp)
     down_sum, gate_sum, up_sum = unfold(
         mlp, [(down_weight.shape[0], True)] + [(gate_weight.shape[1], False)] * 2, "mlp_grads_laid"

time: 674 us -> 692 us (1.027)
  waiting for transfers between devices: 283 us -> 297 us
    psum x1, waiting for transfers between devices: 23.7 us -> 38 us  [shards(): out_sum, up_query_sum = lax.psum((out_part, up_query_part), 'dp')]
    unnamed x206 -> x208, local copies, waits for them, and re-layouts: 27.3 us -> 31.6 us
  transfers between devices with their start and end apart: 81 -> 81, of which waited for: 40 -> 41; matrix products, arithmetic and copies ran while one was open for 14% -> 14% of each run, Pallas kernels for 18% -> 17%
where the time goes in v4:
time: 692 us; the launch traced here: 685 us
  waiting for transfers between devices  297 us (43%)
  Pallas kernels  127 us (18%)
  starting transfers between devices  100 us (14%)
  local copies, waits for them, and re-layouts  57.9 us (8%)
  matrix products  57.9 us (8%)
  other arithmetic  24 us (3%)
  between operations  20.8 us (3%)
    ppermute x27, waiting for transfers between devices, ring_pass(): return lax.ppermute(array, 'mp', pairs)  141 us
    ppermute x40, waiting for transfers between devices, trade(): return lax.ppermute(array, 'dp', [(i, i ^ 1 << bit) for i in range(count)])  103 us
    ppermute x27, starting transfers between devices, ring_pass(): return lax.ppermute(array, 'mp', pairs)  53 us
    pallas_call x4, Pallas kernels, product_blocks(): pl.pallas_call(functools.partial(product_kernel, tuple(groups), split), g...  40.1 us
    psum x1, waiting for transfers between devices, shards(): out_sum, up_query_sum = lax.psum((out_part, up_query_part), 'dp')  38 us
    ppermute x40, starting transfers between devices, trade(): return lax.ppermute(array, 'dp', [(i, i ^ 1 << bit) for i in range(count)])  35.3 us
    unnamed x208, local copies, waits for them, and re-layouts  31.6 us
    dot_general x12, matrix products, dotf(): return jnp.dot(left, right, preferred_element_type=jnp.float32)  23 us
  transfers between devices with their start and end apart: 81, of which 41 were waited for; matrix products, arithmetic and copies ran while one was open for 14% of the time, Pallas kernels for 17%

profile of v4, /device:TPU:0, one launch (start us, length us, event | category | flops | bytes accessed | tf_op | source)
XLA Modules:
  0.0 684.7 jit_solution(18264861729545766198)
XLA Ops:
  22.2 9.9 %collective-permute-done.1 = bf16[160,512]{1,0:T(8,128)(2,1)S(1)} collective-permute-done((bf16[160,512]{1,0:T(8,128)(2,1)S(1)}, bf16[160,512]{1,0:T(8,128)(2,1)S(1)}, u32[]{:S(2)}, u32[]{:S(2)}) %collective-permute-start.1) | collective-permute-done | bytes 163872 | tf_op jit(solution)/shard_map/ppermute | solution.py:436
  41.1 7.3 %collective-permute-done.2 = bf16[160,1024]{1,0:T(8,128)(2,1)S(1)} collective-permute-done((bf16[160,1024]{1,0:T(8,128)(2,1)S(1)}, bf16[160,1024]{1,0:T(8,128)(2,1)S(1)}, u32[]{:S(2)}, u32[]{:S(2)}) %collective-permute-start.2) | collective-permute-done | bytes 327712 | tf_op jit(solution)/shard_map/ppermute | solution.py:436
  94.4 8.9 %attention_forward.1 = (bf16[640,1024]{1,0:T(8,128)(2,1)}, f32[256,2560]{1,0:T(8,128)}, f32[1,2560]{1,0:T(1,128)S(1)}) custom-call(s32[1]{0:T(128)} %bitcast.group, bf16[640,1024]{1,0:T(8,128)(2,1)} %convolution_convert_fusion.2.query, bf16[1280,256]{1,0:T(8,128)(2,1)S(1)} %constant_dynamic-update-slice_fusion.refs_0_, ...), custom_call_target="tpu_custom_call" | custom-call | flops 13421772800 | bytes 5242880 | tf_op jit(solution)/shard_map/attention_forward/pallas_call | solution.py:231
  109.8 5.4 collective-permute-done.17
  120.0 7.8 %fusion = f32[640,1408]{1,0:T(8,128)} fusion(bf16[1408,2048]{1,0:T(8,128)(2,1)S(1)} %bitcast.62, bf16[160,2048]{1,0:T(8,128)(2,1)} %copy-done.60, bf16[160,2048]{1,0:T(8,128)(2,1)} %collective-permute-done.12.refs_2_, bf16[160,2048]{1,0:T(8,128)(2,1)} %collective-permute-done.8.refs_1_, bf16[160,2048]{1,0:T(8,128)(2,1)S(1)} %copy-done.2), kind=kOutput, calls=%fused_computation.2 | convolution fusion | flops 3701473280 | bytes 11993088 | tf_op jit(solution)/shard_map/td,fd->tf/dot_general | solution.py:1051
  127.8 6.6 collective-permute-done.20
  136.0 13.4 %collective-permute-done.21 = bf16[160,2048]{1,0:T(8,128)(2,1)S(1)} collective-permute-done((bf16[160,2048]{1,0:T(8,128)(2,1)S(1)}, bf16[160,2048]{1,0:T(8,128)(2,1)S(1)}, u32[]{:S(2)}, u32[]{:S(2)}) %collective-permute-start.21) | collective-permute-done | bytes 655392 | tf_op jit(solution)/shard_map/ppermute | solution.py:436
  153.0 13.2 %collective-permute-done.22 = bf16[160,2048]{1,0:T(8,128)(2,1)S(1)} collective-permute-done((bf16[160,2048]{1,0:T(8,128)(2,1)S(1)}, bf16[160,2048]{1,0:T(8,128)(2,1)S(1)}, u32[]{:S(2)}, u32[]{:S(2)}) %collective-permute-start.22) | collective-permute-done | bytes 655392 | tf_op jit(solution)/shard_map/ppermute | solution.py:436
  178.1 8.8 %collective-permute-done.23.refs_9_ = bf16[160,2048]{1,0:T(8,128)(2,1)S(1)} collective-permute-done((bf16[160,2048]{1,0:T(8,128)(2,1)S(1)}, bf16[160,2048]{1,0:T(8,128)(2,1)S(1)}, u32[]{:S(2)}, u32[]{:S(2)}) %collective-permute-start.23) | collective-permute-done | bytes 655392 | tf_op jit(solution)/shard_map/ppermute | solution.py:436
  199.9 5.7 collective-permute-done.24.refs_10_
  222.4 6.7 collective-permute-done.25.refs_11_
  237.2 5.6 collective-permute-done.27
  245.8 9.2 %collective-permute-done.28 = bf16[160,2048]{1,0:T(8,128)(2,1)S(1)} collective-permute-done((bf16[160,2048]{1,0:T(8,128)(2,1)S(1)}, bf16[160,2048]{1,0:T(8,128)(2,1)S(1)}, u32[]{:S(2)}, u32[]{:S(2)}) %collective-permute-start.28) | collective-permute-done | bytes 655392 | tf_op jit(solution)/shard_map/ppermute | solution.py:436
  256.6 8.7 %mlp_grads_low_sent.1 = bf16[512,4224]{1,0:T(8,128)(2,1)} custom-call(s32[4]{0:T(128)S(1)} %get-tuple-element.654.places, bf16[160,2048]{1,0:T(8,128)(2,1)S(1)} %copy-done.2, bf16[160,2048]{1,0:T(8,128)(2,1)} %collective-permute-done.8.refs_1_, bf16[160,2048]{1,0:T(8,128)(2,1)} %collective-permute-done.12.refs_2_, bf16[160,2048]{1,0:T(8,128)(2,1)} %copy-done.60, ...), custom_call_target="tpu_custom_call" | custom-call | tf_op jit(solution)/shard_map/mlp_grads_low_sent/pallas_call | solution.py:644
  266.0 8.7 %mlp_grads_high_sent.1 = bf16[512,4224]{1,0:T(8,128)(2,1)} custom-call(s32[4]{0:T(128)S(1)} %get-tuple-element.652.places, bf16[160,2048]{1,0:T(8,128)(2,1)S(1)} %copy-done.2, bf16[160,2048]{1,0:T(8,128)(2,1)} %collective-permute-done.8.refs_1_, bf16[160,2048]{1,0:T(8,128)(2,1)} %collective-permute-done.12.refs_2_, bf16[160,2048]{1,0:T(8,128)(2,1)} %copy-done.60, ...), custom_call_target="tpu_custom_call" | custom-call | tf_op jit(solution)/shard_map/mlp_grads_high_sent/pallas_call | solution.py:644
  277.5 15.4 %collective-permute-done.29.refs_0_ = bf16[160,2048]{1,0:T(8,128)(2,1)S(1)} collective-permute-done((bf16[160,2048]{1,0:T(8,128)(2,1)S(1)}, bf16[160,2048]{1,0:T(8,128)(2,1)S(1)}, u32[]{:S(2)}, u32[]{:S(2)}) %collective-permute-start.29) | collective-permute-done | bytes 655392 | tf_op jit(solution)/shard_map/ppermute | solution.py:436
  298.1 11.3 %mlp_grads_low_kept.1 = (bf16[256,4224]{1,0:T(8,128)(2,1)}, bf16[256,4224]{1,0:T(8,128)(2,1)}) custom-call(s32[4]{0:T(128)S(1)} %get-tuple-element.653.places, bf16[160,2048]{1,0:T(8,128)(2,1)S(1)} %copy-done.2, bf16[160,2048]{1,0:T(8,128)(2,1)} %collective-permute-done.8.refs_1_, bf16[160,2048]{1,0:T(8,128)(2,1)} %collective-permute-done.12.refs_2_, ...), custom_call_target="tpu_custom_call" | custom-call | tf_op jit(solution)/shard_map/mlp_grads_low_kept/pallas_call | solution.py:644
  318.6 11.3 %mlp_grads_high_kept.1 = (bf16[256,4224]{1,0:T(8,128)(2,1)}, bf16[256,4224]{1,0:T(8,128)(2,1)}) custom-call(s32[4]{0:T(128)S(1)} %get-tuple-element.651.places, bf16[160,2048]{1,0:T(8,128)(2,1)S(1)} %copy-done.2, bf16[160,2048]{1,0:T(8,128)(2,1)} %collective-permute-done.8.refs_1_, bf16[160,2048]{1,0:T(8,128)(2,1)} %collective-permute-done.12.refs_2_, ...), custom_call_target="tpu_custom_call" | custom-call | tf_op jit(solution)/shard_map/mlp_grads_high_kept/pallas_call | solution.py:644
  333.0 12.1 %attention_backward.1 = (bf16[640,1024]{1,0:T(8,128)(2,1)}, bf16[5120,256]{1,0:T(8,128)(2,1)}, bf16[5120,256]{1,0:T(8,128)(2,1)}) custom-call(s32[1]{0:T(128)} %bitcast.group, bf16[640,1024]{1,0:T(8,128)(2,1)} %convolution_convert_fusion.2.query, bf16[640,1024]{1,0:T(8,128)(2,1)} %constant_dynamic-update-slice_fusion.20.grad, ...), custom_call_target="tpu_custom_call" | custom-call | flops 13421772800 | bytes 5242880 | tf_op jit(solution)/shard_map/attention_backward/pallas_call | solution.py:257
  345.1 12.6 %collective-permute-done.34.got = bf16[256,4224]{1,0:T(8,128)(2,1)} collective-permute-done((bf16[256,4224]{1,0:T(8,128)(2,1)}, bf16[256,4224]{1,0:T(8,128)(2,1)}, u32[]{:S(2)}, u32[]{:S(2)}) %collective-permute-start.34) | collective-permute-done | bytes 2162720 | tf_op jit(solution)/shard_map/ppermute | solution.py:499
  357.6 5.1 fusion.48
  368.4 9.2 %collective-permute-done.36.got = bf16[256,4224]{1,0:T(8,128)(2,1)} collective-permute-done((bf16[256,4224]{1,0:T(8,128)(2,1)}, bf16[256,4224]{1,0:T(8,128)(2,1)}, u32[]{:S(2)}, u32[]{:S(2)}) %collective-permute-start.36) | collective-permute-done | bytes 2162720 | tf_op jit(solution)/shard_map/ppermute | solution.py:499
  406.7 5.0 convolution_convert_fusion
  411.7 11.3 %collective-permute-done.37.got = bf16[1280,256]{1,0:T(8,128)(2,1)} collective-permute-done((bf16[1280,256]{1,0:T(8,128)(2,1)}, bf16[1280,256]{1,0:T(8,128)(2,1)}, u32[]{:S(2)}, u32[]{:S(2)}) %collective-permute-start.37) | collective-permute-done | bytes 655392 | tf_op jit(solution)/shard_map/ppermute | solution.py:499
  443.6 4.8 collective-permute-done.44
  456.0 13.9 %collective-permute-done.46 = bf16[160,512]{1,0:T(8,128)(2,1)S(1)} collective-permute-done((bf16[160,512]{1,0:T(8,128)(2,1)S(1)}, bf16[160,512]{1,0:T(8,128)(2,1)S(1)}, u32[]{:S(2)}, u32[]{:S(2)}) %collective-permute-start.46) | collective-permute-done | bytes 163872 | tf_op jit(solution)/shard_map/ppermute | solution.py:436
  476.2 4.8 result.1
  485.6 11.8 %collective-permute-done.53.refs_2_ = bf16[128,4224]{1,0:T(8,128)(2,1)} collective-permute-done((bf16[128,4224]{1,0:T(8,128)(2,1)}, bf16[128,4224]{1,0:T(8,128)(2,1)}, u32[]{:S(2)}, u32[]{:S(2)}) %collective-permute-start.53) | collective-permute-done | bytes 1081376 | tf_op jit(solution)/shard_map/ppermute | solution.py:499
  537.7 36.3 %collective-permute-done.60 = bf16[64,512]{1,0:T(8,128)(2,1)S(1)} collective-permute-done((bf16[64,512]{1,0:T(8,128)(2,1)S(1)}, bf16[64,512]{1,0:T(8,128)(2,1)S(1)}, u32[]{:S(2)}, u32[]{:S(2)}) %collective-permute-start.60) | collective-permute-done | bytes 65568 | tf_op jit(solution)/shard_map/ppermute | solution.py:499
  592.1 4.7 query_down_key_value_laid.1
  596.8 38.0 %all-reduce.3.cloned.1.call-done = (bf16[1024,2048]{1,0:T(8,128)(2,1)}, bf16[1024,1024]{1,0:T(8,128)(2,1)}) async-done(((bf16[1024,2048]{1,0:T(8,128)(2,1)}, bf16[1024,1024]{1,0:T(8,128)(2,1)}), (bf16[1024,2048]{1,0:T(8,128)(2,1)}, bf16[1024,1024]{1,0:T(8,128)(2,1)})) %all-reduce.3.cloned.1.call-update) | async-done | bytes 6291472 | tf_op jit(solution)/shard_map/psum | solution.py:1140
  658.3 16.6 %mlp_grads_laid.1 = (f32[1408,2048]{1,0:T(8,128)}, f32[2048,1408]{1,0:T(8,128)}, f32[2048,1408]{1,0:T(8,128)}) custom-call(s32[16]{0:T(128)S(1)} %get-tuple-element.660.places, bf16[512,4224]{1,0:T(8,128)(2,1)S(1)} %join.4.refs_0_, bf16[512,4224]{1,0:T(8,128)(2,1)} %copy-done.66, bf16[512,4224]{1,0:T(8,128)(2,1)} %copy-done.3, bf16[512,4224]{1,0:T(8,128)(2,1)} %copy-done.67), custom_call_target="tpu_custom_call" | custom-call | tf_op jit(solution)/shard_map/mlp_grads_laid/pallas_call | solution.py:795
  (490 shorter events, 313.6 us)
Async XLA Ops:
  8.0 441.1 %reduce-scatter.3.cloned.1.call-start = ((), (), s32[]{:S(2)}) async-start(), calls=%async_computation.2 | async-start | bytes 1638400 | tf_op jit(solution)/shard_map/reduce_scatter | solution.py:1135
  16.6 20.2 %collective-permute-start = (bf16[160,1024]{1,0:T(8,128)(2,1)}, bf16[160,1024]{1,0:T(8,128)(2,1)S(1)}, u32[]{:S(2)}, u32[]{:S(2)}) collective-permute-start(bf16[160,1024]{1,0:T(8,128)(2,1)} %get-tuple-element.658), channel_id=1, source_target_pairs={{0,1},{1,3},{3,2},{2,0},{4,5},{5,7},{7,6},{6,4},{8,9},{9,11},{11,1... | collective-permute-start | bytes 983048 | tf_op jit(solution)/shard_map/ppermute | solution.py:436
  87.2 29.1 %collective-permute-start.16 = (bf16[160,2048]{1,0:T(8,128)(2,1)}, bf16[160,2048]{1,0:T(8,128)(2,1)S(1)}, u32[]{:S(2)}, u32[]{:S(2)}) collective-permute-start(bf16[160,2048]{1,0:T(8,128)(2,1)} %collective-permute-done.12.refs_2_), channel_id=1, source_target_pairs={{0,1},{1,3},{3,2},{2,0},{4,5},{5,7},{7,6},{6,4},{8,9},{9,11},{11,1... | collective-permute-start | bytes 1966088 | tf_op jit(solution)/shard_map/ppermute | solution.py:436
  91.4 18.4 %collective-permute-start.18 = (bf16[160,512]{1,0:T(8,128)(2,1)S(1)}, bf16[160,512]{1,0:T(8,128)(2,1)S(1)}, u32[]{:S(2)}, u32[]{:S(2)}) collective-permute-start(bf16[160,512]{1,0:T(8,128)(2,1)S(1)} %get-tuple-element.634), channel_id=1, source_target_pairs={{0,3},{1,2},{3,0},{2,1},{4,7},{5,6},{7,4},{6,5},{8,11},{9,10},{11,... | collective-permute-start | bytes 491528 | tf_op jit(solution)/shard_map/ppermute | solution.py:968
  94.4 20.8 %collective-permute-start.17 = (bf16[160,512]{1,0:T(8,128)(2,1)S(1)}, bf16[160,512]{1,0:T(8,128)(2,1)S(1)}, u32[]{:S(2)}, u32[]{:S(2)}) collective-permute-start(bf16[160,512]{1,0:T(8,128)(2,1)S(1)} %get-tuple-element.635), channel_id=1, source_target_pairs={{0,1},{1,3},{3,2},{2,0},{4,5},{5,7},{7,6},{6,4},{8,9},{9,11},{11,1... | collective-permute-start | bytes 491528 | tf_op jit(solution)/shard_map/ppermute | solution.py:968
  167.2 19.7 %collective-permute-start.23 = (bf16[160,2048]{1,0:T(8,128)(2,1)S(1)}, bf16[160,2048]{1,0:T(8,128)(2,1)S(1)}, u32[]{:S(2)}, u32[]{:S(2)}) collective-permute-start(bf16[160,2048]{1,0:T(8,128)(2,1)S(1)} %multiply_convert_fusion.refs_8_), channel_id=1, source_target_pairs={{0,1},{1,3},{3,2},{2,0},{4,5},{5,7},{7,6},{6,4},{8,9},{9,11},{11,1... | collective-permute-start | bytes 1966088 | tf_op jit(solution)/shard_map/ppermute | solution.py:436
  186.8 18.8 %collective-permute-start.24 = (bf16[160,2048]{1,0:T(8,128)(2,1)S(1)}, bf16[160,2048]{1,0:T(8,128)(2,1)S(1)}, u32[]{:S(2)}, u32[]{:S(2)}) collective-permute-start(bf16[160,2048]{1,0:T(8,128)(2,1)S(1)} %collective-permute-done.23.refs_9_), channel_id=1, source_target_pairs={{0,1},{1,3},{3,2},{2,0},{4,5},{5,7},{7,6},{6,4},{8,9},{9,11},{11,1... | collective-permute-start | bytes 1966088 | tf_op jit(solution)/shard_map/ppermute | solution.py:436
  196.4 23.2 %collective-permute-start.26 = (bf16[160,2048]{1,0:T(8,128)(2,1)S(1)}, bf16[160,2048]{1,0:T(8,128)(2,1)S(1)}, u32[]{:S(2)}, u32[]{:S(2)}) collective-permute-start(bf16[160,2048]{1,0:T(8,128)(2,1)S(1)} %fusion.9), channel_id=1, source_target_pairs={{0,1},{1,3},{3,2},{2,0},{4,5},{5,7},{7,6},{6,4},{8,9},{9,11},{11,1... | collective-permute-start | bytes 1966088 | tf_op jit(solution)/shard_map/ppermute | solution.py:436
  205.6 23.5 %collective-permute-start.25 = (bf16[160,2048]{1,0:T(8,128)(2,1)S(1)}, bf16[160,2048]{1,0:T(8,128)(2,1)S(1)}, u32[]{:S(2)}, u32[]{:S(2)}) collective-permute-start(bf16[160,2048]{1,0:T(8,128)(2,1)S(1)} %collective-permute-done.24.refs_10_), channel_id=1, source_target_pairs={{0,1},{1,3},{3,2},{2,0},{4,5},{5,7},{7,6},{6,4},{8,9},{9,11},{11,1... | collective-permute-start | bytes 1966088 | tf_op jit(solution)/shard_map/ppermute | solution.py:436
  219.9 23.0 %collective-permute-start.27 = (bf16[160,2048]{1,0:T(8,128)(2,1)S(1)}, bf16[160,2048]{1,0:T(8,128)(2,1)S(1)}, u32[]{:S(2)}, u32[]{:S(2)}) collective-permute-start(bf16[160,2048]{1,0:T(8,128)(2,1)S(1)} %add_convert_fusion.3), channel_id=1, source_target_pairs={{0,1},{1,3},{3,2},{2,0},{4,5},{5,7},{7,6},{6,4},{8,9},{9,11},{11,1... | collective-permute-start | bytes 1966088 | tf_op jit(solution)/shard_map/ppermute | solution.py:436
  265.4 32.7 %collective-permute-start.31 = (bf16[512,4224]{1,0:T(8,128)(2,1)}, bf16[512,4224]{1,0:T(8,128)(2,1)}, u32[]{:S(2)}, u32[]{:S(2)}) collective-permute-start(bf16[512,4224]{1,0:T(8,128)(2,1)} %mlp_grads_low_sent.1), channel_id=1, source_target_pairs={{0,4},{4,0},{8,12},{12,8},{16,20},{20,16},{24,28},{28,24},{1,5},{5... | collective-permute-start | bytes 12976136 | tf_op jit(solution)/shard_map/ppermute | solution.py:499
  274.8 43.8 %collective-permute-start.33 = (bf16[512,4224]{1,0:T(8,128)(2,1)}, bf16[512,4224]{1,0:T(8,128)(2,1)}, u32[]{:S(2)}, u32[]{:S(2)}) collective-permute-start(bf16[512,4224]{1,0:T(8,128)(2,1)} %mlp_grads_high_sent.1), channel_id=1, source_target_pairs={{0,4},{4,0},{8,12},{12,8},{16,20},{20,16},{24,28},{28,24},{1,5},{5... | collective-permute-start | bytes 12976136 | tf_op jit(solution)/shard_map/ppermute | solution.py:499
  309.4 48.2 %collective-permute-start.34 = (bf16[256,4224]{1,0:T(8,128)(2,1)}, bf16[256,4224]{1,0:T(8,128)(2,1)}, u32[]{:S(2)}, u32[]{:S(2)}) collective-permute-start(bf16[256,4224]{1,0:T(8,128)(2,1)} %get-tuple-element.429), channel_id=1, source_target_pairs={{0,8},{4,12},{8,0},{12,4},{16,24},{20,28},{24,16},{28,20},{1,9},{5... | collective-permute-start | bytes 6488072 | tf_op jit(solution)/shard_map/ppermute | solution.py:499
  310.7 20.0 %collective-permute-start.32 = (bf16[160,2048]{1,0:T(8,128)(2,1)S(1)}, bf16[160,2048]{1,0:T(8,128)(2,1)S(1)}, u32[]{:S(2)}, u32[]{:S(2)}) collective-permute-start(bf16[160,2048]{1,0:T(8,128)(2,1)S(1)} %collective-permute-done.30.refs_0_), channel_id=1, source_target_pairs={{0,1},{1,3},{3,2},{2,0},{4,5},{5,7},{7,6},{6,4},{8,9},{9,11},{11,1... | collective-permute-start | bytes 1966088 | tf_op jit(solution)/shard_map/ppermute | solution.py:436
  329.9 47.6 %collective-permute-start.36 = (bf16[256,4224]{1,0:T(8,128)(2,1)}, bf16[256,4224]{1,0:T(8,128)(2,1)}, u32[]{:S(2)}, u32[]{:S(2)}) collective-permute-start(bf16[256,4224]{1,0:T(8,128)(2,1)} %get-tuple-element.454), channel_id=1, source_target_pairs={{0,16},{4,20},{8,24},{12,28},{16,0},{20,4},{24,8},{28,12},{1,17},{... | collective-permute-start | bytes 6488072 | tf_op jit(solution)/shard_map/ppermute | solution.py:499
  362.7 24.7 %collective-permute-start.35 = (bf16[2560,256]{1,0:T(8,128)(2,1)}, bf16[2560,256]{1,0:T(8,128)(2,1)}, u32[]{:S(2)}, u32[]{:S(2)}) collective-permute-start(bf16[2560,256]{1,0:T(8,128)(2,1)} %get-tuple-element.662), channel_id=1, source_target_pairs={{0,4},{4,0},{8,12},{12,8},{16,20},{20,16},{24,28},{28,24},{1,5},{5... | collective-permute-start | bytes 3932168 | tf_op jit(solution)/shard_map/ppermute | solution.py:499
  362.7 30.2 %collective-permute-start.38 = (bf16[2560,256]{1,0:T(8,128)(2,1)}, bf16[2560,256]{1,0:T(8,128)(2,1)}, u32[]{:S(2)}, u32[]{:S(2)}) collective-permute-start(bf16[2560,256]{1,0:T(8,128)(2,1)} %get-tuple-element.614), channel_id=1, source_target_pairs={{0,4},{4,0},{8,12},{12,8},{16,20},{20,16},{24,28},{28,24},{1,5},{5... | collective-permute-start | bytes 3932168 | tf_op jit(solution)/shard_map/ppermute | solution.py:499
  385.3 121.7 %all-gather.2.cloned.1.call-start = ((), (), s32[]{:S(2)}) async-start(), calls=%async_computation.3 | async-start | bytes 1638400 | tf_op jit(solution)/shard_map/all_gather | solution.py:1151
  385.4 52.5 %collective-permute-start.40 = (bf16[128,4224]{1,0:T(8,128)(2,1)}, bf16[128,4224]{1,0:T(8,128)(2,1)}, u32[]{:S(2)}, u32[]{:S(2)}) collective-permute-start(bf16[128,4224]{1,0:T(8,128)(2,1)} %copy-done.49), channel_id=1, source_target_pairs={{0,8},{4,12},{8,0},{12,4},{16,24},{20,28},{24,16},{28,20},{1,9},{5... | collective-permute-start | bytes 3244040 | tf_op jit(solution)/shard_map/ppermute | solution.py:499
  386.2 48.4 %collective-permute-start.41 = (bf16[128,4224]{1,0:T(8,128)(2,1)}, bf16[128,4224]{1,0:T(8,128)(2,1)}, u32[]{:S(2)}, u32[]{:S(2)}) collective-permute-start(bf16[128,4224]{1,0:T(8,128)(2,1)} %copy-done.48), channel_id=1, source_target_pairs={{0,16},{4,20},{8,24},{12,28},{16,0},{20,4},{24,8},{28,12},{1,17},{... | collective-permute-start | bytes 3244040 | tf_op jit(solution)/shard_map/ppermute | solution.py:499
  392.7 30.3 %collective-permute-start.37 = (bf16[1280,256]{1,0:T(8,128)(2,1)}, bf16[1280,256]{1,0:T(8,128)(2,1)}, u32[]{:S(2)}, u32[]{:S(2)}) collective-permute-start(bf16[1280,256]{1,0:T(8,128)(2,1)} %get-tuple-element.479), channel_id=1, source_target_pairs={{0,8},{4,12},{8,0},{12,4},{16,24},{20,28},{24,16},{28,20},{1,9},{5... | collective-permute-start | bytes 1966088 | tf_op jit(solution)/shard_map/ppermute | solution.py:499
  396.6 32.9 %collective-permute-start.42 = (bf16[1280,256]{1,0:T(8,128)(2,1)}, bf16[1280,256]{1,0:T(8,128)(2,1)}, u32[]{:S(2)}, u32[]{:S(2)}) collective-permute-start(bf16[1280,256]{1,0:T(8,128)(2,1)} %get-tuple-element.483), channel_id=1, source_target_pairs={{0,16},{4,20},{8,24},{12,28},{16,0},{20,4},{24,8},{28,12},{1,17},{... | collective-permute-start | bytes 1966088 | tf_op jit(solution)/shard_map/ppermute | solution.py:499
  449.2 185.6 %all-reduce.3.cloned.1.call-start = ((), (), s32[]{:S(2)}) async-start(), calls=%async_computation.5 | async-start | bytes 12582912 | tf_op jit(solution)/shard_map/psum | solution.py:1140
  449.8 35.7 %collective-permute-start.48 = (bf16[128,4224]{1,0:T(8,128)(2,1)}, bf16[128,4224]{1,0:T(8,128)(2,1)}, u32[]{:S(2)}, u32[]{:S(2)}) collective-permute-start(bf16[128,4224]{1,0:T(8,128)(2,1)} %copy-done.24), channel_id=1, source_target_pairs={{0,8},{4,12},{8,0},{12,4},{16,24},{20,28},{24,16},{28,20},{1,9},{5... | collective-permute-start | bytes 3244040 | tf_op jit(solution)/shard_map/ppermute | solution.py:499
  451.3 34.2 %collective-permute-start.47 = (bf16[128,4224]{1,0:T(8,128)(2,1)}, bf16[128,4224]{1,0:T(8,128)(2,1)}, u32[]{:S(2)}, u32[]{:S(2)}) collective-permute-start(bf16[128,4224]{1,0:T(8,128)(2,1)} %copy-done.24), channel_id=1, source_target_pairs={{0,16},{4,20},{8,24},{12,28},{16,0},{20,4},{24,8},{28,12},{1,17},{... | collective-permute-start | bytes 3244040 | tf_op jit(solution)/shard_map/ppermute | solution.py:499
  451.6 45.7 %collective-permute-start.53 = (bf16[128,4224]{1,0:T(8,128)(2,1)}, bf16[128,4224]{1,0:T(8,128)(2,1)}, u32[]{:S(2)}, u32[]{:S(2)}) collective-permute-start(bf16[128,4224]{1,0:T(8,128)(2,1)} %copy-done.22), channel_id=1, source_target_pairs={{0,16},{4,20},{8,24},{12,28},{16,0},{20,4},{24,8},{28,12},{1,17},{... | collective-permute-start | bytes 3244040 | tf_op jit(solution)/shard_map/ppermute | solution.py:499
  453.4 44.0 %collective-permute-start.52 = (bf16[128,4224]{1,0:T(8,128)(2,1)}, bf16[128,4224]{1,0:T(8,128)(2,1)}, u32[]{:S(2)}, u32[]{:S(2)}) collective-permute-start(bf16[128,4224]{1,0:T(8,128)(2,1)} %copy-done.22), channel_id=1, source_target_pairs={{0,8},{4,12},{8,0},{12,4},{16,24},{20,28},{24,16},{28,20},{1,9},{5... | collective-permute-start | bytes 3244040 | tf_op jit(solution)/shard_map/ppermute | solution.py:499
  510.8 164.2 %reduce-scatter.5.cloned.1.call-start = ((), (), s32[]{:S(2)}) async-start(), calls=%async_computation.4 | async-start | bytes 3276800 | tf_op jit(solution)/shard_map/reduce_scatter | solution.py:1176
  533.5 105.0 %collective-permute-start.73 = (bf16[128,4224]{1,0:T(8,128)(2,1)}, bf16[128,4224]{1,0:T(8,128)(2,1)}, u32[]{:S(2)}, u32[]{:S(2)}) collective-permute-start(bf16[128,4224]{1,0:T(8,128)(2,1)} %collective-permute-done.52.refs_1_), channel_id=1, source_target_pairs={{0,16},{4,20},{8,24},{12,28},{16,0},{20,4},{24,8},{28,12},{1,17},{... | collective-permute-start | bytes 3244040 | tf_op jit(solution)/shard_map/ppermute | solution.py:499
  534.2 100.6 %collective-permute-start.50 = (bf16[128,4224]{1,0:T(8,128)(2,1)}, bf16[128,4224]{1,0:T(8,128)(2,1)}, u32[]{:S(2)}, u32[]{:S(2)}) collective-permute-start(bf16[128,4224]{1,0:T(8,128)(2,1)} %collective-permute-done.47.refs_1_), channel_id=1, source_target_pairs={{0,8},{4,12},{8,0},{12,4},{16,24},{20,28},{24,16},{28,20},{1,9},{5... | collective-permute-start | bytes 3244040 | tf_op jit(solution)/shard_map/ppermute | solution.py:499
  535.5 38.4 %collective-permute-start.60 = (bf16[64,512]{1,0:T(8,128)(2,1)S(1)}, bf16[64,512]{1,0:T(8,128)(2,1)S(1)}, u32[]{:S(2)}, u32[]{:S(2)}) collective-permute-start(bf16[64,512]{1,0:T(8,128)(2,1)S(1)} %get-tuple-element.646), channel_id=1, source_target_pairs={{0,16},{4,20},{8,24},{12,28},{16,0},{20,4},{24,8},{28,12},{1,17},{... | collective-permute-start | bytes 196616 | tf_op jit(solution)/shard_map/ppermute | solution.py:499
  536.9 37.5 %collective-permute-start.59 = (bf16[64,1024]{1,0:T(8,128)(2,1)S(1)}, bf16[64,1024]{1,0:T(8,128)(2,1)S(1)}, u32[]{:S(2)}, u32[]{:S(2)}) collective-permute-start(bf16[64,1024]{1,0:T(8,128)(2,1)S(1)} %get-tuple-element.640), channel_id=1, source_target_pairs={{0,8},{4,12},{8,0},{12,4},{16,24},{20,28},{24,16},{28,20},{1,9},{5... | collective-permute-start | bytes 393224 | tf_op jit(solution)/shard_map/ppermute | solution.py:499
  (150 other events, 1802.2 us)
Sparse Core Ops, SparseCore 0:
  385.4 29.1 reduce-scatter.2
  449.3 36.4 all-gather.1
  584.0 50.7 reduce-scatter.4
Sparse Core Ops, SparseCore 1:
  510.9 123.9 all-reduce.2

commit v5 on v3

--- a/solution.py
+++ b/solution.py
@@ -1204,10 +1204,16 @@
     order.mark(out_sum, up_query_sum)
     while len(mlp[0].steps) > 1:
         steps(*mlp)
-    steps(pair_weight, down_query)
     out_sum = order.take(out_sum).astype(jnp.float32)
     up_query_sum = up_query_sum.astype(jnp.float32)
     order.mark(out_sum, up_query_sum)
+    while len(down_query.steps) > 1:
+        steps(pair_weight, down_query)
+    finish(*mlp)
+    down_sum, gate_sum, up_sum = unfold(
+        mlp, [(down_weight.shape[0], True)] + [(gate_weight.shape[1], False)] * 2, "mlp_grads_laid"
+    )
+    order.mark(down_sum)
     finish(pair_weight, down_query)
     while gains.bits:
         steps(gains)
@@ -1219,11 +1225,6 @@
         "query_down_key_value_laid",
     )
     order.mark(down_query_sum)
-    finish(*mlp)
-    down_sum, gate_sum, up_sum = unfold(
-        mlp, [(down_weight.shape[0], True)] + [(gate_weight.shape[1], False)] * 2, "mlp_grads_laid"
-    )
-    order.mark(down_sum)
     result = (hidden_res + order.take(result_sum).astype(jnp.float32)).astype(jnp.bfloat16)
     attn_gain_sum, mlp_gain_sum = gains.held[0], gains.held[1]
     return (

time: 674 us -> 670 us (level)
    ppermute x27, starting transfers between devices: 53.8 us -> 42.4 us  [ring_pass(): return lax.ppermute(array, 'mp', pairs)]
    ppermute x40, waiting for transfers between devices: 103 us -> 94.6 us  [trade(): return lax.ppermute(array, 'dp', [(i, i ^ 1 << bit) for i in range(count)])]
    ppermute x40, starting transfers between devices: 33.7 us -> 41.5 us  [trade(): return lax.ppermute(array, 'dp', [(i, i ^ 1 << bit) for i in range(count)])]
    unnamed x206 -> x204, local copies, waits for them, and re-layouts: 27.3 us -> 27.4 us
  transfers between devices with their start and end apart: 81 -> 81, of which waited for: 40 -> 38; matrix products, arithmetic and copies ran while one was open for 14% -> 15% of each run, Pallas kernels for 18% -> 18%
where the time goes in v5:
time: 670 us; the launch traced here: 662 us
  waiting for transfers between devices  279 us (42%)
  Pallas kernels  130 us (19%)
  starting transfers between devices  94.8 us (14%)
  matrix products  56.7 us (8%)
  local copies, waits for them, and re-layouts  55.6 us (8%)
  other arithmetic  24.9 us (4%)
  between operations  21.1 us (3%)
    ppermute x27, waiting for transfers between devices, ring_pass(): return lax.ppermute(array, 'mp', pairs)  141 us
    ppermute x40, waiting for transfers between devices, trade(): return lax.ppermute(array, 'dp', [(i, i ^ 1 << bit) for i in range(count)])  94.6 us
    ppermute x27, starting transfers between devices, ring_pass(): return lax.ppermute(array, 'mp', pairs)  42.4 us
    ppermute x40, starting transfers between devices, trade(): return lax.ppermute(array, 'dp', [(i, i ^ 1 << bit) for i in range(count)])  41.5 us
    pallas_call x4, Pallas kernels, product_blocks(): pl.pallas_call(functools.partial(product_kernel, tuple(groups), split), g...  40.2 us
    psum x1, waiting for transfers between devices, shards(): out_sum, up_query_sum = lax.psum((out_part, up_query_part), 'dp')  29.6 us
    unnamed x204, local copies, waits for them, and re-layouts  27.4 us
    dot_general x12, matrix products, dotf(): return jnp.dot(left, right, preferred_element_type=jnp.float32)  23 us
  transfers between devices with their start and end apart: 81, of which 38 were waited for; matrix products, arithmetic and copies ran while one was open for 15% of the time, Pallas kernels for 18%

profile of v5, /device:TPU:0, one launch (start us, length us, event | category | flops | bytes accessed | tf_op | source)
XLA Modules:
  0.0 662.3 jit_solution(18043447246778171688)
XLA Ops:
  22.2 9.9 %collective-permute-done.1 = bf16[160,512]{1,0:T(8,128)(2,1)S(1)} collective-permute-done((bf16[160,512]{1,0:T(8,128)(2,1)S(1)}, bf16[160,512]{1,0:T(8,128)(2,1)S(1)}, u32[]{:S(2)}, u32[]{:S(2)}) %collective-permute-start.1) | collective-permute-done | bytes 163872 | tf_op jit(solution)/shard_map/ppermute | solution.py:436
  43.2 5.7 collective-permute-done.2
  93.2 8.8 %attention_forward.1 = (bf16[640,1024]{1,0:T(8,128)(2,1)}, f32[256,2560]{1,0:T(8,128)}, f32[1,2560]{1,0:T(1,128)S(1)}) custom-call(s32[1]{0:T(128)} %bitcast.group, bf16[640,1024]{1,0:T(8,128)(2,1)} %convolution_convert_fusion.2.query, bf16[1280,256]{1,0:T(8,128)(2,1)S(1)} %constant_dynamic-update-slice_fusion.refs_0_, ...), custom_call_target="tpu_custom_call" | custom-call | flops 13421772800 | bytes 5242880 | tf_op jit(solution)/shard_map/attention_forward/pallas_call | solution.py:231
  102.0 12.0 %collective-permute-done.17 = bf16[160,512]{1,0:T(8,128)(2,1)S(1)} collective-permute-done((bf16[160,512]{1,0:T(8,128)(2,1)S(1)}, bf16[160,512]{1,0:T(8,128)(2,1)S(1)}, u32[]{:S(2)}, u32[]{:S(2)}) %collective-permute-start.17) | collective-permute-done | bytes 163872 | tf_op jit(solution)/shard_map/ppermute | solution.py:968
  120.9 7.6 %fusion = f32[640,1408]{1,0:T(8,128)} fusion(bf16[1408,2048]{1,0:T(8,128)(2,1)S(1)} %bitcast.62, bf16[160,2048]{1,0:T(8,128)(2,1)} %copy-done.59, bf16[160,2048]{1,0:T(8,128)(2,1)} %collective-permute-done.12.refs_2_, bf16[160,2048]{1,0:T(8,128)(2,1)} %collective-permute-done.8.refs_1_, bf16[160,2048]{1,0:T(8,128)(2,1)S(1)} %copy-done.2), kind=kOutput, calls=%fused_computation.2 | convolution fusion | flops 3701473280 | bytes 11993088 | tf_op jit(solution)/shard_map/td,fd->tf/dot_general | solution.py:1051
  128.4 4.8 collective-permute-done.20
  135.8 12.3 %collective-permute-done.21 = bf16[160,2048]{1,0:T(8,128)(2,1)S(1)} collective-permute-done((bf16[160,2048]{1,0:T(8,128)(2,1)S(1)}, bf16[160,2048]{1,0:T(8,128)(2,1)S(1)}, u32[]{:S(2)}, u32[]{:S(2)}) %collective-permute-start.21) | collective-permute-done | bytes 655392 | tf_op jit(solution)/shard_map/ppermute | solution.py:436
  150.7 11.0 %collective-permute-done.22 = bf16[160,2048]{1,0:T(8,128)(2,1)S(1)} collective-permute-done((bf16[160,2048]{1,0:T(8,128)(2,1)S(1)}, bf16[160,2048]{1,0:T(8,128)(2,1)S(1)}, u32[]{:S(2)}, u32[]{:S(2)}) %collective-permute-start.22) | collective-permute-done | bytes 655392 | tf_op jit(solution)/shard_map/ppermute | solution.py:436
  172.5 6.6 collective-permute-done.23.refs_9_
  188.3 9.4 %collective-permute-done.24.refs_10_ = bf16[160,2048]{1,0:T(8,128)(2,1)S(1)} collective-permute-done((bf16[160,2048]{1,0:T(8,128)(2,1)S(1)}, bf16[160,2048]{1,0:T(8,128)(2,1)S(1)}, u32[]{:S(2)}, u32[]{:S(2)}) %collective-permute-start.24) | collective-permute-done | bytes 655392 | tf_op jit(solution)/shard_map/ppermute | solution.py:436
  213.3 10.6 %collective-permute-done.25.refs_11_ = bf16[160,2048]{1,0:T(8,128)(2,1)S(1)} collective-permute-done((bf16[160,2048]{1,0:T(8,128)(2,1)S(1)}, bf16[160,2048]{1,0:T(8,128)(2,1)S(1)}, u32[]{:S(2)}, u32[]{:S(2)}) %collective-permute-start.25) | collective-permute-done | bytes 655392 | tf_op jit(solution)/shard_map/ppermute | solution.py:436
  238.5 9.2 %collective-permute-done.28 = bf16[160,2048]{1,0:T(8,128)(2,1)S(1)} collective-permute-done((bf16[160,2048]{1,0:T(8,128)(2,1)S(1)}, bf16[160,2048]{1,0:T(8,128)(2,1)S(1)}, u32[]{:S(2)}, u32[]{:S(2)}) %collective-permute-start.28) | collective-permute-done | bytes 655392 | tf_op jit(solution)/shard_map/ppermute | solution.py:436
  249.3 8.7 %mlp_grads_low_sent.1 = bf16[512,4224]{1,0:T(8,128)(2,1)} custom-call(s32[4]{0:T(128)S(1)} %get-tuple-element.654.places, bf16[160,2048]{1,0:T(8,128)(2,1)S(1)} %copy-done.2, bf16[160,2048]{1,0:T(8,128)(2,1)} %collective-permute-done.8.refs_1_, bf16[160,2048]{1,0:T(8,128)(2,1)} %collective-permute-done.12.refs_2_, bf16[160,2048]{1,0:T(8,128)(2,1)} %copy-done.59, ...), custom_call_target="tpu_custom_call" | custom-call | tf_op jit(solution)/shard_map/mlp_grads_low_sent/pallas_call | solution.py:644
  258.6 8.7 %mlp_grads_high_sent.1 = bf16[512,4224]{1,0:T(8,128)(2,1)} custom-call(s32[4]{0:T(128)S(1)} %get-tuple-element.652.places, bf16[160,2048]{1,0:T(8,128)(2,1)S(1)} %copy-done.2, bf16[160,2048]{1,0:T(8,128)(2,1)} %collective-permute-done.8.refs_1_, bf16[160,2048]{1,0:T(8,128)(2,1)} %collective-permute-done.12.refs_2_, bf16[160,2048]{1,0:T(8,128)(2,1)} %copy-done.59, ...), custom_call_target="tpu_custom_call" | custom-call | tf_op jit(solution)/shard_map/mlp_grads_high_sent/pallas_call | solution.py:644
  269.2 16.3 %collective-permute-done.29.refs_0_ = bf16[160,2048]{1,0:T(8,128)(2,1)S(1)} collective-permute-done((bf16[160,2048]{1,0:T(8,128)(2,1)S(1)}, bf16[160,2048]{1,0:T(8,128)(2,1)S(1)}, u32[]{:S(2)}, u32[]{:S(2)}) %collective-permute-start.29) | collective-permute-done | bytes 655392 | tf_op jit(solution)/shard_map/ppermute | solution.py:436
  288.9 11.4 %mlp_grads_low_kept.1 = (bf16[256,4224]{1,0:T(8,128)(2,1)}, bf16[256,4224]{1,0:T(8,128)(2,1)}) custom-call(s32[4]{0:T(128)S(1)} %get-tuple-element.653.places, bf16[160,2048]{1,0:T(8,128)(2,1)S(1)} %copy-done.2, bf16[160,2048]{1,0:T(8,128)(2,1)} %collective-permute-done.8.refs_1_, bf16[160,2048]{1,0:T(8,128)(2,1)} %collective-permute-done.12.refs_2_, ...), custom_call_target="tpu_custom_call" | custom-call | tf_op jit(solution)/shard_map/mlp_grads_low_kept/pallas_call | solution.py:644
  308.4 11.4 %mlp_grads_high_kept.1 = (bf16[256,4224]{1,0:T(8,128)(2,1)}, bf16[256,4224]{1,0:T(8,128)(2,1)}) custom-call(s32[4]{0:T(128)S(1)} %get-tuple-element.651.places, bf16[160,2048]{1,0:T(8,128)(2,1)S(1)} %copy-done.2, bf16[160,2048]{1,0:T(8,128)(2,1)} %collective-permute-done.8.refs_1_, bf16[160,2048]{1,0:T(8,128)(2,1)} %collective-permute-done.12.refs_2_, ...), custom_call_target="tpu_custom_call" | custom-call | tf_op jit(solution)/shard_map/mlp_grads_high_kept/pallas_call | solution.py:644
  319.7 7.2 %collective-permute-start.36 = (bf16[256,4224]{1,0:T(8,128)(2,1)}, bf16[256,4224]{1,0:T(8,128)(2,1)}, u32[]{:S(2)}, u32[]{:S(2)}) collective-permute-start(bf16[256,4224]{1,0:T(8,128)(2,1)} %get-tuple-element.454), channel_id=1, source_target_pairs={{0,16},{4,20},{8,24},{12,28},{16,0},{20,4},{24,8},{28,12},{1,17},{... | collective-permute-start | bytes 6488072 | tf_op jit(solution)/shard_map/ppermute | solution.py:499
  329.9 11.8 %attention_backward.1 = (bf16[640,1024]{1,0:T(8,128)(2,1)}, bf16[5120,256]{1,0:T(8,128)(2,1)}, bf16[5120,256]{1,0:T(8,128)(2,1)}) custom-call(s32[1]{0:T(128)} %bitcast.group, bf16[640,1024]{1,0:T(8,128)(2,1)} %convolution_convert_fusion.2.query, bf16[640,1024]{1,0:T(8,128)(2,1)} %constant_dynamic-update-slice_fusion.20.grad, ...), custom_call_target="tpu_custom_call" | custom-call | flops 13421772800 | bytes 5242880 | tf_op jit(solution)/shard_map/attention_backward/pallas_call | solution.py:257
  341.8 6.7 %collective-permute-done.34.got = bf16[256,4224]{1,0:T(8,128)(2,1)} collective-permute-done((bf16[256,4224]{1,0:T(8,128)(2,1)}, bf16[256,4224]{1,0:T(8,128)(2,1)}, u32[]{:S(2)}, u32[]{:S(2)}) %collective-permute-start.34) | collective-permute-done | bytes 2162720 | tf_op jit(solution)/shard_map/ppermute | solution.py:499
  348.5 5.1 fusion.48
  359.2 13.6 %collective-permute-done.36.got = bf16[256,4224]{1,0:T(8,128)(2,1)} collective-permute-done((bf16[256,4224]{1,0:T(8,128)(2,1)}, bf16[256,4224]{1,0:T(8,128)(2,1)}, u32[]{:S(2)}, u32[]{:S(2)}) %collective-permute-start.36) | collective-permute-done | bytes 2162720 | tf_op jit(solution)/shard_map/ppermute | solution.py:499
  402.0 5.0 convolution_convert_fusion
  407.0 11.5 %collective-permute-done.37.got = bf16[1280,256]{1,0:T(8,128)(2,1)} collective-permute-done((bf16[1280,256]{1,0:T(8,128)(2,1)}, bf16[1280,256]{1,0:T(8,128)(2,1)}, u32[]{:S(2)}, u32[]{:S(2)}) %collective-permute-start.37) | collective-permute-done | bytes 655392 | tf_op jit(solution)/shard_map/ppermute | solution.py:499
  437.6 4.6 collective-permute-done.44
  450.7 15.0 %collective-permute-done.46 = bf16[160,512]{1,0:T(8,128)(2,1)S(1)} collective-permute-done((bf16[160,512]{1,0:T(8,128)(2,1)S(1)}, bf16[160,512]{1,0:T(8,128)(2,1)S(1)}, u32[]{:S(2)}, u32[]{:S(2)}) %collective-permute-start.46) | collective-permute-done | bytes 163872 | tf_op jit(solution)/shard_map/ppermute | solution.py:436
  471.4 4.8 result.1
  481.1 11.5 %collective-permute-done.49.refs_1_ = bf16[128,4224]{1,0:T(8,128)(2,1)} collective-permute-done((bf16[128,4224]{1,0:T(8,128)(2,1)}, bf16[128,4224]{1,0:T(8,128)(2,1)}, u32[]{:S(2)}, u32[]{:S(2)}) %collective-permute-start.49) | collective-permute-done | bytes 1081376 | tf_op jit(solution)/shard_map/ppermute | solution.py:499
  532.4 35.6 %collective-permute-done.59 = bf16[64,512]{1,0:T(8,128)(2,1)S(1)} collective-permute-done((bf16[64,512]{1,0:T(8,128)(2,1)S(1)}, bf16[64,512]{1,0:T(8,128)(2,1)S(1)}, u32[]{:S(2)}, u32[]{:S(2)}) %collective-permute-start.59) | collective-permute-done | bytes 65568 | tf_op jit(solution)/shard_map/ppermute | solution.py:499
  575.0 29.6 %all-reduce.3.cloned.1.call-done = (bf16[1024,2048]{1,0:T(8,128)(2,1)}, bf16[1024,1024]{1,0:T(8,128)(2,1)}) async-done(((bf16[1024,2048]{1,0:T(8,128)(2,1)}, bf16[1024,1024]{1,0:T(8,128)(2,1)}), (bf16[1024,2048]{1,0:T(8,128)(2,1)}, bf16[1024,1024]{1,0:T(8,128)(2,1)})) %all-reduce.3.cloned.1.call-update) | async-done | bytes 6291472 | tf_op jit(solution)/shard_map/psum | solution.py:1140
  628.4 17.4 %mlp_grads_laid.1 = (f32[1408,2048]{1,0:T(8,128)}, f32[2048,1408]{1,0:T(8,128)}, f32[2048,1408]{1,0:T(8,128)}) custom-call(s32[16]{0:T(128)S(1)} %get-tuple-element.661.places, bf16[512,4224]{1,0:T(8,128)(2,1)} %join.4.refs_0_, bf16[512,4224]{1,0:T(8,128)(2,1)} %collective-permute-done.73.refs_1_, bf16[512,4224]{1,0:T(8,128)(2,1)} %join.5.refs_2_, ...), custom_call_target="tpu_custom_call" | custom-call | tf_op jit(solution)/shard_map/mlp_grads_laid/pallas_call | solution.py:795
  645.9 4.7 query_down_key_value_laid.1
  (486 shorter events, 292.9 us)
Async XLA Ops:
  8.0 435.0 %reduce-scatter.3.cloned.1.call-start = ((), (), s32[]{:S(2)}) async-start(), calls=%async_computation.2 | async-start | bytes 1638400 | tf_op jit(solution)/shard_map/reduce_scatter | solution.py:1135
  16.6 20.3 %collective-permute-start = (bf16[160,1024]{1,0:T(8,128)(2,1)}, bf16[160,1024]{1,0:T(8,128)(2,1)}, u32[]{:S(2)}, u32[]{:S(2)}) collective-permute-start(bf16[160,1024]{1,0:T(8,128)(2,1)} %get-tuple-element.658), channel_id=1, source_target_pairs={{0,1},{1,3},{3,2},{2,0},{4,5},{5,7},{7,6},{6,4},{8,9},{9,11},{11,1... | collective-permute-start | bytes 983048 | tf_op jit(solution)/shard_map/ppermute | solution.py:436
  86.8 28.2 %collective-permute-start.16 = (bf16[160,2048]{1,0:T(8,128)(2,1)}, bf16[160,2048]{1,0:T(8,128)(2,1)S(1)}, u32[]{:S(2)}, u32[]{:S(2)}) collective-permute-start(bf16[160,2048]{1,0:T(8,128)(2,1)} %collective-permute-done.12.refs_2_), channel_id=1, source_target_pairs={{0,1},{1,3},{3,2},{2,0},{4,5},{5,7},{7,6},{6,4},{8,9},{9,11},{11,1... | collective-permute-start | bytes 1966088 | tf_op jit(solution)/shard_map/ppermute | solution.py:436
  89.4 24.6 %collective-permute-start.17 = (bf16[160,512]{1,0:T(8,128)(2,1)S(1)}, bf16[160,512]{1,0:T(8,128)(2,1)S(1)}, u32[]{:S(2)}, u32[]{:S(2)}) collective-permute-start(bf16[160,512]{1,0:T(8,128)(2,1)S(1)} %get-tuple-element.635), channel_id=1, source_target_pairs={{0,1},{1,3},{3,2},{2,0},{4,5},{5,7},{7,6},{6,4},{8,9},{9,11},{11,1... | collective-permute-start | bytes 491528 | tf_op jit(solution)/shard_map/ppermute | solution.py:968
  91.6 22.3 %collective-permute-start.18 = (bf16[160,512]{1,0:T(8,128)(2,1)S(1)}, bf16[160,512]{1,0:T(8,128)(2,1)S(1)}, u32[]{:S(2)}, u32[]{:S(2)}) collective-permute-start(bf16[160,512]{1,0:T(8,128)(2,1)S(1)} %get-tuple-element.634), channel_id=1, source_target_pairs={{0,3},{1,2},{3,0},{2,1},{4,7},{5,6},{7,4},{6,5},{8,11},{9,10},{11,... | collective-permute-start | bytes 491528 | tf_op jit(solution)/shard_map/ppermute | solution.py:968
  92.5 21.5 %collective-permute-start.19 = (bf16[160,512]{1,0:T(8,128)(2,1)S(1)}, bf16[160,512]{1,0:T(8,128)(2,1)S(1)}, u32[]{:S(2)}, u32[]{:S(2)}) collective-permute-start(bf16[160,512]{1,0:T(8,128)(2,1)S(1)} %get-tuple-element.633), channel_id=1, source_target_pairs={{0,2},{1,0},{3,1},{2,3},{4,6},{5,4},{7,5},{6,7},{8,10},{9,8},{11,9... | collective-permute-start | bytes 491528 | tf_op jit(solution)/shard_map/ppermute | solution.py:968
  188.2 23.5 %collective-permute-start.26 = (bf16[160,2048]{1,0:T(8,128)(2,1)S(1)}, bf16[160,2048]{1,0:T(8,128)(2,1)S(1)}, u32[]{:S(2)}, u32[]{:S(2)}) collective-permute-start(bf16[160,2048]{1,0:T(8,128)(2,1)S(1)} %fusion.9), channel_id=1, source_target_pairs={{0,1},{1,3},{3,2},{2,0},{4,5},{5,7},{7,6},{6,4},{8,9},{9,11},{11,1... | collective-permute-start | bytes 1966088 | tf_op jit(solution)/shard_map/ppermute | solution.py:436
  197.7 26.2 %collective-permute-start.25 = (bf16[160,2048]{1,0:T(8,128)(2,1)S(1)}, bf16[160,2048]{1,0:T(8,128)(2,1)S(1)}, u32[]{:S(2)}, u32[]{:S(2)}) collective-permute-start(bf16[160,2048]{1,0:T(8,128)(2,1)S(1)} %collective-permute-done.24.refs_10_), channel_id=1, source_target_pairs={{0,1},{1,3},{3,2},{2,0},{4,5},{5,7},{7,6},{6,4},{8,9},{9,11},{11,1... | collective-permute-start | bytes 1966088 | tf_op jit(solution)/shard_map/ppermute | solution.py:436
  211.9 23.7 %collective-permute-start.27 = (bf16[160,2048]{1,0:T(8,128)(2,1)S(1)}, bf16[160,2048]{1,0:T(8,128)(2,1)S(1)}, u32[]{:S(2)}, u32[]{:S(2)}) collective-permute-start(bf16[160,2048]{1,0:T(8,128)(2,1)S(1)} %add_convert_fusion.3), channel_id=1, source_target_pairs={{0,1},{1,3},{3,2},{2,0},{4,5},{5,7},{7,6},{6,4},{8,9},{9,11},{11,1... | collective-permute-start | bytes 1966088 | tf_op jit(solution)/shard_map/ppermute | solution.py:436
  258.0 30.9 %collective-permute-start.31 = (bf16[512,4224]{1,0:T(8,128)(2,1)}, bf16[512,4224]{1,0:T(8,128)(2,1)}, u32[]{:S(2)}, u32[]{:S(2)}) collective-permute-start(bf16[512,4224]{1,0:T(8,128)(2,1)} %mlp_grads_low_sent.1), channel_id=1, source_target_pairs={{0,4},{4,0},{8,12},{12,8},{16,20},{20,16},{24,28},{28,24},{1,5},{5... | collective-permute-start | bytes 12976136 | tf_op jit(solution)/shard_map/ppermute | solution.py:499
  267.3 41.0 %collective-permute-start.33 = (bf16[512,4224]{1,0:T(8,128)(2,1)}, bf16[512,4224]{1,0:T(8,128)(2,1)}, u32[]{:S(2)}, u32[]{:S(2)}) collective-permute-start(bf16[512,4224]{1,0:T(8,128)(2,1)} %mlp_grads_high_sent.1), channel_id=1, source_target_pairs={{0,4},{4,0},{8,12},{12,8},{16,20},{20,16},{24,28},{28,24},{1,5},{5... | collective-permute-start | bytes 12976136 | tf_op jit(solution)/shard_map/ppermute | solution.py:499
  300.3 48.2 %collective-permute-start.34 = (bf16[256,4224]{1,0:T(8,128)(2,1)}, bf16[256,4224]{1,0:T(8,128)(2,1)}, u32[]{:S(2)}, u32[]{:S(2)}) collective-permute-start(bf16[256,4224]{1,0:T(8,128)(2,1)} %get-tuple-element.429), channel_id=1, source_target_pairs={{0,8},{4,12},{8,0},{12,4},{16,24},{20,28},{24,16},{28,20},{1,9},{5... | collective-permute-start | bytes 6488072 | tf_op jit(solution)/shard_map/ppermute | solution.py:499
  302.2 25.5 %collective-permute-start.32 = (bf16[160,2048]{1,0:T(8,128)(2,1)S(1)}, bf16[160,2048]{1,0:T(8,128)(2,1)S(1)}, u32[]{:S(2)}, u32[]{:S(2)}) collective-permute-start(bf16[160,2048]{1,0:T(8,128)(2,1)S(1)} %collective-permute-done.30.refs_0_), channel_id=1, source_target_pairs={{0,1},{1,3},{3,2},{2,0},{4,5},{5,7},{7,6},{6,4},{8,9},{9,11},{11,1... | collective-permute-start | bytes 1966088 | tf_op jit(solution)/shard_map/ppermute | solution.py:436
  319.7 53.1 %collective-permute-start.36 = (bf16[256,4224]{1,0:T(8,128)(2,1)}, bf16[256,4224]{1,0:T(8,128)(2,1)}, u32[]{:S(2)}, u32[]{:S(2)}) collective-permute-start(bf16[256,4224]{1,0:T(8,128)(2,1)} %get-tuple-element.454), channel_id=1, source_target_pairs={{0,16},{4,20},{8,24},{12,28},{16,0},{20,4},{24,8},{28,12},{1,17},{... | collective-permute-start | bytes 6488072 | tf_op jit(solution)/shard_map/ppermute | solution.py:499
  353.6 29.3 %collective-permute-start.35 = (bf16[2560,256]{1,0:T(8,128)(2,1)}, bf16[2560,256]{1,0:T(8,128)(2,1)}, u32[]{:S(2)}, u32[]{:S(2)}) collective-permute-start(bf16[2560,256]{1,0:T(8,128)(2,1)} %get-tuple-element.662), channel_id=1, source_target_pairs={{0,4},{4,0},{8,12},{12,8},{16,20},{20,16},{24,28},{28,24},{1,5},{5... | collective-permute-start | bytes 3932168 | tf_op jit(solution)/shard_map/ppermute | solution.py:499
  353.6 36.1 %collective-permute-start.38 = (bf16[2560,256]{1,0:T(8,128)(2,1)}, bf16[2560,256]{1,0:T(8,128)(2,1)}, u32[]{:S(2)}, u32[]{:S(2)}) collective-permute-start(bf16[2560,256]{1,0:T(8,128)(2,1)} %get-tuple-element.614), channel_id=1, source_target_pairs={{0,4},{4,0},{8,12},{12,8},{16,20},{20,16},{24,28},{28,24},{1,5},{5... | collective-permute-start | bytes 3932168 | tf_op jit(solution)/shard_map/ppermute | solution.py:499
  380.6 121.7 %all-gather.2.cloned.1.call-start = ((), (), s32[]{:S(2)}) async-start(), calls=%async_computation.3 | async-start | bytes 1638400 | tf_op jit(solution)/shard_map/all_gather | solution.py:1151
  380.6 51.8 %collective-permute-start.40 = (bf16[128,4224]{1,0:T(8,128)(2,1)}, bf16[128,4224]{1,0:T(8,128)(2,1)}, u32[]{:S(2)}, u32[]{:S(2)}) collective-permute-start(bf16[128,4224]{1,0:T(8,128)(2,1)} %copy-done.48), channel_id=1, source_target_pairs={{0,8},{4,12},{8,0},{12,4},{16,24},{20,28},{24,16},{28,20},{1,9},{5... | collective-permute-start | bytes 3244040 | tf_op jit(solution)/shard_map/ppermute | solution.py:499
  381.1 48.1 %collective-permute-start.41 = (bf16[128,4224]{1,0:T(8,128)(2,1)}, bf16[128,4224]{1,0:T(8,128)(2,1)}, u32[]{:S(2)}, u32[]{:S(2)}) collective-permute-start(bf16[128,4224]{1,0:T(8,128)(2,1)} %copy-done.47), channel_id=1, source_target_pairs={{0,16},{4,20},{8,24},{12,28},{16,0},{20,4},{24,8},{28,12},{1,17},{... | collective-permute-start | bytes 3244040 | tf_op jit(solution)/shard_map/ppermute | solution.py:499
  388.0 30.5 %collective-permute-start.37 = (bf16[1280,256]{1,0:T(8,128)(2,1)}, bf16[1280,256]{1,0:T(8,128)(2,1)}, u32[]{:S(2)}, u32[]{:S(2)}) collective-permute-start(bf16[1280,256]{1,0:T(8,128)(2,1)} %get-tuple-element.479), channel_id=1, source_target_pairs={{0,8},{4,12},{8,0},{12,4},{16,24},{20,28},{24,16},{28,20},{1,9},{5... | collective-permute-start | bytes 1966088 | tf_op jit(solution)/shard_map/ppermute | solution.py:499
  393.4 30.8 %collective-permute-start.42 = (bf16[1280,256]{1,0:T(8,128)(2,1)}, bf16[1280,256]{1,0:T(8,128)(2,1)}, u32[]{:S(2)}, u32[]{:S(2)}) collective-permute-start(bf16[1280,256]{1,0:T(8,128)(2,1)} %get-tuple-element.483), channel_id=1, source_target_pairs={{0,16},{4,20},{8,24},{12,28},{16,0},{20,4},{24,8},{28,12},{1,17},{... | collective-permute-start | bytes 1966088 | tf_op jit(solution)/shard_map/ppermute | solution.py:499
  443.0 161.6 %all-reduce.3.cloned.1.call-start = ((), (), s32[]{:S(2)}) async-start(), calls=%async_computation.5 | async-start | bytes 12582912 | tf_op jit(solution)/shard_map/psum | solution.py:1140
  443.8 37.2 %collective-permute-start.51 = (bf16[128,4224]{1,0:T(8,128)(2,1)}, bf16[128,4224]{1,0:T(8,128)(2,1)}, u32[]{:S(2)}, u32[]{:S(2)}) collective-permute-start(bf16[128,4224]{1,0:T(8,128)(2,1)} %copy-done.23), channel_id=1, source_target_pairs={{0,16},{4,20},{8,24},{12,28},{16,0},{20,4},{24,8},{28,12},{1,17},{... | collective-permute-start | bytes 3244040 | tf_op jit(solution)/shard_map/ppermute | solution.py:499
  444.1 36.9 %collective-permute-start.52 = (bf16[128,4224]{1,0:T(8,128)(2,1)}, bf16[128,4224]{1,0:T(8,128)(2,1)}, u32[]{:S(2)}, u32[]{:S(2)}) collective-permute-start(bf16[128,4224]{1,0:T(8,128)(2,1)} %copy-done.23), channel_id=1, source_target_pairs={{0,8},{4,12},{8,0},{12,4},{16,24},{20,28},{24,16},{28,20},{1,9},{5... | collective-permute-start | bytes 3244040 | tf_op jit(solution)/shard_map/ppermute | solution.py:499
  445.9 46.7 %collective-permute-start.49 = (bf16[128,4224]{1,0:T(8,128)(2,1)}, bf16[128,4224]{1,0:T(8,128)(2,1)}, u32[]{:S(2)}, u32[]{:S(2)}) collective-permute-start(bf16[128,4224]{1,0:T(8,128)(2,1)} %copy-done.21), channel_id=1, source_target_pairs={{0,8},{4,12},{8,0},{12,4},{16,24},{20,28},{24,16},{28,20},{1,9},{5... | collective-permute-start | bytes 3244040 | tf_op jit(solution)/shard_map/ppermute | solution.py:499
  446.2 46.4 %collective-permute-start.50 = (bf16[128,4224]{1,0:T(8,128)(2,1)}, bf16[128,4224]{1,0:T(8,128)(2,1)}, u32[]{:S(2)}, u32[]{:S(2)}) collective-permute-start(bf16[128,4224]{1,0:T(8,128)(2,1)} %copy-done.21), channel_id=1, source_target_pairs={{0,16},{4,20},{8,24},{12,28},{16,0},{20,4},{24,8},{28,12},{1,17},{... | collective-permute-start | bytes 3244040 | tf_op jit(solution)/shard_map/ppermute | solution.py:499
  481.0 169.6 %reduce-scatter.5.cloned.1.call-start = ((), (), s32[]{:S(2)}) async-start(), calls=%async_computation.4 | async-start | bytes 3276800 | tf_op jit(solution)/shard_map/reduce_scatter | solution.py:1176
  528.1 81.7 %collective-permute-start.69 = (bf16[128,4224]{1,0:T(8,128)(2,1)}, bf16[128,4224]{1,0:T(8,128)(2,1)}, u32[]{:S(2)}, u32[]{:S(2)}) collective-permute-start(bf16[128,4224]{1,0:T(8,128)(2,1)} %collective-permute-done.49.refs_1_), channel_id=1, source_target_pairs={{0,16},{4,20},{8,24},{12,28},{16,0},{20,4},{24,8},{28,12},{1,17},{... | collective-permute-start | bytes 3244040 | tf_op jit(solution)/shard_map/ppermute | solution.py:499
  529.6 75.0 %collective-permute-start.70 = (bf16[128,4224]{1,0:T(8,128)(2,1)}, bf16[128,4224]{1,0:T(8,128)(2,1)}, u32[]{:S(2)}, u32[]{:S(2)}) collective-permute-start(bf16[128,4224]{1,0:T(8,128)(2,1)} %collective-permute-done.51.refs_1_), channel_id=1, source_target_pairs={{0,8},{4,12},{8,0},{12,4},{16,24},{20,28},{24,16},{28,20},{1,9},{5... | collective-permute-start | bytes 3244040 | tf_op jit(solution)/shard_map/ppermute | solution.py:499
  529.6 38.4 %collective-permute-start.59 = (bf16[64,512]{1,0:T(8,128)(2,1)S(1)}, bf16[64,512]{1,0:T(8,128)(2,1)S(1)}, u32[]{:S(2)}, u32[]{:S(2)}) collective-permute-start(bf16[64,512]{1,0:T(8,128)(2,1)S(1)} %get-tuple-element.646), channel_id=1, source_target_pairs={{0,16},{4,20},{8,24},{12,28},{16,0},{20,4},{24,8},{28,12},{1,17},{... | collective-permute-start | bytes 196616 | tf_op jit(solution)/shard_map/ppermute | solution.py:499
  530.3 39.6 %collective-permute-start.58 = (bf16[64,1024]{1,0:T(8,128)(2,1)S(1)}, bf16[64,1024]{1,0:T(8,128)(2,1)S(1)}, u32[]{:S(2)}, u32[]{:S(2)}) collective-permute-start(bf16[64,1024]{1,0:T(8,128)(2,1)S(1)} %get-tuple-element.640), channel_id=1, source_target_pairs={{0,8},{4,12},{8,0},{12,4},{16,24},{20,28},{24,16},{28,20},{1,9},{5... | collective-permute-start | bytes 393224 | tf_op jit(solution)/shard_map/ppermute | solution.py:499
  627.1 23.5 %collective-permute-start.75 = (f32[2,512]{1,0:T(2,128)S(1)}, f32[2,512]{1,0:T(2,128)S(1)}, u32[]{:S(2)}, u32[]{:S(2)}) collective-permute-start(f32[2,512]{1,0:T(2,128)S(1)} %add.470), channel_id=1, source_target_pairs={{0,8},{4,12},{8,0},{12,4},{16,24},{20,28},{24,16},{28,20},{1,9},{5... | collective-permute-start | bytes 12296 | tf_op jit(solution)/shard_map/ppermute | solution.py:949
  (148 other events, 1800.8 us)
Sparse Core Ops, SparseCore 0:
  380.7 29.5 reduce-scatter.2
  443.1 37.7 all-gather.1
  529.7 51.8 reduce-scatter.4
Sparse Core Ops, SparseCore 1:
  481.1 123.4 all-reduce.2

commit v6 on v5

--- a/solution.py
+++ b/solution.py
@@ -726,16 +726,16 @@
         order.mark(self.held)
 
 
-def block_lanes(order, products, name):
+def block_lanes(order, products, name, between):
     first, second = orders()
     total = products[0][0][0].shape[1]
     rows = total // lax.axis_size("dp")
     if rows % 256:
+        between()
         return [BlockLane(order, products, first, name)]
-    return [
-        BlockLane(order, products, first, name + "_low", 0, rows // 2),
-        BlockLane(order, products, second, name + "_high", total // 2, rows // 2),
-    ]
+    low = BlockLane(order, products, first, name + "_low", 0, rows // 2)
+    between()
+    return [low, BlockLane(order, products, second, name + "_high", total // 2, rows // 2)]
 
 
 def unfold_kernel(firsts, pieces, targets, places, *refs):
@@ -1104,8 +1104,8 @@
         order,
         [(grad_ring.parts, [activated]), (two_ring.parts, [gate_low, up_low])],
         "mlp_grads",
+        lambda: steps(branch_ring),
     )
-    steps(branch_ring)
     low_part()
     low_part()
     steps(mlp[0])

time: 670 us -> 670 us (level)
    unnamed x204 -> x206, local copies, waits for them, and re-layouts: 27.4 us -> 28 us
  transfers between devices with their start and end apart: 81 -> 81, of which waited for: 38 -> 37; matrix products, arithmetic and copies ran while one was open for 15% -> 14% of each run, Pallas kernels for 18% -> 18%
where the time goes in v6:
time: 670 us; the launch traced here: 662 us
  waiting for transfers between devices  281 us (42%)
  Pallas kernels  130 us (19%)
  starting transfers between devices  95.9 us (14%)
  matrix products  56.8 us (8%)
  local copies, waits for them, and re-layouts  53 us (8%)
  other arithmetic  24.7 us (4%)
  between operations  20.9 us (3%)
    ppermute x27, waiting for transfers between devices, ring_pass(): return lax.ppermute(array, 'mp', pairs)  138 us
    ppermute x40, waiting for transfers between devices, trade(): return lax.ppermute(array, 'dp', [(i, i ^ 1 << bit) for i in range(count)])  98.9 us
    ppermute x27, starting transfers between devices, ring_pass(): return lax.ppermute(array, 'mp', pairs)  47.9 us
    pallas_call x4, Pallas kernels, product_blocks(): pl.pallas_call(functools.partial(product_kernel, tuple(groups), split), g...  40.2 us
    ppermute x40, starting transfers between devices, trade(): return lax.ppermute(array, 'dp', [(i, i ^ 1 << bit) for i in range(count)])  37.1 us
    psum x1, waiting for transfers between devices, shards(): out_sum, up_query_sum = lax.psum((out_part, up_query_part), 'dp')  28.2 us
    unnamed x206, local copies, waits for them, and re-layouts  28 us
    dot_general x12, matrix products, dotf(): return jnp.dot(left, right, preferred_element_type=jnp.float32)  23 us
  transfers between devices with their start and end apart: 81, of which 37 were waited for; matrix products, arithmetic and copies ran while one was open for 14% of the time, Pallas kernels for 18%

profile of v6, /device:TPU:0, one launch (start us, length us, event | category | flops | bytes accessed | tf_op | source)
XLA Modules:
  0.0 662.3 jit_solution(16691988734084562135)
XLA Ops:
  22.2 9.9 %collective-permute-done.1 = bf16[160,512]{1,0:T(8,128)(2,1)S(1)} collective-permute-done((bf16[160,512]{1,0:T(8,128)(2,1)S(1)}, bf16[160,512]{1,0:T(8,128)(2,1)S(1)}, u32[]{:S(2)}, u32[]{:S(2)}) %collective-permute-start.1) | collective-permute-done | bytes 163872 | tf_op jit(solution)/shard_map/ppermute | solution.py:436
  43.0 5.7 collective-permute-done.2
  93.0 8.8 %attention_forward.1 = (bf16[640,1024]{1,0:T(8,128)(2,1)}, f32[256,2560]{1,0:T(8,128)}, f32[1,2560]{1,0:T(1,128)S(1)}) custom-call(s32[1]{0:T(128)} %bitcast.group, bf16[640,1024]{1,0:T(8,128)(2,1)} %convolution_convert_fusion.2.query, bf16[1280,256]{1,0:T(8,128)(2,1)S(1)} %constant_dynamic-update-slice_fusion.refs_0_, ...), custom_call_target="tpu_custom_call" | custom-call | flops 13421772800 | bytes 5242880 | tf_op jit(solution)/shard_map/attention_forward/pallas_call | solution.py:231
  101.8 11.9 %collective-permute-done.17 = bf16[160,512]{1,0:T(8,128)(2,1)S(1)} collective-permute-done((bf16[160,512]{1,0:T(8,128)(2,1)S(1)}, bf16[160,512]{1,0:T(8,128)(2,1)S(1)}, u32[]{:S(2)}, u32[]{:S(2)}) %collective-permute-start.17) | collective-permute-done | bytes 163872 | tf_op jit(solution)/shard_map/ppermute | solution.py:968
  120.5 7.6 %fusion = f32[640,1408]{1,0:T(8,128)} fusion(bf16[1408,2048]{1,0:T(8,128)(2,1)S(1)} %bitcast.62, bf16[160,2048]{1,0:T(8,128)(2,1)} %copy-done.59, bf16[160,2048]{1,0:T(8,128)(2,1)} %collective-permute-done.12.refs_2_, bf16[160,2048]{1,0:T(8,128)(2,1)} %collective-permute-done.8.refs_1_, bf16[160,2048]{1,0:T(8,128)(2,1)S(1)} %copy-done.2), kind=kOutput, calls=%fused_computation.2 | convolution fusion | flops 3701473280 | bytes 11993088 | tf_op jit(solution)/shard_map/td,fd->tf/dot_general | solution.py:1051
  135.4 12.2 %collective-permute-done.21 = bf16[160,2048]{1,0:T(8,128)(2,1)S(1)} collective-permute-done((bf16[160,2048]{1,0:T(8,128)(2,1)S(1)}, bf16[160,2048]{1,0:T(8,128)(2,1)S(1)}, u32[]{:S(2)}, u32[]{:S(2)}) %collective-permute-start.21) | collective-permute-done | bytes 655392 | tf_op jit(solution)/shard_map/ppermute | solution.py:436
  150.3 11.6 %collective-permute-done.22 = bf16[160,2048]{1,0:T(8,128)(2,1)S(1)} collective-permute-done((bf16[160,2048]{1,0:T(8,128)(2,1)S(1)}, bf16[160,2048]{1,0:T(8,128)(2,1)S(1)}, u32[]{:S(2)}, u32[]{:S(2)}) %collective-permute-start.22) | collective-permute-done | bytes 655392 | tf_op jit(solution)/shard_map/ppermute | solution.py:436
  172.5 7.8 %collective-permute-done.23.refs_9_ = bf16[160,2048]{1,0:T(8,128)(2,1)S(1)} collective-permute-done((bf16[160,2048]{1,0:T(8,128)(2,1)S(1)}, bf16[160,2048]{1,0:T(8,128)(2,1)S(1)}, u32[]{:S(2)}, u32[]{:S(2)}) %collective-permute-start.23) | collective-permute-done | bytes 655392 | tf_op jit(solution)/shard_map/ppermute | solution.py:436
  188.7 10.1 %collective-permute-done.24.refs_10_ = bf16[160,2048]{1,0:T(8,128)(2,1)S(1)} collective-permute-done((bf16[160,2048]{1,0:T(8,128)(2,1)S(1)}, bf16[160,2048]{1,0:T(8,128)(2,1)S(1)}, u32[]{:S(2)}, u32[]{:S(2)}) %collective-permute-start.24) | collective-permute-done | bytes 655392 | tf_op jit(solution)/shard_map/ppermute | solution.py:436
  207.8 5.1 collective-permute-done.26
  213.7 10.4 %collective-permute-done.25.refs_11_ = bf16[160,2048]{1,0:T(8,128)(2,1)S(1)} collective-permute-done((bf16[160,2048]{1,0:T(8,128)(2,1)S(1)}, bf16[160,2048]{1,0:T(8,128)(2,1)S(1)}, u32[]{:S(2)}, u32[]{:S(2)}) %collective-permute-start.25) | collective-permute-done | bytes 655392 | tf_op jit(solution)/shard_map/ppermute | solution.py:436
  238.8 9.9 %collective-permute-done.28 = bf16[160,2048]{1,0:T(8,128)(2,1)S(1)} collective-permute-done((bf16[160,2048]{1,0:T(8,128)(2,1)S(1)}, bf16[160,2048]{1,0:T(8,128)(2,1)S(1)}, u32[]{:S(2)}, u32[]{:S(2)}) %collective-permute-start.28) | collective-permute-done | bytes 655392 | tf_op jit(solution)/shard_map/ppermute | solution.py:436
  250.4 8.7 %mlp_grads_low_sent.1 = bf16[512,4224]{1,0:T(8,128)(2,1)} custom-call(s32[4]{0:T(128)S(1)} %get-tuple-element.654.places, bf16[160,2048]{1,0:T(8,128)(2,1)S(1)} %copy-done.2, bf16[160,2048]{1,0:T(8,128)(2,1)} %collective-permute-done.8.refs_1_, bf16[160,2048]{1,0:T(8,128)(2,1)} %collective-permute-done.12.refs_2_, bf16[160,2048]{1,0:T(8,128)(2,1)} %copy-done.59, ...), custom_call_target="tpu_custom_call" | custom-call | tf_op jit(solution)/shard_map/mlp_grads_low_sent/pallas_call | solution.py:644
  260.4 16.8 %collective-permute-done.29.refs_0_ = bf16[160,2048]{1,0:T(8,128)(2,1)S(1)} collective-permute-done((bf16[160,2048]{1,0:T(8,128)(2,1)S(1)}, bf16[160,2048]{1,0:T(8,128)(2,1)S(1)}, u32[]{:S(2)}, u32[]{:S(2)}) %collective-permute-start.29) | collective-permute-done | bytes 655392 | tf_op jit(solution)/shard_map/ppermute | solution.py:436
  277.2 8.7 %mlp_grads_high_sent.1 = bf16[512,4224]{1,0:T(8,128)(2,1)} custom-call(s32[4]{0:T(128)S(1)} %get-tuple-element.652.places, bf16[160,2048]{1,0:T(8,128)(2,1)S(1)} %copy-done.2, bf16[160,2048]{1,0:T(8,128)(2,1)} %collective-permute-done.8.refs_1_, bf16[160,2048]{1,0:T(8,128)(2,1)} %collective-permute-done.12.refs_2_, bf16[160,2048]{1,0:T(8,128)(2,1)} %copy-done.59, ...), custom_call_target="tpu_custom_call" | custom-call | tf_op jit(solution)/shard_map/mlp_grads_high_sent/pallas_call | solution.py:644
  289.1 11.4 %mlp_grads_low_kept.1 = (bf16[256,4224]{1,0:T(8,128)(2,1)}, bf16[256,4224]{1,0:T(8,128)(2,1)}) custom-call(s32[4]{0:T(128)S(1)} %get-tuple-element.653.places, bf16[160,2048]{1,0:T(8,128)(2,1)S(1)} %copy-done.2, bf16[160,2048]{1,0:T(8,128)(2,1)} %collective-permute-done.8.refs_1_, bf16[160,2048]{1,0:T(8,128)(2,1)} %collective-permute-done.12.refs_2_, ...), custom_call_target="tpu_custom_call" | custom-call | tf_op jit(solution)/shard_map/mlp_grads_low_kept/pallas_call | solution.py:644
  307.5 11.4 %mlp_grads_high_kept.1 = (bf16[256,4224]{1,0:T(8,128)(2,1)}, bf16[256,4224]{1,0:T(8,128)(2,1)}) custom-call(s32[4]{0:T(128)S(1)} %get-tuple-element.651.places, bf16[160,2048]{1,0:T(8,128)(2,1)S(1)} %copy-done.2, bf16[160,2048]{1,0:T(8,128)(2,1)} %collective-permute-done.8.refs_1_, bf16[160,2048]{1,0:T(8,128)(2,1)} %collective-permute-done.12.refs_2_, ...), custom_call_target="tpu_custom_call" | custom-call | tf_op jit(solution)/shard_map/mlp_grads_high_kept/pallas_call | solution.py:644
  318.8 5.9 collective-permute-start.36
  327.0 11.8 %attention_backward.1 = (bf16[640,1024]{1,0:T(8,128)(2,1)}, bf16[5120,256]{1,0:T(8,128)(2,1)}, bf16[5120,256]{1,0:T(8,128)(2,1)}) custom-call(s32[1]{0:T(128)} %bitcast.group, bf16[640,1024]{1,0:T(8,128)(2,1)} %convolution_convert_fusion.2.query, bf16[640,1024]{1,0:T(8,128)(2,1)} %constant_dynamic-update-slice_fusion.20.grad, ...), custom_call_target="tpu_custom_call" | custom-call | flops 13421772800 | bytes 5242880 | tf_op jit(solution)/shard_map/attention_backward/pallas_call | solution.py:257
  338.8 11.3 %collective-permute-done.34.got = bf16[256,4224]{1,0:T(8,128)(2,1)} collective-permute-done((bf16[256,4224]{1,0:T(8,128)(2,1)}, bf16[256,4224]{1,0:T(8,128)(2,1)}, u32[]{:S(2)}, u32[]{:S(2)}) %collective-permute-start.34) | collective-permute-done | bytes 2162720 | tf_op jit(solution)/shard_map/ppermute | solution.py:499
  350.1 5.1 fusion.48
  360.9 10.9 %collective-permute-done.36.got = bf16[256,4224]{1,0:T(8,128)(2,1)} collective-permute-done((bf16[256,4224]{1,0:T(8,128)(2,1)}, bf16[256,4224]{1,0:T(8,128)(2,1)}, u32[]{:S(2)}, u32[]{:S(2)}) %collective-permute-start.36) | collective-permute-done | bytes 2162720 | tf_op jit(solution)/shard_map/ppermute | solution.py:499
  401.0 5.0 convolution_convert_fusion
  406.0 14.7 %collective-permute-done.37.got = bf16[1280,256]{1,0:T(8,128)(2,1)} collective-permute-done((bf16[1280,256]{1,0:T(8,128)(2,1)}, bf16[1280,256]{1,0:T(8,128)(2,1)}, u32[]{:S(2)}, u32[]{:S(2)}) %collective-permute-start.37) | collective-permute-done | bytes 655392 | tf_op jit(solution)/shard_map/ppermute | solution.py:499
  437.1 6.2 collective-permute-done.44
  452.0 10.1 %collective-permute-done.46 = bf16[160,512]{1,0:T(8,128)(2,1)S(1)} collective-permute-done((bf16[160,512]{1,0:T(8,128)(2,1)S(1)}, bf16[160,512]{1,0:T(8,128)(2,1)S(1)}, u32[]{:S(2)}, u32[]{:S(2)}) %collective-permute-start.46) | collective-permute-done | bytes 163872 | tf_op jit(solution)/shard_map/ppermute | solution.py:436
  469.8 4.8 result.1
  479.9 14.5 %collective-permute-done.49.refs_1_ = bf16[128,4224]{1,0:T(8,128)(2,1)} collective-permute-done((bf16[128,4224]{1,0:T(8,128)(2,1)}, bf16[128,4224]{1,0:T(8,128)(2,1)}, u32[]{:S(2)}, u32[]{:S(2)}) %collective-permute-start.49) | collective-permute-done | bytes 1081376 | tf_op jit(solution)/shard_map/ppermute | solution.py:499
  494.4 6.1 collective-permute-start.53
  538.1 31.7 %collective-permute-done.59 = bf16[64,512]{1,0:T(8,128)(2,1)S(1)} collective-permute-done((bf16[64,512]{1,0:T(8,128)(2,1)S(1)}, bf16[64,512]{1,0:T(8,128)(2,1)S(1)}, u32[]{:S(2)}, u32[]{:S(2)}) %collective-permute-start.59) | collective-permute-done | bytes 65568 | tf_op jit(solution)/shard_map/ppermute | solution.py:499
  576.4 28.2 %all-reduce.3.cloned.1.call-done = (bf16[1024,2048]{1,0:T(8,128)(2,1)}, bf16[1024,1024]{1,0:T(8,128)(2,1)}) async-done(((bf16[1024,2048]{1,0:T(8,128)(2,1)}, bf16[1024,1024]{1,0:T(8,128)(2,1)}), (bf16[1024,2048]{1,0:T(8,128)(2,1)}, bf16[1024,1024]{1,0:T(8,128)(2,1)})) %all-reduce.3.cloned.1.call-update) | async-done | bytes 6291472 | tf_op jit(solution)/shard_map/psum | solution.py:1140
  628.4 17.4 %mlp_grads_laid.1 = (f32[1408,2048]{1,0:T(8,128)}, f32[2048,1408]{1,0:T(8,128)}, f32[2048,1408]{1,0:T(8,128)}) custom-call(s32[16]{0:T(128)S(1)} %get-tuple-element.661.places, bf16[512,4224]{1,0:T(8,128)(2,1)} %join.4.refs_0_, bf16[512,4224]{1,0:T(8,128)(2,1)} %collective-permute-done.73.refs_1_, bf16[512,4224]{1,0:T(8,128)(2,1)} %join.5.refs_2_, ...), custom_call_target="tpu_custom_call" | custom-call | tf_op jit(solution)/shard_map/mlp_grads_laid/pallas_call | solution.py:795
  (488 shorter events, 289.7 us)
Async XLA Ops:
  8.0 436.0 %reduce-scatter.3.cloned.1.call-start = ((), (), s32[]{:S(2)}) async-start(), calls=%async_computation.2 | async-start | bytes 1638400 | tf_op jit(solution)/shard_map/reduce_scatter | solution.py:1135
  16.6 20.1 %collective-permute-start = (bf16[160,1024]{1,0:T(8,128)(2,1)}, bf16[160,1024]{1,0:T(8,128)(2,1)}, u32[]{:S(2)}, u32[]{:S(2)}) collective-permute-start(bf16[160,1024]{1,0:T(8,128)(2,1)} %get-tuple-element.658), channel_id=1, source_target_pairs={{0,1},{1,3},{3,2},{2,0},{4,5},{5,7},{7,6},{6,4},{8,9},{9,11},{11,1... | collective-permute-start | bytes 983048 | tf_op jit(solution)/shard_map/ppermute | solution.py:436
  86.6 28.0 %collective-permute-start.16 = (bf16[160,2048]{1,0:T(8,128)(2,1)}, bf16[160,2048]{1,0:T(8,128)(2,1)S(1)}, u32[]{:S(2)}, u32[]{:S(2)}) collective-permute-start(bf16[160,2048]{1,0:T(8,128)(2,1)} %collective-permute-done.12.refs_2_), channel_id=1, source_target_pairs={{0,1},{1,3},{3,2},{2,0},{4,5},{5,7},{7,6},{6,4},{8,9},{9,11},{11,1... | collective-permute-start | bytes 1966088 | tf_op jit(solution)/shard_map/ppermute | solution.py:436
  89.3 24.3 %collective-permute-start.17 = (bf16[160,512]{1,0:T(8,128)(2,1)S(1)}, bf16[160,512]{1,0:T(8,128)(2,1)S(1)}, u32[]{:S(2)}, u32[]{:S(2)}) collective-permute-start(bf16[160,512]{1,0:T(8,128)(2,1)S(1)} %get-tuple-element.635), channel_id=1, source_target_pairs={{0,1},{1,3},{3,2},{2,0},{4,5},{5,7},{7,6},{6,4},{8,9},{9,11},{11,1... | collective-permute-start | bytes 491528 | tf_op jit(solution)/shard_map/ppermute | solution.py:968
  91.4 22.2 %collective-permute-start.18 = (bf16[160,512]{1,0:T(8,128)(2,1)S(1)}, bf16[160,512]{1,0:T(8,128)(2,1)S(1)}, u32[]{:S(2)}, u32[]{:S(2)}) collective-permute-start(bf16[160,512]{1,0:T(8,128)(2,1)S(1)} %get-tuple-element.634), channel_id=1, source_target_pairs={{0,3},{1,2},{3,0},{2,1},{4,7},{5,6},{7,4},{6,5},{8,11},{9,10},{11,... | collective-permute-start | bytes 491528 | tf_op jit(solution)/shard_map/ppermute | solution.py:968
  92.3 21.3 %collective-permute-start.19 = (bf16[160,512]{1,0:T(8,128)(2,1)S(1)}, bf16[160,512]{1,0:T(8,128)(2,1)S(1)}, u32[]{:S(2)}, u32[]{:S(2)}) collective-permute-start(bf16[160,512]{1,0:T(8,128)(2,1)S(1)} %get-tuple-element.633), channel_id=1, source_target_pairs={{0,2},{1,0},{3,1},{2,3},{4,6},{5,4},{7,5},{6,7},{8,10},{9,8},{11,9... | collective-permute-start | bytes 491528 | tf_op jit(solution)/shard_map/ppermute | solution.py:968
  188.6 24.3 %collective-permute-start.26 = (bf16[160,2048]{1,0:T(8,128)(2,1)S(1)}, bf16[160,2048]{1,0:T(8,128)(2,1)S(1)}, u32[]{:S(2)}, u32[]{:S(2)}) collective-permute-start(bf16[160,2048]{1,0:T(8,128)(2,1)S(1)} %fusion.9), channel_id=1, source_target_pairs={{0,1},{1,3},{3,2},{2,0},{4,5},{5,7},{7,6},{6,4},{8,9},{9,11},{11,1... | collective-permute-start | bytes 1966088 | tf_op jit(solution)/shard_map/ppermute | solution.py:436
  198.8 25.3 %collective-permute-start.25 = (bf16[160,2048]{1,0:T(8,128)(2,1)S(1)}, bf16[160,2048]{1,0:T(8,128)(2,1)S(1)}, u32[]{:S(2)}, u32[]{:S(2)}) collective-permute-start(bf16[160,2048]{1,0:T(8,128)(2,1)S(1)} %collective-permute-done.24.refs_10_), channel_id=1, source_target_pairs={{0,1},{1,3},{3,2},{2,0},{4,5},{5,7},{7,6},{6,4},{8,9},{9,11},{11,1... | collective-permute-start | bytes 1966088 | tf_op jit(solution)/shard_map/ppermute | solution.py:436
  213.1 23.7 %collective-permute-start.27 = (bf16[160,2048]{1,0:T(8,128)(2,1)S(1)}, bf16[160,2048]{1,0:T(8,128)(2,1)S(1)}, u32[]{:S(2)}, u32[]{:S(2)}) collective-permute-start(bf16[160,2048]{1,0:T(8,128)(2,1)S(1)} %add_convert_fusion.3), channel_id=1, source_target_pairs={{0,1},{1,3},{3,2},{2,0},{4,5},{5,7},{7,6},{6,4},{8,9},{9,11},{11,1... | collective-permute-start | bytes 1966088 | tf_op jit(solution)/shard_map/ppermute | solution.py:436
  259.1 29.9 %collective-permute-start.31 = (bf16[512,4224]{1,0:T(8,128)(2,1)}, bf16[512,4224]{1,0:T(8,128)(2,1)}, u32[]{:S(2)}, u32[]{:S(2)}) collective-permute-start(bf16[512,4224]{1,0:T(8,128)(2,1)} %mlp_grads_low_sent.1), channel_id=1, source_target_pairs={{0,4},{4,0},{8,12},{12,8},{16,20},{20,16},{24,28},{28,24},{1,5},{5... | collective-permute-start | bytes 12976136 | tf_op jit(solution)/shard_map/ppermute | solution.py:499
  285.9 21.5 %collective-permute-start.33 = (bf16[512,4224]{1,0:T(8,128)(2,1)}, bf16[512,4224]{1,0:T(8,128)(2,1)}, u32[]{:S(2)}, u32[]{:S(2)}) collective-permute-start(bf16[512,4224]{1,0:T(8,128)(2,1)} %mlp_grads_high_sent.1), channel_id=1, source_target_pairs={{0,4},{4,0},{8,12},{12,8},{16,20},{20,16},{24,28},{28,24},{1,5},{5... | collective-permute-start | bytes 12976136 | tf_op jit(solution)/shard_map/ppermute | solution.py:499
  300.4 49.7 %collective-permute-start.34 = (bf16[256,4224]{1,0:T(8,128)(2,1)}, bf16[256,4224]{1,0:T(8,128)(2,1)}, u32[]{:S(2)}, u32[]{:S(2)}) collective-permute-start(bf16[256,4224]{1,0:T(8,128)(2,1)} %get-tuple-element.429), channel_id=1, source_target_pairs={{0,8},{4,12},{8,0},{12,4},{16,24},{20,28},{24,16},{28,20},{1,9},{5... | collective-permute-start | bytes 6488072 | tf_op jit(solution)/shard_map/ppermute | solution.py:499
  304.0 20.7 %collective-permute-start.32 = (bf16[160,2048]{1,0:T(8,128)(2,1)S(1)}, bf16[160,2048]{1,0:T(8,128)(2,1)S(1)}, u32[]{:S(2)}, u32[]{:S(2)}) collective-permute-start(bf16[160,2048]{1,0:T(8,128)(2,1)S(1)} %collective-permute-done.30.refs_0_), channel_id=1, source_target_pairs={{0,1},{1,3},{3,2},{2,0},{4,5},{5,7},{7,6},{6,4},{8,9},{9,11},{11,1... | collective-permute-start | bytes 1966088 | tf_op jit(solution)/shard_map/ppermute | solution.py:436
  318.8 53.0 %collective-permute-start.36 = (bf16[256,4224]{1,0:T(8,128)(2,1)}, bf16[256,4224]{1,0:T(8,128)(2,1)}, u32[]{:S(2)}, u32[]{:S(2)}) collective-permute-start(bf16[256,4224]{1,0:T(8,128)(2,1)} %get-tuple-element.454), channel_id=1, source_target_pairs={{0,16},{4,20},{8,24},{12,28},{16,0},{20,4},{24,8},{28,12},{1,17},{... | collective-permute-start | bytes 6488072 | tf_op jit(solution)/shard_map/ppermute | solution.py:499
  355.2 27.0 %collective-permute-start.35 = (bf16[2560,256]{1,0:T(8,128)(2,1)}, bf16[2560,256]{1,0:T(8,128)(2,1)}, u32[]{:S(2)}, u32[]{:S(2)}) collective-permute-start(bf16[2560,256]{1,0:T(8,128)(2,1)} %get-tuple-element.662), channel_id=1, source_target_pairs={{0,4},{4,0},{8,12},{12,8},{16,20},{20,16},{24,28},{28,24},{1,5},{5... | collective-permute-start | bytes 3932168 | tf_op jit(solution)/shard_map/ppermute | solution.py:499
  355.3 33.4 %collective-permute-start.38 = (bf16[2560,256]{1,0:T(8,128)(2,1)}, bf16[2560,256]{1,0:T(8,128)(2,1)}, u32[]{:S(2)}, u32[]{:S(2)}) collective-permute-start(bf16[2560,256]{1,0:T(8,128)(2,1)} %get-tuple-element.614), channel_id=1, source_target_pairs={{0,4},{4,0},{8,12},{12,8},{16,20},{20,16},{24,28},{28,24},{1,5},{5... | collective-permute-start | bytes 3932168 | tf_op jit(solution)/shard_map/ppermute | solution.py:499
  379.6 127.3 %all-gather.2.cloned.1.call-start = ((), (), s32[]{:S(2)}) async-start(), calls=%async_computation.3 | async-start | bytes 1638400 | tf_op jit(solution)/shard_map/all_gather | solution.py:1151
  379.7 49.7 %collective-permute-start.41 = (bf16[128,4224]{1,0:T(8,128)(2,1)}, bf16[128,4224]{1,0:T(8,128)(2,1)}, u32[]{:S(2)}, u32[]{:S(2)}) collective-permute-start(bf16[128,4224]{1,0:T(8,128)(2,1)} %copy-done.47), channel_id=1, source_target_pairs={{0,16},{4,20},{8,24},{12,28},{16,0},{20,4},{24,8},{28,12},{1,17},{... | collective-permute-start | bytes 3244040 | tf_op jit(solution)/shard_map/ppermute | solution.py:499
  381.5 51.2 %collective-permute-start.40 = (bf16[128,4224]{1,0:T(8,128)(2,1)}, bf16[128,4224]{1,0:T(8,128)(2,1)}, u32[]{:S(2)}, u32[]{:S(2)}) collective-permute-start(bf16[128,4224]{1,0:T(8,128)(2,1)} %copy-done.48), channel_id=1, source_target_pairs={{0,8},{4,12},{8,0},{12,4},{16,24},{20,28},{24,16},{28,20},{1,9},{5... | collective-permute-start | bytes 3244040 | tf_op jit(solution)/shard_map/ppermute | solution.py:499
  387.4 33.4 %collective-permute-start.37 = (bf16[1280,256]{1,0:T(8,128)(2,1)}, bf16[1280,256]{1,0:T(8,128)(2,1)}, u32[]{:S(2)}, u32[]{:S(2)}) collective-permute-start(bf16[1280,256]{1,0:T(8,128)(2,1)} %get-tuple-element.479), channel_id=1, source_target_pairs={{0,8},{4,12},{8,0},{12,4},{16,24},{20,28},{24,16},{28,20},{1,9},{5... | collective-permute-start | bytes 1966088 | tf_op jit(solution)/shard_map/ppermute | solution.py:499
  392.4 32.0 %collective-permute-start.42 = (bf16[1280,256]{1,0:T(8,128)(2,1)}, bf16[1280,256]{1,0:T(8,128)(2,1)}, u32[]{:S(2)}, u32[]{:S(2)}) collective-permute-start(bf16[1280,256]{1,0:T(8,128)(2,1)} %get-tuple-element.483), channel_id=1, source_target_pairs={{0,16},{4,20},{8,24},{12,28},{16,0},{20,4},{24,8},{28,12},{1,17},{... | collective-permute-start | bytes 1966088 | tf_op jit(solution)/shard_map/ppermute | solution.py:499
  444.0 160.6 %all-reduce.3.cloned.1.call-start = ((), (), s32[]{:S(2)}) async-start(), calls=%async_computation.5 | async-start | bytes 12582912 | tf_op jit(solution)/shard_map/psum | solution.py:1140
  444.4 35.4 %collective-permute-start.51 = (bf16[128,4224]{1,0:T(8,128)(2,1)}, bf16[128,4224]{1,0:T(8,128)(2,1)}, u32[]{:S(2)}, u32[]{:S(2)}) collective-permute-start(bf16[128,4224]{1,0:T(8,128)(2,1)} %copy-done.23), channel_id=1, source_target_pairs={{0,16},{4,20},{8,24},{12,28},{16,0},{20,4},{24,8},{28,12},{1,17},{... | collective-permute-start | bytes 3244040 | tf_op jit(solution)/shard_map/ppermute | solution.py:499
  445.9 34.0 %collective-permute-start.52 = (bf16[128,4224]{1,0:T(8,128)(2,1)}, bf16[128,4224]{1,0:T(8,128)(2,1)}, u32[]{:S(2)}, u32[]{:S(2)}) collective-permute-start(bf16[128,4224]{1,0:T(8,128)(2,1)} %copy-done.23), channel_id=1, source_target_pairs={{0,8},{4,12},{8,0},{12,4},{16,24},{20,28},{24,16},{28,20},{1,9},{5... | collective-permute-start | bytes 3244040 | tf_op jit(solution)/shard_map/ppermute | solution.py:499
  447.3 47.1 %collective-permute-start.49 = (bf16[128,4224]{1,0:T(8,128)(2,1)}, bf16[128,4224]{1,0:T(8,128)(2,1)}, u32[]{:S(2)}, u32[]{:S(2)}) collective-permute-start(bf16[128,4224]{1,0:T(8,128)(2,1)} %copy-done.21), channel_id=1, source_target_pairs={{0,8},{4,12},{8,0},{12,4},{16,24},{20,28},{24,16},{28,20},{1,9},{5... | collective-permute-start | bytes 3244040 | tf_op jit(solution)/shard_map/ppermute | solution.py:499
  447.9 46.5 %collective-permute-start.50 = (bf16[128,4224]{1,0:T(8,128)(2,1)}, bf16[128,4224]{1,0:T(8,128)(2,1)}, u32[]{:S(2)}, u32[]{:S(2)}) collective-permute-start(bf16[128,4224]{1,0:T(8,128)(2,1)} %copy-done.21), channel_id=1, source_target_pairs={{0,16},{4,20},{8,24},{12,28},{16,0},{20,4},{24,8},{28,12},{1,17},{... | collective-permute-start | bytes 3244040 | tf_op jit(solution)/shard_map/ppermute | solution.py:499
  479.8 170.8 %reduce-scatter.5.cloned.1.call-start = ((), (), s32[]{:S(2)}) async-start(), calls=%async_computation.4 | async-start | bytes 3276800 | tf_op jit(solution)/shard_map/reduce_scatter | solution.py:1176
  533.8 75.9 %collective-permute-start.69 = (bf16[128,4224]{1,0:T(8,128)(2,1)}, bf16[128,4224]{1,0:T(8,128)(2,1)}, u32[]{:S(2)}, u32[]{:S(2)}) collective-permute-start(bf16[128,4224]{1,0:T(8,128)(2,1)} %collective-permute-done.49.refs_1_), channel_id=1, source_target_pairs={{0,16},{4,20},{8,24},{12,28},{16,0},{20,4},{24,8},{28,12},{1,17},{... | collective-permute-start | bytes 3244040 | tf_op jit(solution)/shard_map/ppermute | solution.py:499
  535.8 68.9 %collective-permute-start.70 = (bf16[128,4224]{1,0:T(8,128)(2,1)}, bf16[128,4224]{1,0:T(8,128)(2,1)}, u32[]{:S(2)}, u32[]{:S(2)}) collective-permute-start(bf16[128,4224]{1,0:T(8,128)(2,1)} %collective-permute-done.51.refs_1_), channel_id=1, source_target_pairs={{0,8},{4,12},{8,0},{12,4},{16,24},{20,28},{24,16},{28,20},{1,9},{5... | collective-permute-start | bytes 3244040 | tf_op jit(solution)/shard_map/ppermute | solution.py:499
  535.8 34.0 %collective-permute-start.59 = (bf16[64,512]{1,0:T(8,128)(2,1)S(1)}, bf16[64,512]{1,0:T(8,128)(2,1)S(1)}, u32[]{:S(2)}, u32[]{:S(2)}) collective-permute-start(bf16[64,512]{1,0:T(8,128)(2,1)S(1)} %get-tuple-element.646), channel_id=1, source_target_pairs={{0,16},{4,20},{8,24},{12,28},{16,0},{20,4},{24,8},{28,12},{1,17},{... | collective-permute-start | bytes 196616 | tf_op jit(solution)/shard_map/ppermute | solution.py:499
  536.1 35.2 %collective-permute-start.58 = (bf16[64,1024]{1,0:T(8,128)(2,1)S(1)}, bf16[64,1024]{1,0:T(8,128)(2,1)S(1)}, u32[]{:S(2)}, u32[]{:S(2)}) collective-permute-start(bf16[64,1024]{1,0:T(8,128)(2,1)S(1)} %get-tuple-element.640), channel_id=1, source_target_pairs={{0,8},{4,12},{8,0},{12,4},{16,24},{20,28},{24,16},{28,20},{1,9},{5... | collective-permute-start | bytes 393224 | tf_op jit(solution)/shard_map/ppermute | solution.py:499
  627.1 23.5 %collective-permute-start.75 = (f32[2,512]{1,0:T(2,128)S(1)}, f32[2,512]{1,0:T(2,128)S(1)}, u32[]{:S(2)}, u32[]{:S(2)}) collective-permute-start(f32[2,512]{1,0:T(2,128)S(1)} %add.470), channel_id=1, source_target_pairs={{0,8},{4,12},{8,0},{12,4},{16,24},{20,28},{24,16},{28,20},{1,9},{5... | collective-permute-start | bytes 12296 | tf_op jit(solution)/shard_map/ppermute | solution.py:949
  (149 other events, 1811.3 us)
Sparse Core Ops, SparseCore 0:
  379.7 31.3 reduce-scatter.2
  444.1 40.4 all-gather.1
  536.0 50.3 reduce-scatter.4
Sparse Core Ops, SparseCore 1:
  479.9 124.7 all-reduce.2
